TPU v7x, 512 devices: a whole 4x4x16 slice. The times are simulated.
512 devices in a mesh: row: 16 (over z_lo, y), col: 32 (over x, z_hi, core).
Axes of the slice: x: 4, y: 4, z: 16 (z_hi: 4, z_lo: 4; z = z_hi * 4 + z_lo), core: 2. Of those that a mesh axis runs over, the one named last changes fastest.
Arguments:
- inputs: bfloat16 [256, 98304], P('row', 'col'), may hold values from -6 to 6
- first_weight: bfloat16 [9, 36864], replicated, may hold values from -0.15625 to 0.15625
- second_weight: bfloat16 [9, 36864], replicated, may hold values from -0.15625 to 0.15625
- cotangent: bfloat16 [256, 98304], P('row', 'col'), may hold values from -6 to 6
Outputs:
- output_field_grid: bfloat16 [256, 98304], P('row', 'col')
- input_grad: bfloat16 [256, 98304], P('row', 'col')
- first_weight_gradient: bfloat16 [9, 36864], replicated
- second_weight_gradient: bfloat16 [9, 36864], replicated
All inputs are finite; a program needn't handle non-finite values.
Results may differ from a plain program's by a relative error of at most 0.015.
Values may be sent and summed in bfloat16 or wider, within the bound.
No kernel may reach another device: no remote copies, remote signals or barrier semaphores. Data moves between devices by JAX's collectives and lax.ppermute only.
A program may use at most 64 MiB of HBM per device.

v0:
```python
import jax
import jax.numpy as jnp
from jax import lax
from jax.sharding import PartitionSpec as P

C = 192


def gelu_parts(value):
    normal_cdf = 0.5 * (1.0 + lax.erf(value * 0.7071067811865476))
    density = jnp.exp(-0.5 * value * value) * 0.3989422804014327
    return (value * normal_cdf, normal_cdf + value * density)


def offset_taps(field, stride_tiles, direction):
    row_count, col_count, group_cells, channels = field.shape
    padded = jnp.pad(
        field, ((stride_tiles, stride_tiles), (stride_tiles, stride_tiles), (0, 0), (0, 0))
    )
    tap_list = []
    for row_off in (-1, 0, 1):
        for col_off in (-1, 0, 1):
            row_start = stride_tiles + direction * row_off * stride_tiles
            col_start = stride_tiles + direction * col_off * stride_tiles
            piece = padded[row_start : row_start + row_count, col_start : col_start + col_count]
            tap_list.append(piece.reshape(-1, channels))
    return jnp.concatenate(tap_list, axis=1)


def flip_kernel(kernel):
    channels = kernel.shape[1]
    return kernel.reshape(9, channels, channels).transpose(0, 2, 1).reshape(9 * channels, channels)


def per_device(inputs, first_weight, second_weight, cotangent):
    channels = C
    tile_shape = inputs.shape
    tile_rows = inputs.shape[0]
    cell_count = tile_rows * inputs.shape[1] // channels
    kernel_one = first_weight.reshape(9 * channels, channels)
    kernel_two = second_weight.reshape(9 * channels, channels)
    row_count = lax.axis_size("row")
    col_count = lax.axis_size("col")
    group_cells = -(-cell_count // (row_count * col_count))
    padded_cells = group_cells * row_count * col_count

    def spread_field(field):
        flat = jnp.pad(
            field.reshape(cell_count, channels), ((0, padded_cells - cell_count), (0, 0))
        )
        return flat.reshape(1, 1, col_count, row_count, group_cells, channels)

    field_in, grad_in = (
        lax.all_to_all(
            lax.all_to_all(spread_field(inputs), "row", split_axis=3, concat_axis=0, tiled=True),
            "col",
            split_axis=2,
            concat_axis=1,
            tiled=True,
        ),
        lax.all_to_all(
            lax.all_to_all(spread_field(cotangent), "row", split_axis=3, concat_axis=0, tiled=True),
            "col",
            split_axis=2,
            concat_axis=1,
            tiled=True,
        ),
    )
    field_in = field_in.reshape(row_count, col_count, group_cells, channels)
    grad_in = grad_in.reshape(row_count, col_count, group_cells, channels)

    def taps_of(field, stride_tiles, direction):
        return offset_taps(field, stride_tiles, direction)

    field_shape = field_in.shape
    input_padded_field = field_in.astype(jnp.float32)
    gelu_one, slope_one = gelu_parts(input_padded_field)
    activation_first = gelu_one.astype(jnp.bfloat16)
    taps_one = taps_of(activation_first, 2, 1)
    pre_one = jnp.dot(taps_one, kernel_one, preferred_element_type=jnp.float32).reshape(field_shape)
    hidden_state = (input_padded_field + pre_one).astype(jnp.bfloat16)
    hidden_padded_state = hidden_state.astype(jnp.float32)
    gelu_two, slope_two = gelu_parts(hidden_padded_state)
    activation_second = gelu_two.astype(jnp.bfloat16)
    taps_two = taps_of(activation_second, 4, 1)
    pre_two = jnp.dot(taps_two, kernel_two, preferred_element_type=jnp.float32).reshape(field_shape)
    output_local = (hidden_padded_state + pre_two).astype(jnp.bfloat16)
    scale_factor = 1.0 / (tile_rows * row_count)
    contract = (((0,), (0,)), ((), ()))
    grad_taps = taps_of(grad_in, 4, -1)
    backward_second = jnp.dot(
        grad_taps, flip_kernel(kernel_two), preferred_element_type=jnp.float32
    ).reshape(field_shape)
    hidden_gradient = (grad_in.astype(jnp.float32) + backward_second * slope_two).astype(
        jnp.bfloat16
    )
    local_two = lax.dot_general(
        taps_two, grad_in.reshape(-1, channels), contract, preferred_element_type=jnp.float32
    )
    hidden_taps = taps_of(hidden_gradient, 2, -1)
    backward_first = jnp.dot(
        hidden_taps, flip_kernel(kernel_one), preferred_element_type=jnp.float32
    ).reshape(field_shape)
    input_local = (hidden_gradient.astype(jnp.float32) + backward_first * slope_one).astype(
        jnp.bfloat16
    )
    local_one = lax.dot_general(
        taps_one,
        hidden_gradient.reshape(-1, channels),
        contract,
        preferred_element_type=jnp.float32,
    )
    summed_one, summed_two = lax.psum((local_one, local_two), ("row", "col"))
    first_weight_gradient = (
        (summed_one * scale_factor).astype(jnp.bfloat16).reshape(9, channels * channels)
    )
    second_weight_gradient = (
        (summed_two * scale_factor).astype(jnp.bfloat16).reshape(9, channels * channels)
    )
    back_shape = (row_count, col_count, 1, 1, group_cells, channels)
    output_back, input_back = (
        lax.all_to_all(
            lax.all_to_all(
                output_local.reshape(back_shape), "row", split_axis=0, concat_axis=3, tiled=True
            ),
            "col",
            split_axis=1,
            concat_axis=2,
            tiled=True,
        ),
        lax.all_to_all(
            lax.all_to_all(
                input_local.reshape(back_shape), "row", split_axis=0, concat_axis=3, tiled=True
            ),
            "col",
            split_axis=1,
            concat_axis=2,
            tiled=True,
        ),
    )
    output_field_grid = output_back.reshape(padded_cells, channels)[:cell_count].reshape(tile_shape)
    input_grad = input_back.reshape(padded_cells, channels)[:cell_count].reshape(tile_shape)
    return (output_field_grid, input_grad, first_weight_gradient, second_weight_gradient)


def solution(mesh):
    return jax.shard_map(
        per_device,
        mesh=mesh,
        in_specs=(P("row", "col"), P(), P(), P("row", "col")),
        out_specs=(P("row", "col"), P("row", "col"), P(), P()),
        check_vma=False,
    )
```

profile of v0, /device:TPU:1, one launch (start us, length us, event | category | flops | bytes accessed | tf_op | source)
XLA Modules:
  0.0 648.5 jit_solution(14688290115333052364)
XLA Ops:
  9.1 9.2 %all-to-all-start = ((bf16[1,1,32,16,1,192]{5,2,4,1,0,3:T(8,128)(2,1)}), bf16[1,1,32,16,1,192]{5,2,4,1,0,3:T(8,128)(2,1)S(1)}, u32[]{:S(2)}, u32[]{:S(2)}) async-start(bf16[1,1,32,16,1,192]{5,2,4,1,0,3:T(8,128)(2,1)} %copy.43), calls=%async_computation | async-start | bytes 524288 | tf_op jit(solution)/shard_map/all_to_all | solution.py:55
  20.2 7.3 %all-to-all-done = bf16[1,1,32,16,1,192]{5,2,4,1,0,3:T(8,128)(2,1)S(1)} async-done(((bf16[1,1,32,16,1,192]{5,2,4,1,0,3:T(8,128)(2,1)}), bf16[1,1,32,16,1,192]{5,2,4,1,0,3:T(8,128)(2,1)S(1)}, u32[]{:S(2)}, u32[]{:S(2)}) %all-to-all-start) | async-done | bytes 196640 | tf_op jit(solution)/shard_map/all_to_all | solution.py:55
  27.5 4.4 all-to-all-start.4
  32.8 8.0 %all-to-all-done.4 = bf16[1,1,32,16,1,192]{5,2,4,1,0,3:T(8,128)(2,1)S(1)} async-done(((bf16[1,1,32,16,1,192]{5,2,4,1,0,3:T(8,128)(2,1)}), bf16[1,1,32,16,1,192]{5,2,4,1,0,3:T(8,128)(2,1)S(1)}, u32[]{:S(2)}, u32[]{:S(2)}) %all-to-all-start.4) | async-done | bytes 196640 | tf_op jit(solution)/shard_map/all_to_all | solution.py:62
  41.5 17.9 %all-to-all-start.1 = ((bf16[16,1,32,1,1,192]{5,0,4,3,1,2:T(8,128)(2,1)}), bf16[16,1,32,1,1,192]{5,0,4,3,1,2:T(8,128)(2,1)S(1)}, u32[]{:S(2)}, u32[]{:S(2)}) async-start(bf16[16,1,32,1,1,192]{5,0,4,3,1,2:T(8,128)(2,1)} %copy.44), calls=%async_computation.1 | async-start | bytes 524288 | tf_op jit(solution)/shard_map/all_to_all | solution.py:54
  59.4 1.8 reshape.322
  68.9 10.7 %all-to-all-done.1 = bf16[16,1,32,1,1,192]{5,0,4,3,1,2:T(8,128)(2,1)S(1)} async-done(((bf16[16,1,32,1,1,192]{5,0,4,3,1,2:T(8,128)(2,1)}), bf16[16,1,32,1,1,192]{5,0,4,3,1,2:T(8,128)(2,1)S(1)}, u32[]{:S(2)}, u32[]{:S(2)}) %all-to-all-start.1) | async-done | bytes 196640 | tf_op jit(solution)/shard_map/all_to_all | solution.py:54
  79.6 6.9 %all-to-all-start.5 = ((bf16[16,1,32,1,1,192]{5,0,4,3,1,2:T(8,128)(2,1)}), bf16[16,1,32,1,1,192]{5,0,4,3,1,2:T(8,128)(2,1)}, u32[]{:S(2)}, u32[]{:S(2)}) async-start(bf16[16,1,32,1,1,192]{5,0,4,3,1,2:T(8,128)(2,1)} %copy.51), calls=%async_computation.5 | async-start | bytes 524288 | tf_op jit(solution)/shard_map/all_to_all | solution.py:61
  86.7 2.0 pad_slice_fusion.24
  89.5 2.6 concatenate.92
  92.1 2.6 multiply_convert_fusion.2
  94.8 2.1 pad_slice_fusion.8
  96.8 2.8 concatenate.101
  99.6 2.4 fusion.7
  102.0 2.2 all-to-all-done.5
  104.2 9.6 %all-to-all-start.2 = ((bf16[16,32,1,1,1,192]{5,1,4,3,2,0:T(8,128)(2,1)}), bf16[16,32,1,1,1,192]{5,1,4,3,2,0:T(8,128)(2,1)}, u32[]{:S(2)}, u32[]{:S(2)}) async-start(bf16[16,32,1,1,1,192]{5,1,4,3,2,0:T(8,128)(2,1)} %fusion.7), calls=%async_computation.2 | async-start | bytes 524288 | tf_op jit(solution)/shard_map/all_to_all | solution.py:123
  116.1 2.6 concatenate.110
  118.8 2.1 fusion.2
  121.9 3.7 concatenate.119
  126.6 2.7 concatenate.120
  129.3 3.2 fusion.8
  132.5 6.9 %all-to-all-start.6 = ((bf16[16,32,1,1,1,192]{5,1,4,3,2,0:T(8,128)(2,1)}), bf16[16,32,1,1,1,192]{5,1,4,3,2,0:T(8,128)(2,1)}, u32[]{:S(2)}, u32[]{:S(2)}) async-start(bf16[16,32,1,1,1,192]{5,1,4,3,2,0:T(8,128)(2,1)} %fusion.8), calls=%async_computation.6 | async-start | bytes 524288 | tf_op jit(solution)/shard_map/all_to_all | solution.py:132
  141.2 2.6 concatenate.121
  145.5 1.8 copy.49
  148.6 9.4 %all-to-all-start.3 = ((bf16[1,32,1,16,1,192]{5,3,4,2,0,1:T(8,128)(2,1)}), bf16[1,32,1,16,1,192]{5,3,4,2,0,1:T(8,128)(2,1)S(1)}, u32[]{:S(2)}, u32[]{:S(2)}) async-start(bf16[1,32,1,16,1,192]{5,3,4,2,0,1:T(8,128)(2,1)} %copy.49), calls=%async_computation.3 | async-start | bytes 524288 | tf_op jit(solution)/shard_map/all_to_all | solution.py:122
  158.1 1.8 copy.59
  159.9 18.4 %all-to-all-done.3 = bf16[1,32,1,16,1,192]{5,3,4,2,0,1:T(8,128)(2,1)S(1)} async-done(((bf16[1,32,1,16,1,192]{5,3,4,2,0,1:T(8,128)(2,1)}), bf16[1,32,1,16,1,192]{5,3,4,2,0,1:T(8,128)(2,1)S(1)}, u32[]{:S(2)}, u32[]{:S(2)}) %all-to-all-start.3) | async-done | bytes 196640 | tf_op jit(solution)/shard_map/all_to_all | solution.py:122
  178.3 6.8 %all-to-all-start.7 = ((bf16[1,32,1,16,1,192]{5,3,4,2,0,1:T(8,128)(2,1)}), bf16[1,32,1,16,1,192]{5,3,4,2,0,1:T(8,128)(2,1)S(1)}, u32[]{:S(2)}, u32[]{:S(2)}) async-start(bf16[1,32,1,16,1,192]{5,3,4,2,0,1:T(8,128)(2,1)} %copy.59), calls=%async_computation.7 | async-start | bytes 524288 | tf_op jit(solution)/shard_map/all_to_all | solution.py:131
  185.1 448.2 %all-reduce.9.cloned.1.call-done = (f32[1728,192]{0,1:T(8,128)}, f32[1728,192]{0,1:T(8,128)}) async-done(((f32[1728,192]{0,1:T(8,128)}, f32[1728,192]{0,1:T(8,128)}), (f32[1728,192]{0,1:T(8,128)}, f32[1728,192]{0,1:T(8,128)})) %all-reduce.9.cloned.1.call-update) | async-done | bytes 2654224 | tf_op jit(solution)/shard_map/psum | solution.py:113
  633.2 1.9 multiply_convert_fusion
  635.5 2.1 reshape.342
  637.9 2.1 reshape.352
  (52 shorter events, 25.3 us)
Async XLA Ops:
  8.3 51.1 %copy-start = (bf16[9,36864]{1,0:T(8,128)(2,1)S(1)}, bf16[9,36864]{1,0:T(8,128)(2,1)}, u32[]{:S(2)}) copy-start(bf16[9,36864]{1,0:T(8,128)(2,1)} %param.6) | copy-start | bytes 1990660
  9.1 18.4 %all-to-all-start = ((bf16[1,1,32,16,1,192]{5,2,4,1,0,3:T(8,128)(2,1)}), bf16[1,1,32,16,1,192]{5,2,4,1,0,3:T(8,128)(2,1)S(1)}, u32[]{:S(2)}, u32[]{:S(2)}) async-start(bf16[1,1,32,16,1,192]{5,2,4,1,0,3:T(8,128)(2,1)} %copy.43), calls=%async_computation | async-start | bytes 524288 | tf_op jit(solution)/shard_map/all_to_all | solution.py:55
  27.5 13.3 %all-to-all-start.4 = ((bf16[1,1,32,16,1,192]{5,2,4,1,0,3:T(8,128)(2,1)}), bf16[1,1,32,16,1,192]{5,2,4,1,0,3:T(8,128)(2,1)S(1)}, u32[]{:S(2)}, u32[]{:S(2)}) async-start(bf16[1,1,32,16,1,192]{5,2,4,1,0,3:T(8,128)(2,1)} %copy.50), calls=%async_computation.4 | async-start | bytes 524288 | tf_op jit(solution)/shard_map/all_to_all | solution.py:62
  40.8 0.7 copy-start.8
  41.5 38.1 %all-to-all-start.1 = ((bf16[16,1,32,1,1,192]{5,0,4,3,1,2:T(8,128)(2,1)}), bf16[16,1,32,1,1,192]{5,0,4,3,1,2:T(8,128)(2,1)S(1)}, u32[]{:S(2)}, u32[]{:S(2)}) async-start(bf16[16,1,32,1,1,192]{5,0,4,3,1,2:T(8,128)(2,1)} %copy.44), calls=%async_computation.1 | async-start | bytes 524288 | tf_op jit(solution)/shard_map/all_to_all | solution.py:54
  59.4 2.9 copy-start.1
  65.2 2.8 copy-start.9
  79.6 24.6 %all-to-all-start.5 = ((bf16[16,1,32,1,1,192]{5,0,4,3,1,2:T(8,128)(2,1)}), bf16[16,1,32,1,1,192]{5,0,4,3,1,2:T(8,128)(2,1)}, u32[]{:S(2)}, u32[]{:S(2)}) async-start(bf16[16,1,32,1,1,192]{5,0,4,3,1,2:T(8,128)(2,1)} %copy.51), calls=%async_computation.5 | async-start | bytes 524288 | tf_op jit(solution)/shard_map/all_to_all | solution.py:61
  96.8 2.8 copy-start.2
  104.2 28.3 %all-to-all-start.2 = ((bf16[16,32,1,1,1,192]{5,1,4,3,2,0:T(8,128)(2,1)}), bf16[16,32,1,1,1,192]{5,1,4,3,2,0:T(8,128)(2,1)}, u32[]{:S(2)}, u32[]{:S(2)}) async-start(bf16[16,32,1,1,1,192]{5,1,4,3,2,0:T(8,128)(2,1)} %fusion.7), calls=%async_computation.2 | async-start | bytes 524288 | tf_op jit(solution)/shard_map/all_to_all | solution.py:123
  121.9 4.6 copy-start.3
  121.9 4.6 copy-start.4
  132.5 16.2 %all-to-all-start.6 = ((bf16[16,32,1,1,1,192]{5,1,4,3,2,0:T(8,128)(2,1)}), bf16[16,32,1,1,1,192]{5,1,4,3,2,0:T(8,128)(2,1)}, u32[]{:S(2)}, u32[]{:S(2)}) async-start(bf16[16,32,1,1,1,192]{5,1,4,3,2,0:T(8,128)(2,1)} %fusion.8), calls=%async_computation.6 | async-start | bytes 524288 | tf_op jit(solution)/shard_map/all_to_all | solution.py:132
  139.4 493.8 %all-reduce.9.cloned.1.call-start = ((), (), s32[]{:S(2)}) async-start(), calls=%async_computation.8 | async-start | bytes 5505024 | tf_op jit(solution)/shard_map/psum | solution.py:113
  139.5 1.7 copy-start.5
  139.5 1.7 copy-start.6
  139.5 1.7 copy-start.7
  148.6 29.7 %all-to-all-start.3 = ((bf16[1,32,1,16,1,192]{5,3,4,2,0,1:T(8,128)(2,1)}), bf16[1,32,1,16,1,192]{5,3,4,2,0,1:T(8,128)(2,1)S(1)}, u32[]{:S(2)}, u32[]{:S(2)}) async-start(bf16[1,32,1,16,1,192]{5,3,4,2,0,1:T(8,128)(2,1)} %copy.49), calls=%async_computation.3 | async-start | bytes 524288 | tf_op jit(solution)/shard_map/all_to_all | solution.py:122
  178.3 462.6 %all-to-all-start.7 = ((bf16[1,32,1,16,1,192]{5,3,4,2,0,1:T(8,128)(2,1)}), bf16[1,32,1,16,1,192]{5,3,4,2,0,1:T(8,128)(2,1)S(1)}, u32[]{:S(2)}, u32[]{:S(2)}) async-start(bf16[1,32,1,16,1,192]{5,3,4,2,0,1:T(8,128)(2,1)} %copy.59), calls=%async_computation.7 | async-start | bytes 524288 | tf_op jit(solution)/shard_map/all_to_all | solution.py:131
Sparse Core Ops, SparseCore 0:
  145.6 487.5 all-reduce.8
where the time goes:
time: 651 us; the launch traced here: 649 us
  waiting for transfers between devices  496 us (76%)
  starting transfers between devices  71.1 us (11%)
  local copies, waits for them, and re-layouts  49.5 us (8%)
  between operations  14.3 us (2%)
  matrix products  13.7 us (2%)
    psum x1, waiting for transfers between devices, per_device(): summed_one, summed_two = lax.psum((local_one, local_two), ('row', 'col'))  448 us
    concatenate x8, local copies, waits for them, and re-layouts, offset_taps(): return jnp.concatenate(tap_list, axis=1)  19.5 us
    all_to_all x1, waiting for transfers between devices, per_device(): lax.all_to_all(lax.all_to_all(output_local.reshape(back_shape), 'row', sp...  18.4 us
    all_to_all x1, starting transfers between devices, per_device(): lax.all_to_all(lax.all_to_all(spread_field(inputs), 'row', split_axis=3,...  17.9 us
  transfers between devices with their start and end apart: 9, of which 7 were waited for; matrix products, arithmetic and copies ran while one was open for 10% of the time, Pallas kernels for 0%

commit v1 on v0

v1 whole, which is shorter than its diff:
```python
import functools

import jax
import jax.numpy as jnp
from jax import lax
from jax.experimental import pallas as pl
from jax.experimental.pallas import tpu as pltpu
from jax.sharding import Mesh, PartitionSpec as P

C = 192
AXES = ("zl", "yh", "yl", "x", "zh", "core")
SIZES = (4, 2, 2, 4, 4, 2)
PEERS = ("x", "zh", "zl", "yh")
PLANE = ("x", "yh", "yl")
LINE = ("zh", "zl")
BF16 = jnp.bfloat16
F32 = jnp.float32
ROWS = 168
PAD = 32


def call(kernel, out_shape, scratch=(), mem=40, smem_first=False):
    out_specs = jax.tree.map(lambda _: pl.BlockSpec(memory_space=pltpu.VMEM), out_shape)

    def run(*args):
        in_specs = [pl.BlockSpec(memory_space=pltpu.VMEM) for _ in args]
        if smem_first:
            in_specs[0] = pl.BlockSpec(memory_space=pltpu.SMEM)
        return pl.pallas_call(
            kernel,
            out_shape=out_shape,
            in_specs=in_specs,
            out_specs=out_specs,
            scratch_shapes=list(scratch),
            compiler_params=pltpu.CompilerParams(vmem_limit_bytes=mem * 1024 * 1024),
        )(*args)

    return run


def gelu_parts(value):
    normal_cdf = 0.5 * (1.0 + lax.erf(value * 0.7071067811865476))
    density = jnp.exp(-0.5 * value * value) * 0.3989422804014327
    return value * normal_cdf, normal_cdf + value * density


def pack_kernel(x_ref, g_ref, o_ref):
    fields = [x_ref[...].astype(F32), g_ref[...].astype(F32)]
    for pair in range(8):
        blocks = []
        for j in (2 * pair, 2 * pair + 1):
            pieces = [f[k * 8 : k * 8 + 8, j * C : (j + 1) * C] for f in fields for k in (0, 1)]
            blocks.append(jnp.concatenate(pieces, axis=1))
        o_ref[pair * 16 : pair * 16 + 16, :] = jnp.concatenate(blocks, axis=0).astype(BF16)


def main_kernel(core_ref, r_ref, w1_ref, w2_ref, o_ref, keep_ref, send_ref, tap_ref, ft_ref, wg_ref):
    cells = 256

    def unpack(f):
        part = r_ref[:, f * 2 * C : (f + 1) * 2 * C].astype(F32)
        both = [part[:, k * C : (k + 1) * C].reshape(16, 1, 8, C) for k in (0, 1)]
        return jnp.concatenate(both, axis=1).reshape(cells, C)

    def pack(value):
        split = value.reshape(16, 2, 8, C)
        return jnp.concatenate([split[:, k].reshape(128, C) for k in (0, 1)], axis=1)

    within = lax.broadcasted_iota(jnp.int32, (cells, C), 0) % 8

    def put_taps(slot, field, step):
        for a in (-1, 0, 1):
            moved = field
            if a != 0:
                rolled = pltpu.roll(field, (-a * step) % cells, 0)
                seen = (within + a * step >= 0) & (within + a * step < 8)
                moved = jnp.where(seen, rolled, 0.0)
            tap_ref[slot, a + 1, PAD : PAD + cells, :] = moved.astype(BF16)

    def tap(slot, a, b, step):
        start = PAD + 16 * b * step
        return tap_ref[slot, a + 1, start : start + cells, :]

    zeros = jnp.zeros((PAD, C), BF16)
    for slot in range(4):
        for a in range(3):
            tap_ref[slot, a, 0:PAD, :] = zeros
            tap_ref[slot, a, PAD + cells : 2 * PAD + cells, :] = zeros

    offsets = [(a, b) for a in (-1, 0, 1) for b in (-1, 0, 1)]

    def forward(slot, w_ref, step):
        total = None
        for t, (a, b) in enumerate(offsets):
            term = jnp.dot(
                tap(slot, a, b, step), w_ref[t * C : (t + 1) * C, :], preferred_element_type=F32
            )
            total = term if total is None else total + term
        return total

    def backward(slot, w_ref, step):
        total = None
        for t, (a, b) in enumerate(offsets):
            term = lax.dot_general(
                tap(slot, -a, -b, step),
                w_ref[t * C : (t + 1) * C, :],
                (((1,), (1,)), ((), ())),
                preferred_element_type=F32,
            )
            total = term if total is None else total + term
        return total

    def weight_grad(index, field, slot, step):
        turned = field.T
        for h in (0, 1):
            ft_ref[h] = turned[:, h * 128 : h * 128 + 128]
        left = jnp.concatenate(
            [
                jnp.concatenate([ft_ref[h, pl.ds(odd, 96, stride=2), :] for h in (0, 1)], axis=1)
                for odd in (0, 1)
            ],
            axis=0,
        ).astype(BF16)
        for t, (a, b) in enumerate(offsets):
            full = jnp.dot(left, tap(slot, -a, -b, step), preferred_element_type=F32)
            even, odd = full[0:96], full[96:192]
            lanes = (
                even[:, 0:128],
                jnp.concatenate([even[:, 128:192], odd[:, 0:64]], axis=1),
                odd[:, 64:192],
            )
            for q in range(3):
                for u in range(6):
                    wg_ref[index, pl.ds(t * 18 + q * 6 + u, 16, stride=ROWS), :] = lanes[q][
                        u * 16 : u * 16 + 16
                    ]

    x = unpack(0)
    g = unpack(1)
    gelu_one, slope_one = gelu_parts(x)
    act_one = gelu_one.astype(BF16).astype(F32)
    put_taps(0, act_one, 1)
    put_taps(2, g, 2)
    hidden = (x + forward(0, w1_ref, 1)).astype(BF16).astype(F32)
    gelu_two, slope_two = gelu_parts(hidden)
    act_two = gelu_two.astype(BF16).astype(F32)
    put_taps(1, act_two, 2)
    hidden_grad = (g + backward(2, w2_ref, 2) * slope_two).astype(BF16).astype(F32)
    put_taps(3, hidden_grad, 1)
    output = hidden + forward(1, w2_ref, 2)
    input_grad = hidden_grad + backward(3, w1_ref, 1) * slope_one
    o_ref[...] = jnp.concatenate([pack(output), pack(input_grad)], axis=1).astype(BF16)
    for index in (0, 1):
        for c in range(16):
            wg_ref[index, c * ROWS + 162 : c * ROWS + 168, :] = jnp.zeros((6, 128), F32)
    weight_grad(0, act_two, 2, 2)
    weight_grad(1, act_one, 3, 1)
    core = core_ref[0]
    keep_ref[...] = wg_ref[core].astype(BF16)
    send_ref[...] = wg_ref[1 - core].astype(BF16)


def join_kernel(s_ref, o_ref, out_ref, sum_ref, row_ref):
    total = s_ref[0].astype(F32)
    for c in range(1, 16):
        total = total + s_ref[c].astype(F32)
    sum_ref[...] = total
    row_ref[...] = jnp.zeros((2, 128, 128), F32)
    for x in range(4):
        for yh in range(2):
            t = x * 2 + yh
            base = x * 32 + yh
            row_ref[0, pl.ds(base, 16, stride=2), :] = sum_ref[t * 18 : t * 18 + 16, :]
            row_ref[1, pl.ds(base, 2, stride=2), :] = sum_ref[t * 18 + 16 : t * 18 + 18, :]
            row_ref[1, pl.ds(base + 4, 3, stride=2), :] = sum_ref[144 + t * 3 : 147 + t * 3, :]
    out_ref[:, 0:768] = o_ref[...]
    for h in (0, 1):
        out_ref[:, 768 + h * 128 : 896 + h * 128] = row_ref[h].astype(BF16)


def split_kernel(r_ref, out_ref, ig_ref, z_ref):
    value = r_ref[...].astype(F32)
    for f, ref in enumerate((out_ref, ig_ref)):
        halves = []
        for k in (0, 1):
            lo = f * 2 * C + k * C
            halves.append(
                jnp.concatenate([value[j * 8 : j * 8 + 8, lo : lo + C] for j in range(16)], axis=1)
            )
        ref[...] = jnp.concatenate(halves, axis=0).astype(BF16)
    row = lax.broadcasted_iota(jnp.int32, (8, 256), 0)
    total = jnp.zeros((8, 256), F32)
    for x in range(4):
        part = value[x * 32 : x * 32 + 8, 768:1024]
        for zh in range(1, 4):
            part = part + value[x * 32 + zh * 8 : x * 32 + zh * 8 + 8, 768:1024]
        part = part + pltpu.roll(part, 4, 0)
        part = part + pltpu.roll(part, 2, 0)
        total = jnp.where(row // 2 == x, part, total)
    total = total * (1.0 / 256.0)
    mine = jnp.concatenate([total[:, 0:128], total[:, 128:256]], axis=0).astype(BF16)
    for z in range(16):
        z_ref[z] = mine


def spread_kernel(z_ref, out_ref):
    slots = [z_ref[z].astype(F32) for z in range(16)]
    rows = [s[0:8] for s in slots] + [s[8:16] for s in slots[:5]]
    mine = jnp.concatenate(rows, axis=0).astype(BF16)
    for c in range(16):
        out_ref[c] = mine


def final_kernel(core_ref, own_ref, other_ref, one_ref, two_ref, scr_ref):
    core = core_ref[0]
    for c in range(16):
        scr_ref[core, c * ROWS : (c + 1) * ROWS, :] = own_ref[c].astype(F32)
        scr_ref[1 - core, c * ROWS : (c + 1) * ROWS, :] = other_ref[c].astype(F32)
    for index, ref in enumerate((two_ref, one_ref)):
        for n in range(288):
            m, q = n // 3, n % 3
            u, c = m // 16, m % 16
            c8, yl = c // 2, c % 2
            v = q * 6 + u
            eight = scr_ref[index, pl.ds(yl * ROWS + v * 8 + c8, 8, stride=2 * ROWS), :]
            last = ((v // 3) * 2 + yl) * ROWS + (18 + v % 3) * 8 + c8
            nine = jnp.concatenate([eight, scr_ref[index, last : last + 1, :]], axis=0)
            ref[:, n * 128 : (n + 1) * 128] = nine.astype(BF16)


def exchange(value, axes):
    return lax.all_to_all(value, axes, split_axis=0, concat_axis=0, tiled=True)


def shape(*dims, dtype=BF16):
    return jax.ShapeDtypeStruct(dims, dtype)


def per_device(inputs, first_weight, second_weight, cotangent):
    core = lax.axis_index("core").astype(jnp.int32).reshape(1)
    swap = [(0, 1), (1, 0)]
    kernel_one = first_weight.reshape(9 * C, C)
    kernel_two = second_weight.reshape(9 * C, C)
    packed = call(pack_kernel, shape(128, 768))(inputs, cotangent)
    received = exchange(packed, PEERS)
    fields, keep, send = call(
        main_kernel,
        (shape(128, 768), shape(16 * ROWS, 128), shape(16 * ROWS, 128)),
        scratch=(
            pltpu.VMEM((4, 3, 256 + 2 * PAD, C), BF16),
            pltpu.VMEM((2, C, 128), F32),
            pltpu.VMEM((2, 16 * ROWS, 128), F32),
        ),
        smem_first=True,
    )(core, received, kernel_one, kernel_two)
    other = lax.ppermute(send, "core", swap)
    pair = (keep.astype(F32) + other.astype(F32)).astype(BF16).reshape(16, ROWS, 128)
    plane = exchange(pair, PLANE)
    joined = call(
        join_kernel,
        shape(128, 1024),
        scratch=(pltpu.VMEM((ROWS, 128), F32), pltpu.VMEM((2, 128, 128), F32)),
    )(plane, fields)
    back = exchange(joined, PEERS)
    output, input_grad, mine = call(
        split_kernel, (shape(16, 16 * C), shape(16, 16 * C), shape(16, 16, 128))
    )(back)
    line = exchange(mine, LINE)
    spread = call(spread_kernel, shape(16, ROWS, 128))(line)
    gathered = exchange(spread, PLANE)
    partner = lax.ppermute(gathered, "core", swap)
    one, two = call(
        final_kernel,
        (shape(9, C * C), shape(9, C * C)),
        scratch=(pltpu.VMEM((2, 16 * ROWS, 128), F32),),
        smem_first=True,
    )(core, gathered, partner)
    return output, input_grad, one, two


def solution(mesh):
    grid = Mesh(mesh.devices.reshape(SIZES), AXES)
    tile = P(("zl", "yh", "yl"), ("x", "zh", "core"))
    return jax.shard_map(
        per_device,
        mesh=grid,
        in_specs=(tile, P(), P(), tile),
        out_specs=(tile, tile, P(), P()),
        check_vma=False,
    )
```

time: 651 us -> 143 us (0.22)
  waiting for transfers between devices: 496 us -> 20.9 us
  blocking collectives: 0 us -> 71.8 us
  local copies, waits for them, and re-layouts: 49.5 us -> 5.91 us
  starting transfers between devices: 71.1 us -> 35.2 us
  matrix products: 13.7 us -> 0 us
  between operations: 14.3 us -> 0.76 us
  Pallas kernels: 0 us -> 6.65 us
    psum x1 -> x0, waiting for transfers between devices: 448 us -> none  [per_device(): summed_one, summed_two = lax.psum((local_one, local_two), ('row', 'col'))]
    all_to_all x0 -> x4, blocking collectives: none -> 71.8 us  [exchange(): return lax.all_to_all(value, axes, split_axis=0, concat_axis=0, tiled=True)]
    all_to_all x8 -> x1, starting transfers between devices: 71.1 us -> 23.1 us  [exchange(): return lax.all_to_all(value, axes, split_axis=0, concat_axis=0, tiled=True)]
    all_to_all x8 -> x1, waiting for transfers between devices: 47.9 us -> 17.4 us  [exchange(): return lax.all_to_all(value, axes, split_axis=0, concat_axis=0, tiled=True)]
    concatenate x8 -> x0, local copies, waits for them, and re-layouts: 19.5 us -> none  [offset_taps(): return jnp.concatenate(tap_list, axis=1)]
    dot_general x6 -> x0, matrix products: 13.7 us -> none  [the longest x1 3.18 us: per_device(): jnp.dot(hidden_taps, flip_kernel(kernel_one), preferred_element_type=jnp....]
    ppermute x0 -> x2, starting transfers between devices: none -> 12.1 us  [the longest x1 6.91 us: per_device(): partner = lax.ppermute(gathered, 'core', swap)]
    reshape x10 -> x2, local copies, waits for them, and re-layouts: 13.2 us -> 2.23 us  [the longest x1 1.11 us: per_device(): kernel_one = first_weight.reshape(9 * C, C)]
  transfers between devices with their start and end apart: 9 -> 3, of which waited for: 7 -> 3; matrix products, arithmetic and copies ran while one was open for 10% -> 2% of each run, Pallas kernels for 0% -> 0%
where the time goes in v1:
time: 143 us
  blocking collectives  71.8 us (50%)
  starting transfers between devices  35.2 us (25%)
  waiting for transfers between devices  20.9 us (15%)
  Pallas kernels  6.65 us (5%)
  local copies, waits for them, and re-layouts  5.91 us (4%)
  other arithmetic  1.69 us (1%)
    all_to_all x4, blocking collectives, exchange(): return lax.all_to_all(value, axes, split_axis=0, concat_axis=0, tiled=True)  71.8 us
    all_to_all x1, starting transfers between devices, exchange(): return lax.all_to_all(value, axes, split_axis=0, concat_axis=0, tiled=True)  23.1 us
    all_to_all x1, waiting for transfers between devices, exchange(): return lax.all_to_all(value, axes, split_axis=0, concat_axis=0, tiled=True)  17.4 us
    ppermute x1, starting transfers between devices, per_device(): partner = lax.ppermute(gathered, 'core', swap)  6.91 us
    pallas_call x6, Pallas kernels, run(): pl.pallas_call(kernel, out_shape=out_shape, in_specs=in_specs, out_specs=...  6.65 us
    ppermute x1, starting transfers between devices, per_device(): other = lax.ppermute(send, 'core', swap)  5.23 us
    unnamed x14, local copies, waits for them, and re-layouts  3.17 us
  transfers between devices with their start and end apart: 3, of which 3 were waited for; matrix products, arithmetic and copies ran while one was open for 2% of the time, Pallas kernels for 0%

profile of v1, /device:TPU:1, one launch (start us, length us, event | category | flops | bytes accessed | tf_op | source)
XLA Modules:
  0.0 143.0 jit_solution(17200958149757263963)
XLA Ops:
  0.6 0.0 copy-start
  0.6 0.9 copy-done
  1.5 0.9 copy-done.1
  2.4 0.1 shard_map.75
  2.5 0.5 broadcast
  3.0 0.7 reduce
  3.8 0.7 reshape.28
  4.5 23.1 %all-to-all-start = ((bf16[128,2,384]{2,1,0:T(2,128)(2,1)}), bf16[128,2,384]{2,1,0:T(2,128)(2,1)S(1)}, u32[]{:S(2)}, u32[]{:S(2)}) async-start(bf16[128,2,384]{2,1,0:T(2,128)(2,1)} %reshape.28), calls=%async_computation | async-start | bytes 393216 | tf_op jit(solution)/shard_map/all_to_all | solution.py:232
  27.6 0.0 copy-done.2
  27.6 1.1 reshape.25.w1_ref
  28.7 0.0 copy-done.3
  28.7 1.1 reshape.26.w2_ref
  29.9 17.4 %all-to-all-done = bf16[128,2,384]{2,1,0:T(2,128)(2,1)S(1)} async-done(((bf16[128,2,384]{2,1,0:T(2,128)(2,1)}), bf16[128,2,384]{2,1,0:T(2,128)(2,1)S(1)}, u32[]{:S(2)}, u32[]{:S(2)}) %all-to-all-start) | async-done | bytes 196640 | tf_op jit(solution)/shard_map/all_to_all | solution.py:232
  47.3 0.1 reshape.29
  47.5 2.8 %shard_map.76 = (bf16[128,768]{1,0:T(8,128)(2,1)S(1)}, bf16[2688,128]{1,0:T(8,128)(2,1)S(1)}, bf16[2688,128]{1,0:T(8,128)(2,1)S(1)}) custom-call(s32[1]{0:T(128)} %bitcast.core_ref, bf16[128,768]{1,0:T(8,128)(2,1)S(1)} %bitcast.12, bf16[1728,192]{1,0:T(8,128)(2,1)S(1)} %reshape.25.w1_ref, bf16[1728,192]{1,0:T(8,128)(2,1)S(1)} %reshape.26.w2_ref), custom_call_target="tpu_custom_call" | custom-call | tf_op jit(solution)/shard_map/pallas_call | solution.py:29
  50.3 5.2 %collective-permute-start = (bf16[2688,128]{1,0:T(8,128)(2,1)S(1)}, bf16[2688,128]{1,0:T(8,128)(2,1)S(1)}, u32[]{:S(2)}, u32[]{:S(2)}) collective-permute-start(bf16[2688,128]{1,0:T(8,128)(2,1)S(1)} %get-tuple-element.13), channel_id=1, source_target_pairs={{0,1},{1,0},{2,3},{3,2},{4,5},{5,4},{6,7},{7,6},{8,9},{9,8},{10,11... | collective-permute-start | bytes 2064392 | tf_op jit(solution)/shard_map/ppermute | solution.py:256
  55.5 1.7 %collective-permute-done = bf16[2688,128]{1,0:T(8,128)(2,1)S(1)} collective-permute-done((bf16[2688,128]{1,0:T(8,128)(2,1)S(1)}, bf16[2688,128]{1,0:T(8,128)(2,1)S(1)}, u32[]{:S(2)}, u32[]{:S(2)}) %collective-permute-start) | collective-permute-done | bytes 688160 | tf_op jit(solution)/shard_map/ppermute | solution.py:256
  57.3 0.2 add_convert_fusion
  57.5 15.3 %all_to_all.37.s_ref = bf16[16,168,128]{2,1,0:T(8,128)(2,1)S(1)} all-to-all(bf16[16,168,128]{2,1,0:T(8,128)(2,1)S(1)} %bitcast.14), channel_id=1, replica_groups=mesh['zl'=4,'yh'=2,'yl'=2,'x'=4,'zh'=4,'core'=2] {'x','yh','yl'}, dimensions={0} | all-to-all | bytes 1376256 | tf_op jit(solution)/shard_map/all_to_all | solution.py:232
  72.8 0.1 shard_map.77
  72.9 0.8 reduce.1
  73.7 0.2 reshape.30
  73.9 27.8 %all_to_all.38 = bf16[128,2,512]{2,1,0:T(2,128)(2,1)S(1)} all-to-all(bf16[128,2,512]{2,1,0:T(2,128)(2,1)S(1)} %reshape.30), channel_id=1, replica_groups=mesh['zl'=4,'yh'=2,'yl'=2,'x'=4,'zh'=4,'core'=2] {'x','zh','zl','yh'}, dimensions={0} | all-to-all | bytes 524288 | tf_op jit(solution)/shard_map/all_to_all | solution.py:232
  101.7 0.2 reshape.31
  101.9 0.1 copy.16
  102.0 0.8 shard_map.78
  102.8 15.6 %all_to_all.39.z_ref = bf16[16,16,128]{2,1,0:T(8,128)(2,1)S(1)} all-to-all(bf16[16,16,128]{2,1,0:T(8,128)(2,1)S(1)} %get-tuple-element.17), channel_id=1, replica_groups=mesh['zl'=4,'yh'=2,'yl'=2,'x'=4,'zh'=4,'core'=2] {'zh','zl'}, dimensions={0} | all-to-all | bytes 131072 | tf_op jit(solution)/shard_map/all_to_all | solution.py:232
  118.4 0.1 shard_map.79
  118.5 13.1 %all_to_all.40.own_ref = bf16[16,168,128]{2,1,0:T(8,128)(2,1)S(1)} all-to-all(bf16[16,168,128]{2,1,0:T(8,128)(2,1)S(1)} %shard_map.79), channel_id=1, replica_groups=mesh['zl'=4,'yh'=2,'yl'=2,'x'=4,'zh'=4,'core'=2] {'x','yh','yl'}, dimensions={0} | all-to-all | bytes 1376256 | tf_op jit(solution)/shard_map/all_to_all | solution.py:232
  131.6 6.9 %collective-permute-start.1 = (bf16[16,168,128]{2,1,0:T(8,128)(2,1)S(1)}, bf16[16,168,128]{2,1,0:T(8,128)(2,1)S(1)}, u32[]{:S(2)}, u32[]{:S(2)}) collective-permute-start(bf16[16,168,128]{2,1,0:T(8,128)(2,1)S(1)} %all_to_all.40.own_ref), channel_id=1, source_target_pairs={{0,1},{1,0},{2,3},{3,2},{4,5},{5,4},{6,7},{7,6},{8,9},{9,8},{10,11... | collective-permute-start | bytes 2064392 | tf_op jit(solution)/shard_map/ppermute | solution.py:271
  138.5 1.7 %collective-permute-done.1.other_ref = bf16[16,168,128]{2,1,0:T(8,128)(2,1)S(1)} collective-permute-done((bf16[16,168,128]{2,1,0:T(8,128)(2,1)S(1)}, bf16[16,168,128]{2,1,0:T(8,128)(2,1)S(1)}, u32[]{:S(2)}, u32[]{:S(2)}) %collective-permute-start.1) | collective-permute-done | bytes 688160 | tf_op jit(solution)/shard_map/ppermute | solution.py:271
  140.2 2.7 %shard_map.80 = (bf16[9,36864]{1,0:T(8,128)(2,1)}, bf16[9,36864]{1,0:T(8,128)(2,1)}) custom-call(s32[1]{0:T(128)} %bitcast.core_ref, bf16[16,168,128]{2,1,0:T(8,128)(2,1)S(1)} %all_to_all.40.own_ref, bf16[16,168,128]{2,1,0:T(8,128)(2,1)S(1)} %collective-permute-done.1.other_ref), custom_call_target="tpu_custom_call" | custom-call | tf_op jit(solution)/shard_map/pallas_call | solution.py:29
  (4 shorter events, 0.0 us)
Async XLA Ops:
  0.6 0.9 copy-start
  1.5 0.9 copy-start.1
  2.4 25.2 %copy-start.2 = (bf16[9,36864]{1,0:T(8,128)(2,1)S(1)}, bf16[9,36864]{1,0:T(8,128)(2,1)}, u32[]{:S(2)}) copy-start(bf16[9,36864]{1,0:T(8,128)(2,1)} %param.5) | copy-start | bytes 1990660
  4.5 24.2 %copy-start.3 = (bf16[9,36864]{1,0:T(8,128)(2,1)S(1)}, bf16[9,36864]{1,0:T(8,128)(2,1)}, u32[]{:S(2)}) copy-start(bf16[9,36864]{1,0:T(8,128)(2,1)} %param.6) | copy-start | bytes 1990660
  4.5 42.8 %all-to-all-start = ((bf16[128,2,384]{2,1,0:T(2,128)(2,1)}), bf16[128,2,384]{2,1,0:T(2,128)(2,1)S(1)}, u32[]{:S(2)}, u32[]{:S(2)}) async-start(bf16[128,2,384]{2,1,0:T(2,128)(2,1)} %reshape.28), calls=%async_computation | async-start | bytes 393216 | tf_op jit(solution)/shard_map/all_to_all | solution.py:232
  50.3 7.0 %collective-permute-start = (bf16[2688,128]{1,0:T(8,128)(2,1)S(1)}, bf16[2688,128]{1,0:T(8,128)(2,1)S(1)}, u32[]{:S(2)}, u32[]{:S(2)}) collective-permute-start(bf16[2688,128]{1,0:T(8,128)(2,1)S(1)} %get-tuple-element.13), channel_id=1, source_target_pairs={{0,1},{1,0},{2,3},{3,2},{4,5},{5,4},{6,7},{7,6},{8,9},{9,8},{10,11... | collective-permute-start | bytes 2064392 | tf_op jit(solution)/shard_map/ppermute | solution.py:256
  131.6 8.7 %collective-permute-start.1 = (bf16[16,168,128]{2,1,0:T(8,128)(2,1)S(1)}, bf16[16,168,128]{2,1,0:T(8,128)(2,1)S(1)}, u32[]{:S(2)}, u32[]{:S(2)}) collective-permute-start(bf16[16,168,128]{2,1,0:T(8,128)(2,1)S(1)} %all_to_all.40.own_ref), channel_id=1, source_target_pairs={{0,1},{1,0},{2,3},{3,2},{4,5},{5,4},{6,7},{7,6},{8,9},{9,8},{10,11... | collective-permute-start | bytes 2064392 | tf_op jit(solution)/shard_map/ppermute | solution.py:271

commit v2 on v1

--- a/solution.py
+++ b/solution.py
@@ -1,5 +1,3 @@
-import functools
-
 import jax
 import jax.numpy as jnp
 from jax import lax
@@ -10,12 +8,13 @@
 C = 192
 AXES = ("zl", "yh", "yl", "x", "zh", "core")
 SIZES = (4, 2, 2, 4, 4, 2)
-PEERS = ("x", "zh", "zl", "yh")
-PLANE = ("x", "yh", "yl")
 LINE = ("zh", "zl")
+BLOCK = ("x", "yh")
+PLANE = ("yl", "x", "yh")
 BF16 = jnp.bfloat16
 F32 = jnp.float32
-ROWS = 168
+ROWS = 176
+FIELD = 96
 PAD = 32
 
 
@@ -46,35 +45,57 @@
 
 def pack_kernel(x_ref, g_ref, o_ref):
     fields = [x_ref[...].astype(F32), g_ref[...].astype(F32)]
-    for pair in range(8):
-        blocks = []
-        for j in (2 * pair, 2 * pair + 1):
-            pieces = [f[k * 8 : k * 8 + 8, j * C : (j + 1) * C] for f in fields for k in (0, 1)]
-            blocks.append(jnp.concatenate(pieces, axis=1))
-        o_ref[pair * 16 : pair * 16 + 16, :] = jnp.concatenate(blocks, axis=0).astype(BF16)
+    for z in range(16):
+        pieces = [f[k * 8 : k * 8 + 8, z * C : (z + 1) * C] for f in fields for k in (0, 1)]
+        wide = jnp.concatenate(pieces, axis=1)
+        tiles = [wide[:, t * 128 : t * 128 + 128] for t in range(6)]
+        o_ref[z] = jnp.concatenate(tiles, axis=0).astype(BF16)
+
+
+def relay_kernel(r_ref, o_ref, scr_ref):
+    for z in range(16):
+        scr_ref[z * 48 : z * 48 + 48, :] = r_ref[z].astype(F32)
+    for e in range(8):
+        tiles = [scr_ref[pl.ds(t * 8 + e, 16, stride=48), :] for t in range(6)]
+        o_ref[e] = jnp.concatenate(tiles, axis=0).astype(BF16)
 
 
 def main_kernel(core_ref, r_ref, w1_ref, w2_ref, o_ref, keep_ref, send_ref, tap_ref, ft_ref, wg_ref):
     cells = 256
 
     def unpack(f):
-        part = r_ref[:, f * 2 * C : (f + 1) * 2 * C].astype(F32)
+        tiles = []
+        for t in range(3 * f, 3 * f + 3):
+            pieces = []
+            for x in range(4):
+                pair = [r_ref[x * 2 + yh, t * 16 : t * 16 + 16, :].astype(F32) for yh in (0, 1)]
+                for zh in range(4):
+                    pieces += [p[zh * 4 : zh * 4 + 4] for p in pair]
+            tiles.append(jnp.concatenate(pieces, axis=0))
+        part = jnp.concatenate(tiles, axis=1)
         both = [part[:, k * C : (k + 1) * C].reshape(16, 1, 8, C) for k in (0, 1)]
         return jnp.concatenate(both, axis=1).reshape(cells, C)
 
     def pack(value):
         split = value.reshape(16, 2, 8, C)
-        return jnp.concatenate([split[:, k].reshape(128, C) for k in (0, 1)], axis=1)
+        wide = jnp.concatenate([split[:, k].reshape(128, C) for k in (0, 1)], axis=1)
+        return [wide[:, t * 128 : t * 128 + 128] for t in range(3)]
 
     within = lax.broadcasted_iota(jnp.int32, (cells, C), 0) % 8
+    yh_of, zl_of = within // 4, within % 4
+
+    def ahead(field, rows):
+        return pltpu.roll(field, (-rows) % cells, 0)
 
     def put_taps(slot, field, step):
         for a in (-1, 0, 1):
             moved = field
-            if a != 0:
-                rolled = pltpu.roll(field, (-a * step) % cells, 0)
-                seen = (within + a * step >= 0) & (within + a * step < 8)
-                moved = jnp.where(seen, rolled, 0.0)
+            if a != 0 and step == 2:
+                moved = jnp.where((zl_of + a >= 0) & (zl_of + a < 4), ahead(field, a), 0.0)
+            elif a != 0:
+                start = 0 if a == 1 else 1
+                crossed = jnp.where((zl_of + a >= 0) & (zl_of + a < 4), ahead(field, -3 * a), 0.0)
+                moved = jnp.where(yh_of == start, ahead(field, 4 * a), crossed)
             tap_ref[slot, a + 1, PAD : PAD + cells, :] = moved.astype(BF16)
 
     def tap(slot, a, b, step):
@@ -149,64 +170,67 @@
     put_taps(3, hidden_grad, 1)
     output = hidden + forward(1, w2_ref, 2)
     input_grad = hidden_grad + backward(3, w1_ref, 1) * slope_one
-    o_ref[...] = jnp.concatenate([pack(output), pack(input_grad)], axis=1).astype(BF16)
+    tiles = pack(output) + pack(input_grad)
+    for x in range(4):
+        for yh in (0, 1):
+            pieces = []
+            for tile in tiles:
+                for zh in range(4):
+                    start = (x * 4 + zh) * 8 + yh * 4
+                    pieces.append(tile[start : start + 4])
+            o_ref[x * 2 + yh] = jnp.concatenate(pieces, axis=0).astype(BF16)
     for index in (0, 1):
         for c in range(16):
-            wg_ref[index, c * ROWS + 162 : c * ROWS + 168, :] = jnp.zeros((6, 128), F32)
+            wg_ref[index, c * ROWS + 162 : (c + 1) * ROWS, :] = jnp.zeros((ROWS - 162, 128), F32)
     weight_grad(0, act_two, 2, 2)
     weight_grad(1, act_one, 3, 1)
     core = core_ref[0]
-    keep_ref[...] = wg_ref[core].astype(BF16)
-    send_ref[...] = wg_ref[1 - core].astype(BF16)
-
-
-def join_kernel(s_ref, o_ref, out_ref, sum_ref, row_ref):
-    total = s_ref[0].astype(F32)
+    for c in range(16):
+        keep_ref[c] = wg_ref[core, c * ROWS : (c + 1) * ROWS, :].astype(BF16)
+        send_ref[c] = wg_ref[1 - core, c * ROWS : (c + 1) * ROWS, :].astype(BF16)
+
+
+def join_kernel(f_ref, keep_ref, other_ref, o_ref):
+    for c in range(16):
+        o_ref[c, 0:FIELD, :] = f_ref[c % 8]
+        pair = keep_ref[c].astype(F32) + other_ref[c].astype(F32)
+        o_ref[c, FIELD : FIELD + ROWS, :] = pair.astype(BF16)
+
+
+def line_kernel(yl_ref, s_ref, o_ref, sum_ref, scr_ref):
+    yl = yl_ref[0]
+    total = s_ref[0, FIELD : FIELD + ROWS, :].astype(F32)
     for c in range(1, 16):
-        total = total + s_ref[c].astype(F32)
-    sum_ref[...] = total
-    row_ref[...] = jnp.zeros((2, 128, 128), F32)
-    for x in range(4):
-        for yh in range(2):
-            t = x * 2 + yh
-            base = x * 32 + yh
-            row_ref[0, pl.ds(base, 16, stride=2), :] = sum_ref[t * 18 : t * 18 + 16, :]
-            row_ref[1, pl.ds(base, 2, stride=2), :] = sum_ref[t * 18 + 16 : t * 18 + 18, :]
-            row_ref[1, pl.ds(base + 4, 3, stride=2), :] = sum_ref[144 + t * 3 : 147 + t * 3, :]
-    out_ref[:, 0:768] = o_ref[...]
-    for h in (0, 1):
-        out_ref[:, 768 + h * 128 : 896 + h * 128] = row_ref[h].astype(BF16)
+        total = total + s_ref[c, FIELD : FIELD + ROWS, :].astype(F32)
+    sum_ref[0:ROWS, :] = total
+    sum_ref[ROWS : ROWS + 8, :] = jnp.zeros((8, 128), F32)
+    for s in range(8):
+        scr_ref[s * FIELD : (s + 1) * FIELD, :] = s_ref[yl * 8 + s, 0:FIELD, :].astype(F32)
+    for z in range(16):
+        tiles = [scr_ref[pl.ds(t * 16 + z, 8, stride=FIELD), :] for t in range(6)]
+        tiles.append(sum_ref[z * 11 : z * 11 + 16, :])
+        o_ref[z] = jnp.concatenate(tiles, axis=0).astype(BF16)
 
 
 def split_kernel(r_ref, out_ref, ig_ref, z_ref):
-    value = r_ref[...].astype(F32)
-    for f, ref in enumerate((out_ref, ig_ref)):
-        halves = []
-        for k in (0, 1):
-            lo = f * 2 * C + k * C
-            halves.append(
-                jnp.concatenate([value[j * 8 : j * 8 + 8, lo : lo + C] for j in range(16)], axis=1)
-            )
-        ref[...] = jnp.concatenate(halves, axis=0).astype(BF16)
-    row = lax.broadcasted_iota(jnp.int32, (8, 256), 0)
-    total = jnp.zeros((8, 256), F32)
-    for x in range(4):
-        part = value[x * 32 : x * 32 + 8, 768:1024]
-        for zh in range(1, 4):
-            part = part + value[x * 32 + zh * 8 : x * 32 + zh * 8 + 8, 768:1024]
-        part = part + pltpu.roll(part, 4, 0)
-        part = part + pltpu.roll(part, 2, 0)
-        total = jnp.where(row // 2 == x, part, total)
-    total = total * (1.0 / 256.0)
-    mine = jnp.concatenate([total[:, 0:128], total[:, 128:256]], axis=0).astype(BF16)
+    total = r_ref[0, 48:64, :].astype(F32)
+    for z in range(1, 16):
+        total = total + r_ref[z, 48:64, :].astype(F32)
+    mine = (total * (1.0 / 256.0)).astype(BF16)
     for z in range(16):
         z_ref[z] = mine
-
-
-def spread_kernel(z_ref, out_ref):
-    slots = [z_ref[z].astype(F32) for z in range(16)]
-    rows = [s[0:8] for s in slots] + [s[8:16] for s in slots[:5]]
-    mine = jnp.concatenate(rows, axis=0).astype(BF16)
+    for z in range(16):
+        value = r_ref[z, 0:48, :].astype(F32)
+        wide = jnp.concatenate([value[t * 8 : t * 8 + 8] for t in range(6)], axis=1)
+        for f, ref in enumerate((out_ref, ig_ref)):
+            halves = [wide[:, (2 * f + k) * C : (2 * f + k + 1) * C] for k in (0, 1)]
+            ref[:, z * C : (z + 1) * C] = jnp.concatenate(halves, axis=0).astype(BF16)
+
+
+def spread_kernel(z_ref, out_ref, scr_ref):
+    for z in range(16):
+        scr_ref[z * 11 : z * 11 + 16, :] = z_ref[z].astype(F32)
+    mine = scr_ref[0:ROWS, :].astype(BF16)
     for c in range(16):
         out_ref[c] = mine
 
@@ -219,12 +243,9 @@
     for index, ref in enumerate((two_ref, one_ref)):
         for n in range(288):
             m, q = n // 3, n % 3
-            u, c = m // 16, m % 16
-            c8, yl = c // 2, c % 2
-            v = q * 6 + u
-            eight = scr_ref[index, pl.ds(yl * ROWS + v * 8 + c8, 8, stride=2 * ROWS), :]
-            last = ((v // 3) * 2 + yl) * ROWS + (18 + v % 3) * 8 + c8
-            nine = jnp.concatenate([eight, scr_ref[index, last : last + 1, :]], axis=0)
+            base = (m % 16) * ROWS + q * 6 + m // 16
+            eight = scr_ref[index, pl.ds(base, 8, stride=18), :]
+            nine = jnp.concatenate([eight, scr_ref[index, base + 144 : base + 145, :]], axis=0)
             ref[:, n * 128 : (n + 1) * 128] = nine.astype(BF16)
 
 
@@ -238,14 +259,17 @@
 
 def per_device(inputs, first_weight, second_weight, cotangent):
     core = lax.axis_index("core").astype(jnp.int32).reshape(1)
+    half = lax.axis_index("yl").astype(jnp.int32).reshape(1)
     swap = [(0, 1), (1, 0)]
     kernel_one = first_weight.reshape(9 * C, C)
     kernel_two = second_weight.reshape(9 * C, C)
-    packed = call(pack_kernel, shape(128, 768))(inputs, cotangent)
-    received = exchange(packed, PEERS)
+    packed = call(pack_kernel, shape(16, 48, 128))(inputs, cotangent)
+    line_in = exchange(packed, LINE)
+    relayed = call(relay_kernel, shape(8, FIELD, 128), scratch=(pltpu.VMEM((768, 128), F32),))(line_in)
+    received = exchange(relayed, BLOCK)
     fields, keep, send = call(
         main_kernel,
-        (shape(128, 768), shape(16 * ROWS, 128), shape(16 * ROWS, 128)),
+        (shape(8, FIELD, 128), shape(16, ROWS, 128), shape(16, ROWS, 128)),
         scratch=(
             pltpu.VMEM((4, 3, 256 + 2 * PAD, C), BF16),
             pltpu.VMEM((2, C, 128), F32),
@@ -254,19 +278,22 @@
         smem_first=True,
     )(core, received, kernel_one, kernel_two)
     other = lax.ppermute(send, "core", swap)
-    pair = (keep.astype(F32) + other.astype(F32)).astype(BF16).reshape(16, ROWS, 128)
-    plane = exchange(pair, PLANE)
-    joined = call(
-        join_kernel,
-        shape(128, 1024),
-        scratch=(pltpu.VMEM((ROWS, 128), F32), pltpu.VMEM((2, 128, 128), F32)),
-    )(plane, fields)
-    back = exchange(joined, PEERS)
+    joined = call(join_kernel, shape(16, FIELD + ROWS, 128))(fields, keep, other)
+    plane = exchange(joined, PLANE)
+    to_line = call(
+        line_kernel,
+        shape(16, 64, 128),
+        scratch=(pltpu.VMEM((ROWS + 8, 128), F32), pltpu.VMEM((8 * FIELD, 128), F32)),
+        smem_first=True,
+    )(half, plane)
+    back = exchange(to_line, LINE)
     output, input_grad, mine = call(
         split_kernel, (shape(16, 16 * C), shape(16, 16 * C), shape(16, 16, 128))
     )(back)
     line = exchange(mine, LINE)
-    spread = call(spread_kernel, shape(16, ROWS, 128))(line)
+    spread = call(
+        spread_kernel, shape(16, ROWS, 128), scratch=(pltpu.VMEM((ROWS + 8, 128), F32),)
+    )(line)
     gathered = exchange(spread, PLANE)
     partner = lax.ppermute(gathered, "core", swap)
     one, two = call(

time: 143 us -> 148 us (1.035)
  blocking collectives: 71.8 us -> 82.1 us
  starting transfers between devices: 35.2 us -> 25.1 us
  waiting for transfers between devices: 20.9 us -> 26.5 us
  Pallas kernels: 6.65 us -> 8.86 us
  local copies, waits for them, and re-layouts: 5.91 us -> 4.01 us
  other arithmetic: 1.69 us -> 0 us
    all_to_all x1 -> x2, starting transfers between devices: 23.1 us -> 10.5 us  [exchange(): return lax.all_to_all(value, axes, split_axis=0, concat_axis=0, tiled=True)]
    all_to_all x4, blocking collectives: 71.8 us -> 82.1 us  [exchange(): return lax.all_to_all(value, axes, split_axis=0, concat_axis=0, tiled=True)]
    all_to_all x1 -> x2, waiting for transfers between devices: 17.4 us -> 22.9 us  [exchange(): return lax.all_to_all(value, axes, split_axis=0, concat_axis=0, tiled=True)]
    ppermute x1, starting transfers between devices: 5.23 us -> 8.17 us  [per_device(): other = lax.ppermute(send, 'core', swap)]
    pallas_call x6 -> x8, Pallas kernels: 6.65 us -> 8.86 us  [run(): pl.pallas_call(kernel, out_shape=out_shape, in_specs=in_specs, out_specs=...]
    all_to_all x2 -> x0, other arithmetic: 1.51 us -> none  [exchange(): return lax.all_to_all(value, axes, split_axis=0, concat_axis=0, tiled=True)]
    unnamed x14 -> x8, local copies, waits for them, and re-layouts: 3.17 us -> 1.79 us
  transfers between devices with their start and end apart: 3 -> 4, of which waited for: 3 -> 4; matrix products, arithmetic and copies ran while one was open for 2% -> 2% of each run, Pallas kernels for 0% -> 0%
where the time goes in v2:
time: 148 us; the launch traced here: 147 us
  blocking collectives  82.1 us (55%)
  waiting for transfers between devices  26.5 us (18%)
  starting transfers between devices  25.1 us (17%)
  Pallas kernels  8.86 us (6%)
  local copies, waits for them, and re-layouts  4.01 us (3%)
    all_to_all x4, blocking collectives, exchange(): return lax.all_to_all(value, axes, split_axis=0, concat_axis=0, tiled=True)  82.1 us
    all_to_all x2, waiting for transfers between devices, exchange(): return lax.all_to_all(value, axes, split_axis=0, concat_axis=0, tiled=True)  22.9 us
    all_to_all x2, starting transfers between devices, exchange(): return lax.all_to_all(value, axes, split_axis=0, concat_axis=0, tiled=True)  10.5 us
    pallas_call x8, Pallas kernels, run(): pl.pallas_call(kernel, out_shape=out_shape, in_specs=in_specs, out_specs=...  8.86 us
    ppermute x1, starting transfers between devices, per_device(): other = lax.ppermute(send, 'core', swap)  8.17 us
    ppermute x1, starting transfers between devices, per_device(): partner = lax.ppermute(gathered, 'core', swap)  6.49 us
  transfers between devices with their start and end apart: 4, of which 4 were waited for; matrix products, arithmetic and copies ran while one was open for 2% of the time, Pallas kernels for 0%

profile of v2, /device:TPU:1, one launch (start us, length us, event | category | flops | bytes accessed | tf_op | source)
XLA Modules:
  0.0 147.3 jit_solution(7300554250829945284)
XLA Ops:
  0.6 0.0 copy-start
  0.6 0.9 copy-done
  1.5 0.0 copy-start.1
  1.5 0.9 copy-done.1
  2.4 0.0 copy-start.2
  2.4 0.1 shard_map.75
  2.5 28.2 %all_to_all.30.r_ref = bf16[16,48,128]{2,1,0:T(8,128)(2,1)S(1)} all-to-all(bf16[16,48,128]{2,1,0:T(8,128)(2,1)S(1)} %shard_map.75), channel_id=1, replica_groups=mesh['zl'=4,'yh'=2,'yl'=2,'x'=4,'zh'=4,'core'=2] {'zh','zl'}, dimensions={0} | all-to-all | bytes 393216 | tf_op jit(solution)/shard_map/all_to_all | solution.py:253
  30.8 0.8 shard_map.76
  31.6 0.0 copy-start.3
  31.6 6.8 %all-to-all-start.1 = ((bf16[8,96,128]{2,1,0:T(8,128)(2,1)}), bf16[8,96,128]{2,1,0:T(8,128)(2,1)S(1)}, u32[]{:S(2)}, u32[]{:S(2)}) async-start(bf16[8,96,128]{2,1,0:T(8,128)(2,1)} %shard_map.76), calls=%async_computation.1 | async-start | bytes 393216 | tf_op jit(solution)/shard_map/all_to_all | solution.py:253
  38.4 0.0 copy-done.2
  38.4 1.1 reshape.22.w1_ref
  39.5 0.0 copy-done.3
  39.5 1.1 reshape.23.w2_ref
  40.6 4.8 %all-to-all-done.1.r_ref = bf16[8,96,128]{2,1,0:T(8,128)(2,1)S(1)} async-done(((bf16[8,96,128]{2,1,0:T(8,128)(2,1)}), bf16[8,96,128]{2,1,0:T(8,128)(2,1)S(1)}, u32[]{:S(2)}, u32[]{:S(2)}) %all-to-all-start.1) | async-done | bytes 196640 | tf_op jit(solution)/shard_map/all_to_all | solution.py:253
  45.4 3.4 %shard_map.77 = (bf16[8,96,128]{2,1,0:T(8,128)(2,1)S(1)}, bf16[16,176,128]{2,1,0:T(8,128)(2,1)S(1)}, bf16[16,176,128]{2,1,0:T(8,128)(2,1)S(1)}) custom-call(s32[1]{0:T(128)} %bitcast.1.core_ref, bf16[8,96,128]{2,1,0:T(8,128)(2,1)S(1)} %all-to-all-done.1.r_ref, bf16[1728,192]{1,0:T(8,128)(2,1)S(1)} %reshape.22.w1_ref, bf16[1728,192]{1,0:T(8,128)(2,1)S(1)} %reshape.23.w2_ref), custom_call_target="tpu_custom_call" | custom-call | tf_op jit(solution)/shard_map/pallas_call | solution.py:28
  48.8 8.2 %collective-permute-start = (bf16[16,176,128]{2,1,0:T(8,128)(2,1)S(1)}, bf16[16,176,128]{2,1,0:T(8,128)(2,1)S(1)}, u32[]{:S(2)}, u32[]{:S(2)}) collective-permute-start(bf16[16,176,128]{2,1,0:T(8,128)(2,1)S(1)} %get-tuple-element.14), channel_id=1, source_target_pairs={{0,1},{1,0},{2,3},{3,2},{4,5},{5,4},{6,7},{7,6},{8,9},{9,8},{10,11... | collective-permute-start | bytes 2162696 | tf_op jit(solution)/shard_map/ppermute | solution.py:280
  57.0 1.8 %collective-permute-done.other_ref = bf16[16,176,128]{2,1,0:T(8,128)(2,1)S(1)} collective-permute-done((bf16[16,176,128]{2,1,0:T(8,128)(2,1)S(1)}, bf16[16,176,128]{2,1,0:T(8,128)(2,1)S(1)}, u32[]{:S(2)}, u32[]{:S(2)}) %collective-permute-start) | collective-permute-done | bytes 720928 | tf_op jit(solution)/shard_map/ppermute | solution.py:280
  58.8 1.2 shard_map.78
  60.0 3.7 %all-to-all-start.2 = ((bf16[16,272,128]{2,1,0:T(8,128)(2,1)}), bf16[16,272,128]{2,1,0:T(8,128)(2,1)S(1)}, u32[]{:S(2)}, u32[]{:S(2)}) async-start(bf16[16,272,128]{2,1,0:T(8,128)(2,1)} %shard_map.78), calls=%async_computation.2 | async-start | bytes 2228224 | tf_op jit(solution)/shard_map/all_to_all | solution.py:253
  63.7 18.1 %all-to-all-done.2.s_ref = bf16[16,272,128]{2,1,0:T(8,128)(2,1)S(1)} async-done(((bf16[16,272,128]{2,1,0:T(8,128)(2,1)}), bf16[16,272,128]{2,1,0:T(8,128)(2,1)S(1)}, u32[]{:S(2)}, u32[]{:S(2)}) %all-to-all-start.2) | async-done | bytes 1114144 | tf_op jit(solution)/shard_map/all_to_all | solution.py:253
  81.8 0.3 shard_map.79
  82.1 17.2 %all_to_all.31.r_ref = bf16[16,64,128]{2,1,0:T(8,128)(2,1)S(1)} all-to-all(bf16[16,64,128]{2,1,0:T(8,128)(2,1)S(1)} %shard_map.79), channel_id=1, replica_groups=mesh['zl'=4,'yh'=2,'yl'=2,'x'=4,'zh'=4,'core'=2] {'zh','zl'}, dimensions={0} | all-to-all | bytes 524288 | tf_op jit(solution)/shard_map/all_to_all | solution.py:253
  99.4 0.9 shard_map.80
  100.2 21.3 %all_to_all.32.z_ref = bf16[16,16,128]{2,1,0:T(8,128)(2,1)S(1)} all-to-all(bf16[16,16,128]{2,1,0:T(8,128)(2,1)S(1)} %get-tuple-element.17), channel_id=1, replica_groups=mesh['zl'=4,'yh'=2,'yl'=2,'x'=4,'zh'=4,'core'=2] {'zh','zl'}, dimensions={0} | all-to-all | bytes 131072 | tf_op jit(solution)/shard_map/all_to_all | solution.py:253
  121.5 0.1 shard_map.81
  121.6 15.3 %all_to_all.33.own_ref = bf16[16,176,128]{2,1,0:T(8,128)(2,1)S(1)} all-to-all(bf16[16,176,128]{2,1,0:T(8,128)(2,1)S(1)} %shard_map.81), channel_id=1, replica_groups=mesh['zl'=4,'yh'=2,'yl'=2,'x'=4,'zh'=4,'core'=2] {'yl','x','yh'}, dimensions={0} | all-to-all | bytes 1441792 | tf_op jit(solution)/shard_map/all_to_all | solution.py:253
  136.9 6.5 %collective-permute-start.1 = (bf16[16,176,128]{2,1,0:T(8,128)(2,1)S(1)}, bf16[16,176,128]{2,1,0:T(8,128)(2,1)S(1)}, u32[]{:S(2)}, u32[]{:S(2)}) collective-permute-start(bf16[16,176,128]{2,1,0:T(8,128)(2,1)S(1)} %all_to_all.33.own_ref), channel_id=1, source_target_pairs={{0,1},{1,0},{2,3},{3,2},{4,5},{5,4},{6,7},{7,6},{8,9},{9,8},{10,11... | collective-permute-start | bytes 2162696 | tf_op jit(solution)/shard_map/ppermute | solution.py:298
  143.4 1.8 %collective-permute-done.1.other_ref = bf16[16,176,128]{2,1,0:T(8,128)(2,1)S(1)} collective-permute-done((bf16[16,176,128]{2,1,0:T(8,128)(2,1)S(1)}, bf16[16,176,128]{2,1,0:T(8,128)(2,1)S(1)}, u32[]{:S(2)}, u32[]{:S(2)}) %collective-permute-start.1) | collective-permute-done | bytes 720928 | tf_op jit(solution)/shard_map/ppermute | solution.py:298
  145.2 2.1 %shard_map.82 = (bf16[9,36864]{1,0:T(8,128)(2,1)}, bf16[9,36864]{1,0:T(8,128)(2,1)}) custom-call(s32[1]{0:T(128)} %bitcast.1.core_ref, bf16[16,176,128]{2,1,0:T(8,128)(2,1)S(1)} %all_to_all.33.own_ref, bf16[16,176,128]{2,1,0:T(8,128)(2,1)S(1)} %collective-permute-done.1.other_ref), custom_call_target="tpu_custom_call" | custom-call | tf_op jit(solution)/shard_map/pallas_call | solution.py:28
Async XLA Ops:
  0.6 0.9 copy-start
  1.5 0.9 copy-start.1
  2.4 35.9 %copy-start.2 = (bf16[9,36864]{1,0:T(8,128)(2,1)S(1)}, bf16[9,36864]{1,0:T(8,128)(2,1)}, u32[]{:S(2)}) copy-start(bf16[9,36864]{1,0:T(8,128)(2,1)} %param.5) | copy-start | bytes 1990660
  31.6 7.9 %copy-start.3 = (bf16[9,36864]{1,0:T(8,128)(2,1)S(1)}, bf16[9,36864]{1,0:T(8,128)(2,1)}, u32[]{:S(2)}) copy-start(bf16[9,36864]{1,0:T(8,128)(2,1)} %param.6) | copy-start | bytes 1990660
  31.6 13.8 %all-to-all-start.1 = ((bf16[8,96,128]{2,1,0:T(8,128)(2,1)}), bf16[8,96,128]{2,1,0:T(8,128)(2,1)S(1)}, u32[]{:S(2)}, u32[]{:S(2)}) async-start(bf16[8,96,128]{2,1,0:T(8,128)(2,1)} %shard_map.76), calls=%async_computation.1 | async-start | bytes 393216 | tf_op jit(solution)/shard_map/all_to_all | solution.py:253
  48.8 10.0 %collective-permute-start = (bf16[16,176,128]{2,1,0:T(8,128)(2,1)S(1)}, bf16[16,176,128]{2,1,0:T(8,128)(2,1)S(1)}, u32[]{:S(2)}, u32[]{:S(2)}) collective-permute-start(bf16[16,176,128]{2,1,0:T(8,128)(2,1)S(1)} %get-tuple-element.14), channel_id=1, source_target_pairs={{0,1},{1,0},{2,3},{3,2},{4,5},{5,4},{6,7},{7,6},{8,9},{9,8},{10,11... | collective-permute-start | bytes 2162696 | tf_op jit(solution)/shard_map/ppermute | solution.py:280
  60.0 21.8 %all-to-all-start.2 = ((bf16[16,272,128]{2,1,0:T(8,128)(2,1)}), bf16[16,272,128]{2,1,0:T(8,128)(2,1)S(1)}, u32[]{:S(2)}, u32[]{:S(2)}) async-start(bf16[16,272,128]{2,1,0:T(8,128)(2,1)} %shard_map.78), calls=%async_computation.2 | async-start | bytes 2228224 | tf_op jit(solution)/shard_map/all_to_all | solution.py:253
  136.9 8.3 %collective-permute-start.1 = (bf16[16,176,128]{2,1,0:T(8,128)(2,1)S(1)}, bf16[16,176,128]{2,1,0:T(8,128)(2,1)S(1)}, u32[]{:S(2)}, u32[]{:S(2)}) collective-permute-start(bf16[16,176,128]{2,1,0:T(8,128)(2,1)S(1)} %all_to_all.33.own_ref), channel_id=1, source_target_pairs={{0,1},{1,0},{2,3},{3,2},{4,5},{5,4},{6,7},{7,6},{8,9},{9,8},{10,11... | collective-permute-start | bytes 2162696 | tf_op jit(solution)/shard_map/ppermute | solution.py:298

commit v3 on v1

--- a/solution.py
+++ b/solution.py
@@ -1,5 +1,3 @@
-import functools
-
 import jax
 import jax.numpy as jnp
 from jax import lax
@@ -11,7 +9,7 @@
 AXES = ("zl", "yh", "yl", "x", "zh", "core")
 SIZES = (4, 2, 2, 4, 4, 2)
 PEERS = ("x", "zh", "zl", "yh")
-PLANE = ("x", "yh", "yl")
+PLANE = ("core", "yl", "x", "yh")
 LINE = ("zh", "zl")
 BF16 = jnp.bfloat16
 F32 = jnp.float32
@@ -19,20 +17,17 @@
 PAD = 32
 
 
-def call(kernel, out_shape, scratch=(), mem=40, smem_first=False):
+def call(kernel, out_shape, scratch=(), space=pltpu.VMEM):
     out_specs = jax.tree.map(lambda _: pl.BlockSpec(memory_space=pltpu.VMEM), out_shape)
 
     def run(*args):
-        in_specs = [pl.BlockSpec(memory_space=pltpu.VMEM) for _ in args]
-        if smem_first:
-            in_specs[0] = pl.BlockSpec(memory_space=pltpu.SMEM)
         return pl.pallas_call(
             kernel,
             out_shape=out_shape,
-            in_specs=in_specs,
+            in_specs=[pl.BlockSpec(memory_space=space) for _ in args],
             out_specs=out_specs,
             scratch_shapes=list(scratch),
-            compiler_params=pltpu.CompilerParams(vmem_limit_bytes=mem * 1024 * 1024),
+            compiler_params=pltpu.CompilerParams(vmem_limit_bytes=40 * 1024 * 1024),
         )(*args)
 
     return run
@@ -44,21 +39,31 @@
     return value * normal_cdf, normal_cdf + value * density
 
 
-def pack_kernel(x_ref, g_ref, o_ref):
-    fields = [x_ref[...].astype(F32), g_ref[...].astype(F32)]
-    for pair in range(8):
-        blocks = []
-        for j in (2 * pair, 2 * pair + 1):
-            pieces = [f[k * 8 : k * 8 + 8, j * C : (j + 1) * C] for f in fields for k in (0, 1)]
-            blocks.append(jnp.concatenate(pieces, axis=1))
-        o_ref[pair * 16 : pair * 16 + 16, :] = jnp.concatenate(blocks, axis=0).astype(BF16)
-
-
-def main_kernel(core_ref, r_ref, w1_ref, w2_ref, o_ref, keep_ref, send_ref, tap_ref, ft_ref, wg_ref):
+def pack_kernel(x_hbm, g_hbm, o_ref, in_ref, row_ref, sems):
+    copies = [pltpu.make_async_copy(h, in_ref.at[n], sems.at[n]) for n, h in enumerate((x_hbm, g_hbm))]
+    for copy in copies:
+        copy.start()
+    row_ref[...] = jnp.zeros((1024, 128), F32)
+    for copy in copies:
+        copy.wait()
+    fields = [in_ref[n].astype(F32) for n in (0, 1)]
+    for j in range(16):
+        pieces = [f[k * 8 : k * 8 + 8, j * C : (j + 1) * C] for f in fields for k in (0, 1)]
+        wide = jnp.concatenate(pieces, axis=1)
+        for t in range(6):
+            row_ref[pl.ds(j * 64 + t, 8, stride=8), :] = wide[:, t * 128 : t * 128 + 128]
+    for j in range(16):
+        o_ref[j * 64 : j * 64 + 64, :] = row_ref[j * 64 : j * 64 + 64, :].astype(BF16)
+
+
+def main_kernel(r_ref, w1_ref, w2_ref, o_ref, g_ref, row_ref, tap_ref, ft_ref, wg_ref):
     cells = 256
 
+    row_ref[...] = r_ref[...].astype(F32)
+
     def unpack(f):
-        part = r_ref[:, f * 2 * C : (f + 1) * 2 * C].astype(F32)
+        tiles = [row_ref[pl.ds(3 * f + t, 128, stride=8), :] for t in range(3)]
+        part = jnp.concatenate(tiles, axis=1)
         both = [part[:, k * C : (k + 1) * C].reshape(16, 1, 8, C) for k in (0, 1)]
         return jnp.concatenate(both, axis=1).reshape(cells, C)
 
@@ -155,45 +160,47 @@
             wg_ref[index, c * ROWS + 162 : c * ROWS + 168, :] = jnp.zeros((6, 128), F32)
     weight_grad(0, act_two, 2, 2)
     weight_grad(1, act_one, 3, 1)
-    core = core_ref[0]
-    keep_ref[...] = wg_ref[core].astype(BF16)
-    send_ref[...] = wg_ref[1 - core].astype(BF16)
-
-
-def join_kernel(s_ref, o_ref, out_ref, sum_ref, row_ref):
+    for c in range(32):
+        g_ref[c] = wg_ref[c // 16, (c % 16) * ROWS : (c % 16 + 1) * ROWS, :].astype(BF16)
+
+
+def join_kernel(s_ref, f_ref, out_ref, sum_ref, row_ref):
     total = s_ref[0].astype(F32)
-    for c in range(1, 16):
+    for c in range(1, 32):
         total = total + s_ref[c].astype(F32)
     sum_ref[...] = total
-    row_ref[...] = jnp.zeros((2, 128, 128), F32)
+    value = f_ref[...].astype(F32)
+    for t in range(6):
+        row_ref[pl.ds(t, 128, stride=8), :] = value[:, t * 128 : t * 128 + 128]
+    for t in (6, 7):
+        row_ref[pl.ds(t, 128, stride=8), :] = jnp.zeros((128, 128), F32)
     for x in range(4):
         for yh in range(2):
             t = x * 2 + yh
-            base = x * 32 + yh
-            row_ref[0, pl.ds(base, 16, stride=2), :] = sum_ref[t * 18 : t * 18 + 16, :]
-            row_ref[1, pl.ds(base, 2, stride=2), :] = sum_ref[t * 18 + 16 : t * 18 + 18, :]
-            row_ref[1, pl.ds(base + 4, 3, stride=2), :] = sum_ref[144 + t * 3 : 147 + t * 3, :]
-    out_ref[:, 0:768] = o_ref[...]
-    for h in (0, 1):
-        out_ref[:, 768 + h * 128 : 896 + h * 128] = row_ref[h].astype(BF16)
-
-
-def split_kernel(r_ref, out_ref, ig_ref, z_ref):
-    value = r_ref[...].astype(F32)
+            base = (x * 32 + yh) * 8 + 6
+            row_ref[pl.ds(base, 16, stride=16), :] = sum_ref[t * 18 : t * 18 + 16, :]
+            row_ref[pl.ds(base + 1, 2, stride=16), :] = sum_ref[t * 18 + 16 : t * 18 + 18, :]
+            row_ref[pl.ds(base + 33, 3, stride=16), :] = sum_ref[144 + t * 3 : 147 + t * 3, :]
+    out_ref[...] = row_ref[...].astype(BF16)
+
+
+def split_kernel(r_ref, out_ref, ig_ref, z_ref, row_ref):
+    row_ref[...] = r_ref[...].astype(F32)
+    tiles = [row_ref[pl.ds(t, 128, stride=8), :] for t in range(8)]
     for f, ref in enumerate((out_ref, ig_ref)):
+        wide = jnp.concatenate(tiles[3 * f : 3 * f + 3], axis=1)
         halves = []
         for k in (0, 1):
-            lo = f * 2 * C + k * C
-            halves.append(
-                jnp.concatenate([value[j * 8 : j * 8 + 8, lo : lo + C] for j in range(16)], axis=1)
-            )
+            part = wide[:, k * C : (k + 1) * C]
+            halves.append(jnp.concatenate([part[j * 8 : j * 8 + 8] for j in range(16)], axis=1))
         ref[...] = jnp.concatenate(halves, axis=0).astype(BF16)
+    value = jnp.concatenate(tiles[6:8], axis=1)
     row = lax.broadcasted_iota(jnp.int32, (8, 256), 0)
     total = jnp.zeros((8, 256), F32)
     for x in range(4):
-        part = value[x * 32 : x * 32 + 8, 768:1024]
+        part = value[x * 32 : x * 32 + 8]
         for zh in range(1, 4):
-            part = part + value[x * 32 + zh * 8 : x * 32 + zh * 8 + 8, 768:1024]
+            part = part + value[x * 32 + zh * 8 : x * 32 + zh * 8 + 8]
         part = part + pltpu.roll(part, 4, 0)
         part = part + pltpu.roll(part, 2, 0)
         total = jnp.where(row // 2 == x, part, total)
@@ -207,24 +214,22 @@
     slots = [z_ref[z].astype(F32) for z in range(16)]
     rows = [s[0:8] for s in slots] + [s[8:16] for s in slots[:5]]
     mine = jnp.concatenate(rows, axis=0).astype(BF16)
-    for c in range(16):
+    for c in range(32):
         out_ref[c] = mine
 
 
-def final_kernel(core_ref, own_ref, other_ref, one_ref, two_ref, scr_ref):
-    core = core_ref[0]
-    for c in range(16):
-        scr_ref[core, c * ROWS : (c + 1) * ROWS, :] = own_ref[c].astype(F32)
-        scr_ref[1 - core, c * ROWS : (c + 1) * ROWS, :] = other_ref[c].astype(F32)
+def final_kernel(r_ref, one_ref, two_ref, scr_ref):
+    for c in range(32):
+        scr_ref[c * ROWS : (c + 1) * ROWS, :] = r_ref[c].astype(F32)
     for index, ref in enumerate((two_ref, one_ref)):
         for n in range(288):
             m, q = n // 3, n % 3
             u, c = m // 16, m % 16
-            c8, yl = c // 2, c % 2
             v = q * 6 + u
-            eight = scr_ref[index, pl.ds(yl * ROWS + v * 8 + c8, 8, stride=2 * ROWS), :]
-            last = ((v // 3) * 2 + yl) * ROWS + (18 + v % 3) * 8 + c8
-            nine = jnp.concatenate([eight, scr_ref[index, last : last + 1, :]], axis=0)
+            first = (index * 16 + (c // 8) * 8) * ROWS + c % 8
+            eight = scr_ref[pl.ds(first + v * 8, 8, stride=ROWS), :]
+            last = first + (v // 3) * ROWS + (18 + v % 3) * 8
+            nine = jnp.concatenate([eight, scr_ref[last : last + 1, :]], axis=0)
             ref[:, n * 128 : (n + 1) * 128] = nine.astype(BF16)
 
 
@@ -237,44 +242,44 @@
 
 
 def per_device(inputs, first_weight, second_weight, cotangent):
-    core = lax.axis_index("core").astype(jnp.int32).reshape(1)
-    swap = [(0, 1), (1, 0)]
+    rows = pltpu.VMEM((1024, 128), F32)
     kernel_one = first_weight.reshape(9 * C, C)
     kernel_two = second_weight.reshape(9 * C, C)
-    packed = call(pack_kernel, shape(128, 768))(inputs, cotangent)
-    received = exchange(packed, PEERS)
-    fields, keep, send = call(
+    packed = call(
+        pack_kernel,
+        shape(1024, 128),
+        scratch=(pltpu.VMEM((2, 16, 16 * C), BF16), rows, pltpu.SemaphoreType.DMA((2,))),
+        space=pl.ANY,
+    )(inputs, cotangent)
+    received = exchange(packed.reshape(128, 8, 128), PEERS).reshape(1024, 128)
+    fields, grads = call(
         main_kernel,
-        (shape(128, 768), shape(16 * ROWS, 128), shape(16 * ROWS, 128)),
+        (shape(128, 768), shape(32, ROWS, 128)),
         scratch=(
+            rows,
             pltpu.VMEM((4, 3, 256 + 2 * PAD, C), BF16),
             pltpu.VMEM((2, C, 128), F32),
             pltpu.VMEM((2, 16 * ROWS, 128), F32),
         ),
-        smem_first=True,
-    )(core, received, kernel_one, kernel_two)
-    other = lax.ppermute(send, "core", swap)
-    pair = (keep.astype(F32) + other.astype(F32)).astype(BF16).reshape(16, ROWS, 128)
-    plane = exchange(pair, PLANE)
-    joined = call(
-        join_kernel,
-        shape(128, 1024),
-        scratch=(pltpu.VMEM((ROWS, 128), F32), pltpu.VMEM((2, 128, 128), F32)),
-    )(plane, fields)
-    back = exchange(joined, PEERS)
+    )(received, kernel_one, kernel_two)
+    plane = exchange(grads, PLANE)
+    joined = call(join_kernel, shape(1024, 128), scratch=(pltpu.VMEM((ROWS, 128), F32), rows))(
+        plane, fields
+    )
+    back = exchange(joined.reshape(128, 8, 128), PEERS).reshape(1024, 128)
     output, input_grad, mine = call(
-        split_kernel, (shape(16, 16 * C), shape(16, 16 * C), shape(16, 16, 128))
+        split_kernel,
+        (shape(16, 16 * C), shape(16, 16 * C), shape(16, 16, 128)),
+        scratch=(rows,),
     )(back)
     line = exchange(mine, LINE)
-    spread = call(spread_kernel, shape(16, ROWS, 128))(line)
+    spread = call(spread_kernel, shape(32, ROWS, 128))(line)
     gathered = exchange(spread, PLANE)
-    partner = lax.ppermute(gathered, "core", swap)
     one, two = call(
         final_kernel,
         (shape(9, C * C), shape(9, C * C)),
-        scratch=(pltpu.VMEM((2, 16 * ROWS, 128), F32),),
-        smem_first=True,
-    )(core, gathered, partner)
+        scratch=(pltpu.VMEM((32 * ROWS, 128), F32),),
+    )(gathered)
     return output, input_grad, one, two
 
 

time: 143 us -> 155 us (1.084)
  blocking collectives: 71.8 us -> 99.2 us
  starting transfers between devices: 35.2 us -> 23.1 us
  waiting for transfers between devices: 20.9 us -> 18.5 us
  other arithmetic: 1.69 us -> 0 us
    all_to_all x4, blocking collectives: 71.8 us -> 99.2 us  [exchange(): return lax.all_to_all(value, axes, split_axis=0, concat_axis=0, tiled=True)]
    ppermute x2 -> x0, starting transfers between devices: 12.1 us -> none  [the longest x1 6.91 us: per_device(): partner = lax.ppermute(gathered, 'core', swap)]
    ppermute x2 -> x0, waiting for transfers between devices: 3.5 us -> none  [the longest x1 1.75 us: per_device(): other = lax.ppermute(send, 'core', swap)]
    unnamed x14 -> x6, local copies, waits for them, and re-layouts: 3.17 us -> 1.78 us
  transfers between devices with their start and end apart: 3 -> 1, of which waited for: 3 -> 1; matrix products, arithmetic and copies ran while one was open for 2% -> 2% of each run, Pallas kernels for 0% -> 0%
where the time goes in v3:
time: 155 us; the launch traced here: 154 us
  blocking collectives  99.2 us (64%)
  starting transfers between devices  23.1 us (15%)
  waiting for transfers between devices  18.5 us (12%)
  Pallas kernels  7.71 us (5%)
  local copies, waits for them, and re-layouts  5.06 us (3%)
    all_to_all x4, blocking collectives, exchange(): return lax.all_to_all(value, axes, split_axis=0, concat_axis=0, tiled=True)  99.2 us
    all_to_all x1, starting transfers between devices, exchange(): return lax.all_to_all(value, axes, split_axis=0, concat_axis=0, tiled=True)  23.1 us
    all_to_all x1, waiting for transfers between devices, exchange(): return lax.all_to_all(value, axes, split_axis=0, concat_axis=0, tiled=True)  18.5 us
    pallas_call x6, Pallas kernels, run(): pl.pallas_call(kernel, out_shape=out_shape, in_specs=[pl.BlockSpec(memory...  7.71 us
  transfers between devices with their start and end apart: 1, of which 1 were waited for; matrix products, arithmetic and copies ran while one was open for 2% of the time, Pallas kernels for 0%

profile of v3, /device:TPU:1, one launch (start us, length us, event | category | flops | bytes accessed | tf_op | source)
XLA Modules:
  0.0 154.3 jit_solution(7899041566357198858)
XLA Ops:
  0.6 0.0 copy-start
  0.6 0.9 copy-done
  1.5 0.0 copy-start.1
  1.5 0.9 copy-done.1
  2.4 1.1 shard_map.75
  3.5 0.0 copy-start.2
  3.6 23.1 %all-to-all-start = ((bf16[128,8,128]{2,1,0:T(8,128)(2,1)}), bf16[128,8,128]{2,1,0:T(8,128)(2,1)S(1)}, u32[]{:S(2)}, u32[]{:S(2)}) async-start(bf16[128,8,128]{2,1,0:T(8,128)(2,1)} %bitcast), calls=%async_computation | async-start | bytes 524288 | tf_op jit(solution)/shard_map/all_to_all | solution.py:237
  26.7 2.2 %reshape.28.w1_ref = bf16[1728,192]{1,0:T(8,128)(2,1)S(1)} reshape(bf16[9,36864]{1,0:T(8,128)(2,1)} %param.5) | data formatting | bytes 1327104 | tf_op jit(solution)/shard_map/reshape | solution.py:246
  28.8 0.0 copy-done.2
  28.9 1.1 reshape.29.w2_ref
  30.0 18.5 %all-to-all-done = bf16[128,8,128]{2,1,0:T(8,128)(2,1)S(1)} async-done(((bf16[128,8,128]{2,1,0:T(8,128)(2,1)}), bf16[128,8,128]{2,1,0:T(8,128)(2,1)S(1)}, u32[]{:S(2)}, u32[]{:S(2)}) %all-to-all-start) | async-done | bytes 262176 | tf_op jit(solution)/shard_map/all_to_all | solution.py:237
  48.5 2.9 %shard_map.76 = (bf16[128,768]{1,0:T(8,128)(2,1)S(1)}, bf16[32,168,128]{2,1,0:T(8,128)(2,1)S(1)}) custom-call(bf16[1024,128]{1,0:T(8,128)(2,1)S(1)} %bitcast.6, bf16[1728,192]{1,0:T(8,128)(2,1)S(1)} %reshape.28.w1_ref, bf16[1728,192]{1,0:T(8,128)(2,1)S(1)} %reshape.29.w2_ref), custom_call_target="tpu_custom_call" | custom-call | tf_op jit(solution)/shard_map/pallas_call | solution.py:24
  51.4 28.2 %all_to_all.25.s_ref = bf16[32,168,128]{2,1,0:T(8,128)(2,1)S(1)} all-to-all(bf16[32,168,128]{2,1,0:T(8,128)(2,1)S(1)} %get-tuple-element.11), channel_id=1, replica_groups=mesh['zl'=4,'yh'=2,'yl'=2,'x'=4,'zh'=4,'core'=2] {'core','yl','x','yh'}, dimensions={0} | all-to-all | bytes 2752512 | tf_op jit(solution)/shard_map/all_to_all | solution.py:237
  79.7 0.3 shard_map.77
  80.0 28.3 %all_to_all.26 = bf16[128,8,128]{2,1,0:T(8,128)(2,1)S(1)} all-to-all(bf16[128,8,128]{2,1,0:T(8,128)(2,1)S(1)} %bitcast.4), channel_id=1, replica_groups=mesh['zl'=4,'yh'=2,'yl'=2,'x'=4,'zh'=4,'core'=2] {'x','zh','zl','yh'}, dimensions={0} | all-to-all | bytes 524288 | tf_op jit(solution)/shard_map/all_to_all | solution.py:237
  108.3 0.8 shard_map.78
  109.1 15.8 %all_to_all.27.z_ref = bf16[16,16,128]{2,1,0:T(8,128)(2,1)S(1)} all-to-all(bf16[16,16,128]{2,1,0:T(8,128)(2,1)S(1)} %get-tuple-element.15), channel_id=1, replica_groups=mesh['zl'=4,'yh'=2,'yl'=2,'x'=4,'zh'=4,'core'=2] {'zh','zl'}, dimensions={0} | all-to-all | bytes 131072 | tf_op jit(solution)/shard_map/all_to_all | solution.py:237
  124.9 0.2 shard_map.79
  125.1 26.9 %all_to_all.28.r_ref = bf16[32,168,128]{2,1,0:T(8,128)(2,1)S(1)} all-to-all(bf16[32,168,128]{2,1,0:T(8,128)(2,1)S(1)} %shard_map.79), channel_id=1, replica_groups=mesh['zl'=4,'yh'=2,'yl'=2,'x'=4,'zh'=4,'core'=2] {'core','yl','x','yh'}, dimensions={0} | all-to-all | bytes 2752512 | tf_op jit(solution)/shard_map/all_to_all | solution.py:237
  151.9 2.4 %shard_map.80 = (bf16[9,36864]{1,0:T(8,128)(2,1)}, bf16[9,36864]{1,0:T(8,128)(2,1)}) custom-call(bf16[32,168,128]{2,1,0:T(8,128)(2,1)S(1)} %all_to_all.28.r_ref), custom_call_target="tpu_custom_call" | custom-call | tf_op jit(solution)/shard_map/pallas_call | solution.py:24
Async XLA Ops:
  0.6 0.9 copy-start
  1.5 0.9 copy-start.1
  3.5 25.3 %copy-start.2 = (bf16[9,36864]{1,0:T(8,128)(2,1)S(1)}, bf16[9,36864]{1,0:T(8,128)(2,1)}, u32[]{:S(2)}) copy-start(bf16[9,36864]{1,0:T(8,128)(2,1)} %param.6) | copy-start | bytes 1990660
  3.6 45.0 %all-to-all-start = ((bf16[128,8,128]{2,1,0:T(8,128)(2,1)}), bf16[128,8,128]{2,1,0:T(8,128)(2,1)S(1)}, u32[]{:S(2)}, u32[]{:S(2)}) async-start(bf16[128,8,128]{2,1,0:T(8,128)(2,1)} %bitcast), calls=%async_computation | async-start | bytes 524288 | tf_op jit(solution)/shard_map/all_to_all | solution.py:237

commit v4 on v2

--- a/solution.py
+++ b/solution.py
@@ -9,7 +9,7 @@
 AXES = ("zl", "yh", "yl", "x", "zh", "core")
 SIZES = (4, 2, 2, 4, 4, 2)
 LINE = ("zh", "zl")
-BLOCK = ("x", "yh")
+PEERS = ("zh", "zl", "x", "yh")
 PLANE = ("yl", "x", "yh")
 BF16 = jnp.bfloat16
 F32 = jnp.float32
@@ -18,20 +18,20 @@
 PAD = 32
 
 
-def call(kernel, out_shape, scratch=(), mem=40, smem_first=False):
-    out_specs = jax.tree.map(lambda _: pl.BlockSpec(memory_space=pltpu.VMEM), out_shape)
+def call(kernel, out_shape, scratch=(), spaces={}, out_specs=None, limit=40 * 1024 * 1024):
+    if out_specs is None:
+        out_specs = jax.tree.map(lambda _: pl.BlockSpec(memory_space=pltpu.VMEM), out_shape)
 
     def run(*args):
-        in_specs = [pl.BlockSpec(memory_space=pltpu.VMEM) for _ in args]
-        if smem_first:
-            in_specs[0] = pl.BlockSpec(memory_space=pltpu.SMEM)
         return pl.pallas_call(
             kernel,
             out_shape=out_shape,
-            in_specs=in_specs,
+            in_specs=[
+                pl.BlockSpec(memory_space=spaces.get(n, pltpu.VMEM)) for n in range(len(args))
+            ],
             out_specs=out_specs,
             scratch_shapes=list(scratch),
-            compiler_params=pltpu.CompilerParams(vmem_limit_bytes=mem * 1024 * 1024),
+            compiler_params=pltpu.CompilerParams(vmem_limit_bytes=limit),
         )(*args)
 
     return run
@@ -43,34 +43,41 @@
     return value * normal_cdf, normal_cdf + value * density
 
 
-def pack_kernel(x_ref, g_ref, o_ref):
-    fields = [x_ref[...].astype(F32), g_ref[...].astype(F32)]
+def pack_kernel(core_ref, half_ref, x_hbm, g_hbm, o_ref, where_ref, in_ref, row_ref, sems):
+    copies = [pltpu.make_async_copy(h, in_ref.at[n], sems.at[n]) for n, h in enumerate((x_hbm, g_hbm))]
+    for copy in copies:
+        copy.start()
+    where_ref[0] = core_ref[0]
+    where_ref[1] = half_ref[0]
+    row_ref[...] = jnp.zeros((1024, 128), F32)
+    for copy in copies:
+        copy.wait()
+    fields = [in_ref[n].astype(F32) for n in (0, 1)]
     for z in range(16):
         pieces = [f[k * 8 : k * 8 + 8, z * C : (z + 1) * C] for f in fields for k in (0, 1)]
         wide = jnp.concatenate(pieces, axis=1)
-        tiles = [wide[:, t * 128 : t * 128 + 128] for t in range(6)]
-        o_ref[z] = jnp.concatenate(tiles, axis=0).astype(BF16)
-
-
-def relay_kernel(r_ref, o_ref, scr_ref):
-    for z in range(16):
-        scr_ref[z * 48 : z * 48 + 48, :] = r_ref[z].astype(F32)
-    for e in range(8):
-        tiles = [scr_ref[pl.ds(t * 8 + e, 16, stride=48), :] for t in range(6)]
-        o_ref[e] = jnp.concatenate(tiles, axis=0).astype(BF16)
-
-
-def main_kernel(core_ref, r_ref, w1_ref, w2_ref, o_ref, keep_ref, send_ref, tap_ref, ft_ref, wg_ref):
+        for t in range(6):
+            row_ref[pl.ds(z * 64 + t, 8, stride=8), :] = wide[:, t * 128 : t * 128 + 128]
+    for z in range(16):
+        o_ref[z * 64 : z * 64 + 64, :] = row_ref[z * 64 : z * 64 + 64, :].astype(BF16)
+
+
+def main_kernel(
+    where_ref, r_ref, w1_ref, w2_ref, o_ref, keep_ref, send_ref, row_ref, tap_ref, ft_ref, wg_ref
+):
     cells = 256
+
+    row_ref[...] = r_ref[...].astype(F32)
 
     def unpack(f):
         tiles = []
         for t in range(3 * f, 3 * f + 3):
             pieces = []
             for x in range(4):
-                pair = [r_ref[x * 2 + yh, t * 16 : t * 16 + 16, :].astype(F32) for yh in (0, 1)]
                 for zh in range(4):
-                    pieces += [p[zh * 4 : zh * 4 + 4] for p in pair]
+                    for yh in (0, 1):
+                        first = (zh * 32 + x * 2 + yh) * 8 + t
+                        pieces.append(row_ref[pl.ds(first, 4, stride=64), :])
             tiles.append(jnp.concatenate(pieces, axis=0))
         part = jnp.concatenate(tiles, axis=1)
         both = [part[:, k * C : (k + 1) * C].reshape(16, 1, 8, C) for k in (0, 1)]
@@ -184,7 +191,7 @@
             wg_ref[index, c * ROWS + 162 : (c + 1) * ROWS, :] = jnp.zeros((ROWS - 162, 128), F32)
     weight_grad(0, act_two, 2, 2)
     weight_grad(1, act_one, 3, 1)
-    core = core_ref[0]
+    core = where_ref[0]
     for c in range(16):
         keep_ref[c] = wg_ref[core, c * ROWS : (c + 1) * ROWS, :].astype(BF16)
         send_ref[c] = wg_ref[1 - core, c * ROWS : (c + 1) * ROWS, :].astype(BF16)
@@ -197,8 +204,8 @@
         o_ref[c, FIELD : FIELD + ROWS, :] = pair.astype(BF16)
 
 
-def line_kernel(yl_ref, s_ref, o_ref, sum_ref, scr_ref):
-    yl = yl_ref[0]
+def line_kernel(where_ref, s_ref, o_ref, sum_ref, scr_ref):
+    yl = where_ref[1]
     total = s_ref[0, FIELD : FIELD + ROWS, :].astype(F32)
     for c in range(1, 16):
         total = total + s_ref[c, FIELD : FIELD + ROWS, :].astype(F32)
@@ -235,8 +242,8 @@
         out_ref[c] = mine
 
 
-def final_kernel(core_ref, own_ref, other_ref, one_ref, two_ref, scr_ref):
-    core = core_ref[0]
+def final_kernel(where_ref, own_ref, other_ref, one_ref, two_ref, scr_ref):
+    core = where_ref[0]
     for c in range(16):
         scr_ref[core, c * ROWS : (c + 1) * ROWS, :] = own_ref[c].astype(F32)
         scr_ref[1 - core, c * ROWS : (c + 1) * ROWS, :] = other_ref[c].astype(F32)
@@ -258,50 +265,56 @@
 
 
 def per_device(inputs, first_weight, second_weight, cotangent):
+    smem, hbm, vmem = pltpu.SMEM, pltpu.HBM, pltpu.VMEM
     core = lax.axis_index("core").astype(jnp.int32).reshape(1)
     half = lax.axis_index("yl").astype(jnp.int32).reshape(1)
     swap = [(0, 1), (1, 0)]
+    rows = vmem((1024, 128), F32)
     kernel_one = first_weight.reshape(9 * C, C)
     kernel_two = second_weight.reshape(9 * C, C)
-    packed = call(pack_kernel, shape(16, 48, 128))(inputs, cotangent)
-    line_in = exchange(packed, LINE)
-    relayed = call(relay_kernel, shape(8, FIELD, 128), scratch=(pltpu.VMEM((768, 128), F32),))(line_in)
-    received = exchange(relayed, BLOCK)
+    packed, where = call(
+        pack_kernel,
+        (shape(1024, 128), shape(2, dtype=jnp.int32)),
+        scratch=(vmem((2, 16, 16 * C), BF16), rows, pltpu.SemaphoreType.DMA((2,))),
+        spaces={0: smem, 1: smem, 2: hbm, 3: hbm},
+        out_specs=(pl.BlockSpec(memory_space=vmem), pl.BlockSpec(memory_space=smem)),
+        limit=63400000,
+    )(core, half, inputs, cotangent)
+    received = exchange(packed.reshape(128, 8, 128), PEERS).reshape(1024, 128)
     fields, keep, send = call(
         main_kernel,
         (shape(8, FIELD, 128), shape(16, ROWS, 128), shape(16, ROWS, 128)),
         scratch=(
-            pltpu.VMEM((4, 3, 256 + 2 * PAD, C), BF16),
-            pltpu.VMEM((2, C, 128), F32),
-            pltpu.VMEM((2, 16 * ROWS, 128), F32),
+            rows,
+            vmem((4, 3, 256 + 2 * PAD, C), BF16),
+            vmem((2, C, 128), F32),
+            vmem((2, 16 * ROWS, 128), F32),
         ),
-        smem_first=True,
-    )(core, received, kernel_one, kernel_two)
+        spaces={0: smem},
+    )(where, received, kernel_one, kernel_two)
     other = lax.ppermute(send, "core", swap)
     joined = call(join_kernel, shape(16, FIELD + ROWS, 128))(fields, keep, other)
     plane = exchange(joined, PLANE)
     to_line = call(
         line_kernel,
         shape(16, 64, 128),
-        scratch=(pltpu.VMEM((ROWS + 8, 128), F32), pltpu.VMEM((8 * FIELD, 128), F32)),
-        smem_first=True,
-    )(half, plane)
+        scratch=(vmem((ROWS + 8, 128), F32), vmem((8 * FIELD, 128), F32)),
+        spaces={0: smem},
+    )(where, plane)
     back = exchange(to_line, LINE)
     output, input_grad, mine = call(
         split_kernel, (shape(16, 16 * C), shape(16, 16 * C), shape(16, 16, 128))
     )(back)
     line = exchange(mine, LINE)
-    spread = call(
-        spread_kernel, shape(16, ROWS, 128), scratch=(pltpu.VMEM((ROWS + 8, 128), F32),)
-    )(line)
+    spread = call(spread_kernel, shape(16, ROWS, 128), scratch=(vmem((ROWS + 8, 128), F32),))(line)
     gathered = exchange(spread, PLANE)
     partner = lax.ppermute(gathered, "core", swap)
     one, two = call(
         final_kernel,
         (shape(9, C * C), shape(9, C * C)),
-        scratch=(pltpu.VMEM((2, 16 * ROWS, 128), F32),),
-        smem_first=True,
-    )(core, gathered, partner)
+        scratch=(vmem((2, 16 * ROWS, 128), F32),),
+        spaces={0: smem},
+    )(where, gathered, partner)
     return output, input_grad, one, two
 
 

time: 148 us -> 144 us (0.973)
  starting transfers between devices: 25.1 us -> 34.5 us
  waiting for transfers between devices: 26.5 us -> 18.2 us
  blocking collectives: 82.1 us -> 76 us
  Pallas kernels: 8.86 us -> 10.5 us
    all_to_all x2 -> x1, starting transfers between devices: 10.5 us -> 23.1 us  [exchange(): return lax.all_to_all(value, axes, split_axis=0, concat_axis=0, tiled=True)]
    all_to_all x2 -> x1, waiting for transfers between devices: 22.9 us -> 14.6 us  [exchange(): return lax.all_to_all(value, axes, split_axis=0, concat_axis=0, tiled=True)]
    all_to_all x4, blocking collectives: 82.1 us -> 76 us  [exchange(): return lax.all_to_all(value, axes, split_axis=0, concat_axis=0, tiled=True)]
    ppermute x1, starting transfers between devices: 8.17 us -> 6.09 us  [per_device(): other = lax.ppermute(send, 'core', swap)]
    unnamed x8 -> x4, local copies, waits for them, and re-layouts: 1.79 us -> 0.01 us
    pallas_call x8 -> x7, Pallas kernels: 8.86 us -> 10.5 us  [run(): pl.pallas_call(kernel, out_shape=out_shape, in_specs=[pl.BlockSpec(memory...]
  transfers between devices with their start and end apart: 4 -> 3, of which waited for: 4 -> 3; matrix products, arithmetic and copies ran while one was open for 2% -> 2% of each run, Pallas kernels for 0% -> 0%
where the time goes in v4:
time: 144 us; the launch traced here: 143 us
  blocking collectives  76 us (53%)
  starting transfers between devices  34.5 us (24%)
  waiting for transfers between devices  18.2 us (13%)
  Pallas kernels  10.5 us (7%)
  local copies, waits for them, and re-layouts  3.29 us (2%)
    all_to_all x4, blocking collectives, exchange(): return lax.all_to_all(value, axes, split_axis=0, concat_axis=0, tiled=True)  76 us
    all_to_all x1, starting transfers between devices, exchange(): return lax.all_to_all(value, axes, split_axis=0, concat_axis=0, tiled=True)  23.1 us
    all_to_all x1, waiting for transfers between devices, exchange(): return lax.all_to_all(value, axes, split_axis=0, concat_axis=0, tiled=True)  14.6 us
    pallas_call x7, Pallas kernels, run(): pl.pallas_call(kernel, out_shape=out_shape, in_specs=[pl.BlockSpec(memory...  10.5 us
    ppermute x1, starting transfers between devices, per_device(): other = lax.ppermute(send, 'core', swap)  6.09 us
    ppermute x1, starting transfers between devices, per_device(): partner = lax.ppermute(gathered, 'core', swap)  5.34 us
  transfers between devices with their start and end apart: 3, of which 3 were waited for; matrix products, arithmetic and copies ran while one was open for 2% of the time, Pallas kernels for 0%

profile of v4, /device:TPU:1, one launch (start us, length us, event | category | flops | bytes accessed | tf_op | source)
XLA Modules:
  0.0 143.3 jit_solution(677018241005654253)
XLA Ops:
  0.6 1.8 %shard_map.75 = (bf16[1024,128]{1,0:T(8,128)(2,1)}, s32[2]{0:T(128)}) custom-call(s32[1]{0:T(128)} %bitcast.core_ref, s32[1]{0:T(128)} %bitcast.1.half_ref, bf16[16,3072]{1,0:T(8,128)(2,1)} %x_hbm.1, bf16[16,3072]{1,0:T(8,128)(2,1)} %g_hbm.1), custom_call_target="tpu_custom_call" | custom-call | tf_op jit(solution)/shard_map/pallas_call | solution.py:26
  2.5 0.0 copy-start.1
  2.5 23.1 %all-to-all-start = ((bf16[128,8,128]{2,1,0:T(8,128)(2,1)}), bf16[128,8,128]{2,1,0:T(8,128)(2,1)S(1)}, u32[]{:S(2)}, u32[]{:S(2)}) async-start(bf16[128,8,128]{2,1,0:T(8,128)(2,1)} %bitcast.5), calls=%async_computation | async-start | bytes 524288 | tf_op jit(solution)/shard_map/all_to_all | solution.py:260
  25.6 2.2 %reshape.30.w1_ref = bf16[1728,192]{1,0:T(8,128)(2,1)S(1)} reshape(bf16[9,36864]{1,0:T(8,128)(2,1)} %param.5) | data formatting | bytes 1327104 | tf_op jit(solution)/shard_map/reshape | solution.py:273
  27.7 0.0 copy-done.1
  27.8 0.0 copy-start
  27.8 1.1 reshape.31.w2_ref
  28.9 14.6 %all-to-all-done = bf16[128,8,128]{2,1,0:T(8,128)(2,1)S(1)} async-done(((bf16[128,8,128]{2,1,0:T(8,128)(2,1)}), bf16[128,8,128]{2,1,0:T(8,128)(2,1)S(1)}, u32[]{:S(2)}, u32[]{:S(2)}) %all-to-all-start) | async-done | bytes 262176 | tf_op jit(solution)/shard_map/all_to_all | solution.py:260
  43.5 0.0 copy-done
  43.5 4.2 %shard_map.76 = (bf16[8,96,128]{2,1,0:T(8,128)(2,1)S(1)}, bf16[16,176,128]{2,1,0:T(8,128)(2,1)S(1)}, bf16[16,176,128]{2,1,0:T(8,128)(2,1)S(1)}) custom-call(s32[2]{0:T(128)S(1)} %copy-done, bf16[1024,128]{1,0:T(8,128)(2,1)S(1)} %bitcast.4, bf16[1728,192]{1,0:T(8,128)(2,1)S(1)} %reshape.30.w1_ref, bf16[1728,192]{1,0:T(8,128)(2,1)S(1)} %reshape.31.w2_ref), custom_call_target="tpu_custom_call" | custom-call | tf_op jit(solution)/shard_map/pallas_call | solution.py:26
  47.7 6.1 %collective-permute-start = (bf16[16,176,128]{2,1,0:T(8,128)(2,1)S(1)}, bf16[16,176,128]{2,1,0:T(8,128)(2,1)S(1)}, u32[]{:S(2)}, u32[]{:S(2)}) collective-permute-start(bf16[16,176,128]{2,1,0:T(8,128)(2,1)S(1)} %get-tuple-element.18), channel_id=1, source_target_pairs={{0,1},{1,0},{2,3},{3,2},{4,5},{5,4},{6,7},{7,6},{8,9},{9,8},{10,11... | collective-permute-start | bytes 2162696 | tf_op jit(solution)/shard_map/ppermute | solution.py:295
  53.8 1.8 %collective-permute-done.other_ref = bf16[16,176,128]{2,1,0:T(8,128)(2,1)S(1)} collective-permute-done((bf16[16,176,128]{2,1,0:T(8,128)(2,1)S(1)}, bf16[16,176,128]{2,1,0:T(8,128)(2,1)S(1)}, u32[]{:S(2)}, u32[]{:S(2)}) %collective-permute-start) | collective-permute-done | bytes 720928 | tf_op jit(solution)/shard_map/ppermute | solution.py:295
  55.5 0.2 shard_map.77
  55.7 23.7 %all_to_all.25.s_ref = bf16[16,272,128]{2,1,0:T(8,128)(2,1)S(1)} all-to-all(bf16[16,272,128]{2,1,0:T(8,128)(2,1)S(1)} %shard_map.77), channel_id=1, replica_groups=mesh['zl'=4,'yh'=2,'yl'=2,'x'=4,'zh'=4,'core'=2] {'yl','x','yh'}, dimensions={0} | all-to-all | bytes 2228224 | tf_op jit(solution)/shard_map/all_to_all | solution.py:260
  79.4 0.9 shard_map.78
  80.3 15.4 %all_to_all.26.r_ref = bf16[16,64,128]{2,1,0:T(8,128)(2,1)S(1)} all-to-all(bf16[16,64,128]{2,1,0:T(8,128)(2,1)S(1)} %shard_map.78), channel_id=1, replica_groups=mesh['zl'=4,'yh'=2,'yl'=2,'x'=4,'zh'=4,'core'=2] {'zh','zl'}, dimensions={0} | all-to-all | bytes 524288 | tf_op jit(solution)/shard_map/all_to_all | solution.py:260
  95.7 0.9 shard_map.79
  96.5 22.3 %all_to_all.27.z_ref = bf16[16,16,128]{2,1,0:T(8,128)(2,1)S(1)} all-to-all(bf16[16,16,128]{2,1,0:T(8,128)(2,1)S(1)} %get-tuple-element.21), channel_id=1, replica_groups=mesh['zl'=4,'yh'=2,'yl'=2,'x'=4,'zh'=4,'core'=2] {'zh','zl'}, dimensions={0} | all-to-all | bytes 131072 | tf_op jit(solution)/shard_map/all_to_all | solution.py:260
  118.8 0.1 shard_map.80
  118.9 14.7 %all_to_all.28.own_ref = bf16[16,176,128]{2,1,0:T(8,128)(2,1)S(1)} all-to-all(bf16[16,176,128]{2,1,0:T(8,128)(2,1)S(1)} %shard_map.80), channel_id=1, replica_groups=mesh['zl'=4,'yh'=2,'yl'=2,'x'=4,'zh'=4,'core'=2] {'yl','x','yh'}, dimensions={0} | all-to-all | bytes 1441792 | tf_op jit(solution)/shard_map/all_to_all | solution.py:260
  133.5 5.3 %collective-permute-start.1 = (bf16[16,176,128]{2,1,0:T(8,128)(2,1)S(1)}, bf16[16,176,128]{2,1,0:T(8,128)(2,1)S(1)}, u32[]{:S(2)}, u32[]{:S(2)}) collective-permute-start(bf16[16,176,128]{2,1,0:T(8,128)(2,1)S(1)} %all_to_all.28.own_ref), channel_id=1, source_target_pairs={{0,1},{1,0},{2,3},{3,2},{4,5},{5,4},{6,7},{7,6},{8,9},{9,8},{10,11... | collective-permute-start | bytes 2162696 | tf_op jit(solution)/shard_map/ppermute | solution.py:311
  138.9 1.8 %collective-permute-done.1.other_ref = bf16[16,176,128]{2,1,0:T(8,128)(2,1)S(1)} collective-permute-done((bf16[16,176,128]{2,1,0:T(8,128)(2,1)S(1)}, bf16[16,176,128]{2,1,0:T(8,128)(2,1)S(1)}, u32[]{:S(2)}, u32[]{:S(2)}) %collective-permute-start.1) | collective-permute-done | bytes 720928 | tf_op jit(solution)/shard_map/ppermute | solution.py:311
  140.7 2.6 %shard_map.81 = (bf16[9,36864]{1,0:T(8,128)(2,1)}, bf16[9,36864]{1,0:T(8,128)(2,1)}) custom-call(s32[2]{0:T(128)S(1)} %copy-done, bf16[16,176,128]{2,1,0:T(8,128)(2,1)S(1)} %all_to_all.28.own_ref, bf16[16,176,128]{2,1,0:T(8,128)(2,1)S(1)} %collective-permute-done.1.other_ref), custom_call_target="tpu_custom_call" | custom-call | tf_op jit(solution)/shard_map/pallas_call | solution.py:26
Async XLA Ops:
  2.5 25.3 %copy-start.1 = (bf16[9,36864]{1,0:T(8,128)(2,1)S(1)}, bf16[9,36864]{1,0:T(8,128)(2,1)}, u32[]{:S(2)}) copy-start(bf16[9,36864]{1,0:T(8,128)(2,1)} %param.6) | copy-start | bytes 1990660
  2.5 41.0 %all-to-all-start = ((bf16[128,8,128]{2,1,0:T(8,128)(2,1)}), bf16[128,8,128]{2,1,0:T(8,128)(2,1)S(1)}, u32[]{:S(2)}, u32[]{:S(2)}) async-start(bf16[128,8,128]{2,1,0:T(8,128)(2,1)} %bitcast.5), calls=%async_computation | async-start | bytes 524288 | tf_op jit(solution)/shard_map/all_to_all | solution.py:260
  27.8 15.7 %copy-start = (s32[2]{0:T(128)S(1)}, s32[2]{0:T(128)}, u32[]{:S(2)}) copy-start(s32[2]{0:T(128)} %get-tuple-element.14.where_ref) | copy-start | bytes 28
  47.7 7.9 %collective-permute-start = (bf16[16,176,128]{2,1,0:T(8,128)(2,1)S(1)}, bf16[16,176,128]{2,1,0:T(8,128)(2,1)S(1)}, u32[]{:S(2)}, u32[]{:S(2)}) collective-permute-start(bf16[16,176,128]{2,1,0:T(8,128)(2,1)S(1)} %get-tuple-element.18), channel_id=1, source_target_pairs={{0,1},{1,0},{2,3},{3,2},{4,5},{5,4},{6,7},{7,6},{8,9},{9,8},{10,11... | collective-permute-start | bytes 2162696 | tf_op jit(solution)/shard_map/ppermute | solution.py:295
  133.5 7.1 %collective-permute-start.1 = (bf16[16,176,128]{2,1,0:T(8,128)(2,1)S(1)}, bf16[16,176,128]{2,1,0:T(8,128)(2,1)S(1)}, u32[]{:S(2)}, u32[]{:S(2)}) collective-permute-start(bf16[16,176,128]{2,1,0:T(8,128)(2,1)S(1)} %all_to_all.28.own_ref), channel_id=1, source_target_pairs={{0,1},{1,0},{2,3},{3,2},{4,5},{5,4},{6,7},{7,6},{8,9},{9,8},{10,11... | collective-permute-start | bytes 2162696 | tf_op jit(solution)/shard_map/ppermute | solution.py:311

commit v5 on v3

v5 whole, which is shorter than its diff:
```python
import jax
import jax.numpy as jnp
from jax import lax
from jax.experimental import pallas as pl
from jax.experimental.pallas import tpu as pltpu
from jax.sharding import Mesh, PartitionSpec as P

C = 192
AXES = ("zl", "yh", "yl", "x", "zh", "core")
SIZES = (4, 2, 2, 4, 4, 2)
PEERS = ("x", "zh", "zl", "yh")
PLANE = ("yl", "x", "yh")
BF16 = jnp.bfloat16
F32 = jnp.float32
ROWS = 168
PITCH = 169
PAD = 32
CELLS = 256
OFFSETS = [(a, b) for a in (-1, 0, 1) for b in (-1, 0, 1)]


def call(kernel, out_shape, scratch=(), spaces={}, out_specs=None, limit=40 * 1024 * 1024):
    if out_specs is None:
        out_specs = jax.tree.map(lambda _: pl.BlockSpec(memory_space=pltpu.VMEM), out_shape)

    def run(*args):
        return pl.pallas_call(
            kernel,
            out_shape=out_shape,
            in_specs=[
                pl.BlockSpec(memory_space=spaces.get(n, pltpu.VMEM)) for n in range(len(args))
            ],
            out_specs=out_specs,
            scratch_shapes=list(scratch),
            compiler_params=pltpu.CompilerParams(vmem_limit_bytes=limit),
        )(*args)

    return run


def gelu_parts(value):
    normal_cdf = 0.5 * (1.0 + lax.erf(value * 0.7071067811865476))
    density = jnp.exp(-0.5 * value * value) * 0.3989422804014327
    return value * normal_cdf, normal_cdf + value * density


def pack_kernel(core_ref, x_hbm, g_hbm, o_ref, where_ref, in_ref, row_ref, sems):
    copies = [pltpu.make_async_copy(h, in_ref.at[n], sems.at[n]) for n, h in enumerate((x_hbm, g_hbm))]
    for copy in copies:
        copy.start()
    where_ref[0] = core_ref[0]
    for copy in copies:
        copy.wait()
    fields = [in_ref[n].astype(F32) for n in (0, 1)]
    for j in range(16):
        pieces = [f[k * 8 : k * 8 + 8, j * C : (j + 1) * C] for f in fields for k in (0, 1)]
        wide = jnp.concatenate(pieces, axis=1)
        for t in range(6):
            row_ref[pl.ds(j * 48 + t, 8, stride=6), :] = wide[:, t * 128 : t * 128 + 128]
    for j in range(16):
        o_ref[j * 48 : j * 48 + 48, :] = row_ref[j * 48 : j * 48 + 48, :].astype(BF16)


def put_taps(tap_ref, slot, field, step):
    within = lax.broadcasted_iota(jnp.int32, (CELLS, C), 0) % 8
    for a in (-1, 0, 1):
        moved = field
        if a != 0:
            rolled = pltpu.roll(field, (-a * step) % CELLS, 0)
            seen = (within + a * step >= 0) & (within + a * step < 8)
            moved = jnp.where(seen, rolled, 0.0)
        tap_ref[slot, a + 1, PAD : PAD + CELLS, :] = moved.astype(BF16)
    for a in range(3):
        tap_ref[slot, a, 0:PAD, :] = jnp.zeros((PAD, C), BF16)
        tap_ref[slot, a, PAD + CELLS : 2 * PAD + CELLS, :] = jnp.zeros((PAD, C), BF16)


def get_tap(tap_ref, slot, a, b, step):
    start = PAD + 16 * b * step
    return tap_ref[slot, a + 1, start : start + CELLS, :]


def main_kernel(where_ref, r_ref, w1_ref, w2_ref, o_ref, keep_ref, send_ref, row_ref, tap_ref, pair_ref):
    row_ref[...] = r_ref[...].astype(F32)

    def unpack(f):
        tiles = [row_ref[pl.ds(3 * f + t, 128, stride=6), :] for t in range(3)]
        part = jnp.concatenate(tiles, axis=1)
        both = [part[:, k * C : (k + 1) * C].reshape(16, 1, 8, C) for k in (0, 1)]
        return jnp.concatenate(both, axis=1).reshape(CELLS, C)

    def pack(value):
        split = value.reshape(16, 2, 8, C)
        return jnp.concatenate([split[:, k].reshape(128, C) for k in (0, 1)], axis=1)

    def forward(slot, w_ref, step):
        total = None
        for t, (a, b) in enumerate(OFFSETS):
            term = jnp.dot(
                get_tap(tap_ref, slot, a, b, step), w_ref[t * C : (t + 1) * C, :], preferred_element_type=F32
            )
            total = term if total is None else total + term
        return total

    def backward(slot, w_ref, step):
        total = None
        for t, (a, b) in enumerate(OFFSETS):
            term = lax.dot_general(
                get_tap(tap_ref, slot, -a, -b, step),
                w_ref[t * C : (t + 1) * C, :],
                (((1,), (1,)), ((), ())),
                preferred_element_type=F32,
            )
            total = term if total is None else total + term
        return total

    x = unpack(0)
    g = unpack(1)
    gelu_one, slope_one = gelu_parts(x)
    act_one = gelu_one.astype(BF16).astype(F32)
    put_taps(tap_ref, 0, act_one, 1)
    put_taps(tap_ref, 2, g, 2)
    hidden = (x + forward(0, w1_ref, 1)).astype(BF16).astype(F32)
    gelu_two, slope_two = gelu_parts(hidden)
    act_two = gelu_two.astype(BF16).astype(F32)
    put_taps(tap_ref, 1, act_two, 2)
    hidden_grad = (g + backward(2, w2_ref, 2) * slope_two).astype(BF16).astype(F32)
    put_taps(tap_ref, 3, hidden_grad, 1)
    output = hidden + forward(1, w2_ref, 2)
    input_grad = hidden_grad + backward(3, w1_ref, 1) * slope_one
    o_ref[...] = jnp.concatenate([pack(output), pack(input_grad)], axis=1).astype(BF16)
    for index, (act, grad) in enumerate(((act_two, g), (act_one, hidden_grad))):
        pair_ref[index, 0] = act[:, 0:128].astype(BF16)
        pair_ref[index, 1] = jnp.concatenate([act[:, 128:C], grad[:, 128:C]], axis=1).astype(BF16)
        pair_ref[index, 2] = grad[:, 0:128].astype(BF16)
    core = where_ref[0]
    keep_ref[...] = pair_ref[core]
    send_ref[...] = pair_ref[1 - core]


def weight_kernel(where_ref, own_ref, other_ref, o_ref, tap_ref, ft_ref, wg_ref):
    turned = []
    grads = []
    for ref in (own_ref, other_ref):
        first, mixed, last = [ref[n].astype(F32) for n in range(3)]
        turned.append(jnp.concatenate([first, mixed[:, 0:64]], axis=1).T)
        grads.append(jnp.concatenate([last, mixed[:, 64:128]], axis=1))
    for n in range(4):
        ft_ref[n] = turned[n // 2][:, (n % 2) * 128 : (n % 2) * 128 + 128]
    left = [
        jnp.concatenate(
            [
                jnp.concatenate(
                    [ft_ref[n, pl.ds(odd, 96, stride=2), :] for n in (2 * half, 2 * half + 1)], axis=1
                )
                for odd in (0, 1)
            ],
            axis=0,
        ).astype(BF16)
        for half in (0, 1)
    ]
    for c in range(16):
        wg_ref[c * ROWS + 162 : c * ROWS + 168, :] = jnp.zeros((6, 128), F32)

    def weight_grad(step):
        for half in (0, 1):
            put_taps(tap_ref, half, grads[half], step)
        for t, (a, b) in enumerate(OFFSETS):
            full = jnp.dot(left[0], get_tap(tap_ref, 0, -a, -b, step), preferred_element_type=F32)
            full = full + jnp.dot(
                left[1], get_tap(tap_ref, 1, -a, -b, step), preferred_element_type=F32
            )
            even, odd = full[0:96], full[96:192]
            lanes = (
                even[:, 0:128],
                jnp.concatenate([even[:, 128:192], odd[:, 0:64]], axis=1),
                odd[:, 64:192],
            )
            for q in range(3):
                for u in range(6):
                    wg_ref[pl.ds(t * 18 + q * 6 + u, 16, stride=ROWS), :] = lanes[q][
                        u * 16 : u * 16 + 16
                    ]

    for core, step in ((0, 2), (1, 1)):
        pl.when(where_ref[0] == core)(lambda step=step: weight_grad(step))
    for c in range(16):
        o_ref[c] = wg_ref[c * ROWS : (c + 1) * ROWS, :].astype(BF16)


def join_kernel(s_ref, f_ref, out_ref, sum_ref, row_ref):
    total = s_ref[0].astype(F32)
    for c in range(1, 16):
        total = total + s_ref[c].astype(F32)
    sum_ref[0:ROWS, :] = total
    sum_ref[ROWS : ROWS + 8, :] = jnp.zeros((8, 128), F32)
    value = f_ref[...].astype(F32)
    for t in range(6):
        row_ref[pl.ds(t, 128, stride=12), :] = value[:, t * 128 : t * 128 + 128]
    for x in range(4):
        for yh in range(2):
            t = x * 2 + yh
            for zl in range(4):
                first = t * 18 + zl * 6 if zl < 3 else 144 + t * 3
                piece = sum_ref[first : first + 6, :]
                for zh in range(4):
                    start = (x * 32 + zh * 8 + zl * 2 + yh) * 12 + 6
                    row_ref[start : start + 6, :] = piece
    out_ref[...] = row_ref[...].astype(BF16)


def split_kernel(r_ref, out_ref, ig_ref, z_ref, row_ref):
    row_ref[...] = r_ref[...].astype(F32)
    tiles = [row_ref[pl.ds(t, 128, stride=12), :] for t in range(12)]
    for f, ref in enumerate((out_ref, ig_ref)):
        wide = jnp.concatenate(tiles[3 * f : 3 * f + 3], axis=1)
        halves = []
        for k in (0, 1):
            part = wide[:, k * C : (k + 1) * C]
            halves.append(jnp.concatenate([part[j * 8 : j * 8 + 8] for j in range(16)], axis=1))
        ref[...] = jnp.concatenate(halves, axis=0).astype(BF16)
    row = lax.broadcasted_iota(jnp.int32, (8, 128), 0)
    slots = []
    for value in tiles[6:12]:
        total = jnp.zeros((8, 128), F32)
        for x in range(4):
            part = value[x * 32 : x * 32 + 8]
            for zh in range(1, 4):
                part = part + value[x * 32 + zh * 8 : x * 32 + zh * 8 + 8]
            part = part + pltpu.roll(part, 4, 0)
            part = part + pltpu.roll(part, 2, 0)
            total = jnp.where(row // 2 == x, part, total)
        slots.append(total * (1.0 / 256.0))
    mine = jnp.concatenate(slots, axis=0).astype(BF16)
    for z in range(4):
        z_ref[z] = mine


def spread_kernel(z_ref, out_ref):
    mine = jnp.concatenate([z_ref[0], z_ref[1], z_ref[2], z_ref[3, 0:32, :]], axis=0)
    for c in range(16):
        out_ref[c, 0:160, :] = mine[0:160]
        out_ref[c, 160:168, :] = z_ref[3, 16:32, :][0:8]


def final_kernel(where_ref, own_ref, other_ref, one_ref, two_ref, scr_ref):
    core = where_ref[0]
    for c in range(16):
        scr_ref[core, c * PITCH : c * PITCH + ROWS, :] = own_ref[c].astype(F32)
        scr_ref[1 - core, c * PITCH : c * PITCH + ROWS, :] = other_ref[c].astype(F32)
    for index, ref in enumerate((two_ref, one_ref)):
        for n in range(288):
            m, q = n // 3, n % 3
            u, c = m // 16, m % 16
            v = q * 6 + u
            first = (c // 8) * 8 * PITCH + c % 8
            eight = scr_ref[index, pl.ds(first + v * 8, 8, stride=PITCH), :]
            last = first + (v // 3) * PITCH + (18 + v % 3) * 8
            nine = jnp.concatenate([eight, scr_ref[index, last : last + 1, :]], axis=0)
            ref[:, n * 128 : (n + 1) * 128] = nine.astype(BF16)


def exchange(value, axes):
    return lax.all_to_all(value, axes, split_axis=0, concat_axis=0, tiled=True)


def shape(*dims, dtype=BF16):
    return jax.ShapeDtypeStruct(dims, dtype)


def per_device(inputs, first_weight, second_weight, cotangent):
    smem, hbm, vmem = pltpu.SMEM, pltpu.HBM, pltpu.VMEM
    core = lax.axis_index("core").astype(jnp.int32).reshape(1)
    swap = [(0, 1), (1, 0)]
    kernel_one = first_weight.reshape(9 * C, C)
    kernel_two = second_weight.reshape(9 * C, C)
    packed, where = call(
        pack_kernel,
        (shape(768, 128), shape(1, dtype=jnp.int32)),
        scratch=(
            vmem((2, 16, 16 * C), BF16),
            vmem((768, 128), F32),
            pltpu.SemaphoreType.DMA((2,)),
        ),
        spaces={0: smem, 1: hbm, 2: hbm},
        out_specs=(pl.BlockSpec(memory_space=vmem), pl.BlockSpec(memory_space=smem)),
        limit=63400000,
    )(core, inputs, cotangent)
    received = exchange(packed.reshape(384, 2, 128), PEERS).reshape(768, 128)
    fields, keep, send = call(
        main_kernel,
        (shape(128, 768), shape(3, CELLS, 128), shape(3, CELLS, 128)),
        scratch=(
            vmem((768, 128), F32),
            vmem((4, 3, CELLS + 2 * PAD, C), BF16),
            vmem((2, 3, CELLS, 128), BF16),
        ),
        spaces={0: smem},
    )(where, received, kernel_one, kernel_two)
    other = lax.ppermute(send, "core", swap)
    terms = call(
        weight_kernel,
        shape(16, ROWS, 128),
        scratch=(
            vmem((2, 3, CELLS + 2 * PAD, C), BF16),
            vmem((4, C, 128), F32),
            vmem((16 * ROWS, 128), F32),
        ),
        spaces={0: smem},
    )(where, keep, other)
    plane = exchange(terms, PLANE)
    joined = call(
        join_kernel, shape(1536, 128), scratch=(vmem((ROWS + 8, 128), F32), vmem((1536, 128), F32))
    )(plane, fields)
    back = exchange(joined.reshape(384, 4, 128), PEERS).reshape(1536, 128)
    output, input_grad, mine = call(
        split_kernel,
        (shape(16, 16 * C), shape(16, 16 * C), shape(4, 48, 128)),
        scratch=(vmem((1536, 128), F32),),
    )(back)
    line = exchange(mine, "zl")
    spread = call(spread_kernel, shape(16, ROWS, 128))(line)
    gathered = exchange(spread, PLANE)
    partner = lax.ppermute(gathered, "core", swap)
    one, two = call(
        final_kernel,
        (shape(9, C * C), shape(9, C * C)),
        scratch=(vmem((2, 16 * PITCH, 128), F32),),
        spaces={0: smem},
    )(where, gathered, partner)
    return output, input_grad, one, two


def solution(mesh):
    grid = Mesh(mesh.devices.reshape(SIZES), AXES)
    tile = P(("zl", "yh", "yl"), ("x", "zh", "core"))
    return jax.shard_map(
        per_device,
        mesh=grid,
        in_specs=(tile, P(), P(), tile),
        out_specs=(tile, tile, P(), P()),
        check_vma=False,
    )
```

time: 155 us -> 140 us (0.903)
  blocking collectives: 99.2 us -> 70.1 us
  starting transfers between devices: 23.1 us -> 35.9 us
  Pallas kernels: 7.71 us -> 10.3 us
  local copies, waits for them, and re-layouts: 5.06 us -> 3.28 us
    all_to_all x4, blocking collectives: 99.2 us -> 70.1 us  [exchange(): return lax.all_to_all(value, axes, split_axis=0, concat_axis=0, tiled=True)]
    ppermute x0 -> x2, starting transfers between devices: none -> 12.8 us  [the longest x1 7.53 us: per_device(): partner = lax.ppermute(gathered, 'core', swap)]
    ppermute x0 -> x2, waiting for transfers between devices: none -> 2.8 us  [the longest x1 1.75 us: per_device(): partner = lax.ppermute(gathered, 'core', swap)]
    pallas_call x6 -> x7, Pallas kernels: 7.71 us -> 10.3 us  [run(): pl.pallas_call(kernel, out_shape=out_shape, in_specs=[pl.BlockSpec(memory...]
    all_to_all x1, waiting for transfers between devices: 18.5 us -> 16.4 us  [exchange(): return lax.all_to_all(value, axes, split_axis=0, concat_axis=0, tiled=True)]
    unnamed x6 -> x2, local copies, waits for them, and re-layouts: 1.78 us -> 0.01 us
  transfers between devices with their start and end apart: 1 -> 3, of which waited for: 1 -> 3; matrix products, arithmetic and copies ran while one was open for 2% -> 2% of each run, Pallas kernels for 0% -> 0%
where the time goes in v5:
time: 140 us; the launch traced here: 139 us
  blocking collectives  70.1 us (50%)
  starting transfers between devices  35.9 us (26%)
  waiting for transfers between devices  19.2 us (14%)
  Pallas kernels  10.3 us (7%)
  local copies, waits for them, and re-layouts  3.28 us (2%)
    all_to_all x4, blocking collectives, exchange(): return lax.all_to_all(value, axes, split_axis=0, concat_axis=0, tiled=True)  70.1 us
    all_to_all x1, starting transfers between devices, exchange(): return lax.all_to_all(value, axes, split_axis=0, concat_axis=0, tiled=True)  23.1 us
    all_to_all x1, waiting for transfers between devices, exchange(): return lax.all_to_all(value, axes, split_axis=0, concat_axis=0, tiled=True)  16.4 us
    pallas_call x7, Pallas kernels, run(): pl.pallas_call(kernel, out_shape=out_shape, in_specs=[pl.BlockSpec(memory...  10.3 us
    ppermute x1, starting transfers between devices, per_device(): partner = lax.ppermute(gathered, 'core', swap)  7.53 us
    ppermute x1, starting transfers between devices, per_device(): other = lax.ppermute(send, 'core', swap)  5.23 us
  transfers between devices with their start and end apart: 3, of which 3 were waited for; matrix products, arithmetic and copies ran while one was open for 2% of the time, Pallas kernels for 0%

profile of v5, /device:TPU:1, one launch (start us, length us, event | category | flops | bytes accessed | tf_op | source)
XLA Modules:
  0.0 139.5 jit_solution(8515795541478326667)
XLA Ops:
  0.6 1.8 %shard_map.75 = (bf16[768,128]{1,0:T(8,128)(2,1)}, s32[1]{0:T(128)}) custom-call(s32[1]{0:T(128)} %bitcast.core_ref, bf16[16,3072]{1,0:T(8,128)(2,1)} %x_hbm.1, bf16[16,3072]{1,0:T(8,128)(2,1)} %g_hbm.1), custom_call_target="tpu_custom_call" | custom-call | tf_op jit(solution)/shard_map/pallas_call | solution.py:27
  2.4 0.0 copy-start
  2.4 23.1 %all-to-all-start = ((bf16[384,2,128]{2,1,0:T(2,128)(2,1)}), bf16[384,2,128]{2,1,0:T(2,128)(2,1)S(1)}, u32[]{:S(2)}, u32[]{:S(2)}) async-start(bf16[384,2,128]{2,1,0:T(2,128)(2,1)} %bitcast.8), calls=%async_computation | async-start | bytes 393216 | tf_op jit(solution)/shard_map/all_to_all | solution.py:264
  25.5 2.2 %reshape.32.w1_ref = bf16[1728,192]{1,0:T(8,128)(2,1)S(1)} reshape(bf16[9,36864]{1,0:T(8,128)(2,1)} %param.5) | data formatting | bytes 1327104 | tf_op jit(solution)/shard_map/reshape | solution.py:275
  27.7 0.0 copy-done
  27.7 1.1 reshape.33.w2_ref
  28.8 16.4 %all-to-all-done = bf16[384,2,128]{2,1,0:T(2,128)(2,1)S(1)} async-done(((bf16[384,2,128]{2,1,0:T(2,128)(2,1)}), bf16[384,2,128]{2,1,0:T(2,128)(2,1)S(1)}, u32[]{:S(2)}, u32[]{:S(2)}) %all-to-all-start) | async-done | bytes 196640 | tf_op jit(solution)/shard_map/all_to_all | solution.py:264
  45.2 2.9 %shard_map.76 = (bf16[128,768]{1,0:T(8,128)(2,1)S(1)}, bf16[3,256,128]{2,1,0:T(8,128)(2,1)S(1)}, bf16[3,256,128]{2,1,0:T(8,128)(2,1)S(1)}) custom-call(s32[1]{0:T(128)} %get-tuple-element.14.where_ref, bf16[768,128]{1,0:T(8,128)(2,1)S(1)} %bitcast.7, bf16[1728,192]{1,0:T(8,128)(2,1)S(1)} %reshape.32.w1_ref, bf16[1728,192]{1,0:T(8,128)(2,1)S(1)} %reshape.33.w2_ref), custom_call_target="tpu_custom_call" | custom-call | tf_op jit(solution)/shard_map/pallas_call | solution.py:27
  48.1 5.2 %collective-permute-start = (bf16[3,256,128]{2,1,0:T(8,128)(2,1)S(1)}, bf16[3,256,128]{2,1,0:T(8,128)(2,1)S(1)}, u32[]{:S(2)}, u32[]{:S(2)}) collective-permute-start(bf16[3,256,128]{2,1,0:T(8,128)(2,1)S(1)} %get-tuple-element.17), channel_id=1, source_target_pairs={{0,1},{1,0},{2,3},{3,2},{4,5},{5,4},{6,7},{7,6},{8,9},{9,8},{10,11... | collective-permute-start | bytes 589832 | tf_op jit(solution)/shard_map/ppermute | solution.py:300
  53.3 1.0 collective-permute-done.other_ref
  54.4 1.8 %shard_map.77 = bf16[16,168,128]{2,1,0:T(8,128)(2,1)S(1)} custom-call(s32[1]{0:T(128)} %get-tuple-element.14.where_ref, bf16[3,256,128]{2,1,0:T(8,128)(2,1)S(1)} %get-tuple-element.16.own_ref, bf16[3,256,128]{2,1,0:T(8,128)(2,1)S(1)} %collective-permute-done.other_ref), custom_call_target="tpu_custom_call" | custom-call | tf_op jit(solution)/shard_map/pallas_call | solution.py:27
  56.2 15.9 %all_to_all.25.s_ref = bf16[16,168,128]{2,1,0:T(8,128)(2,1)S(1)} all-to-all(bf16[16,168,128]{2,1,0:T(8,128)(2,1)S(1)} %shard_map.77), channel_id=1, replica_groups=mesh['zl'=4,'yh'=2,'yl'=2,'x'=4,'zh'=4,'core'=2] {'yl','x','yh'}, dimensions={0} | all-to-all | bytes 1376256 | tf_op jit(solution)/shard_map/all_to_all | solution.py:264
  72.2 0.2 shard_map.78
  72.4 32.0 %all_to_all.26 = bf16[384,4,128]{2,1,0:T(4,128)(2,1)S(1)} all-to-all(bf16[384,4,128]{2,1,0:T(4,128)(2,1)S(1)} %bitcast.6), channel_id=1, replica_groups=mesh['zl'=4,'yh'=2,'yl'=2,'x'=4,'zh'=4,'core'=2] {'x','zh','zl','yh'}, dimensions={0} | all-to-all | bytes 786432 | tf_op jit(solution)/shard_map/all_to_all | solution.py:264
  104.3 0.8 shard_map.79
  105.2 7.2 %all_to_all.27.z_ref = bf16[4,48,128]{2,1,0:T(8,128)(2,1)S(1)} all-to-all(bf16[4,48,128]{2,1,0:T(8,128)(2,1)S(1)} %get-tuple-element.21), channel_id=1, replica_groups=mesh['zl'=4,'yh'=2,'yl'=2,'x'=4,'zh'=4,'core'=2] {'zl'}, dimensions={0} | all-to-all | bytes 98304 | tf_op jit(solution)/shard_map/all_to_all | solution.py:264
  112.3 0.1 shard_map.80
  112.4 15.0 %all_to_all.28.own_ref = bf16[16,168,128]{2,1,0:T(8,128)(2,1)S(1)} all-to-all(bf16[16,168,128]{2,1,0:T(8,128)(2,1)S(1)} %shard_map.80), channel_id=1, replica_groups=mesh['zl'=4,'yh'=2,'yl'=2,'x'=4,'zh'=4,'core'=2] {'yl','x','yh'}, dimensions={0} | all-to-all | bytes 1376256 | tf_op jit(solution)/shard_map/all_to_all | solution.py:264
  127.4 7.5 %collective-permute-start.1 = (bf16[16,168,128]{2,1,0:T(8,128)(2,1)S(1)}, bf16[16,168,128]{2,1,0:T(8,128)(2,1)S(1)}, u32[]{:S(2)}, u32[]{:S(2)}) collective-permute-start(bf16[16,168,128]{2,1,0:T(8,128)(2,1)S(1)} %all_to_all.28.own_ref), channel_id=1, source_target_pairs={{0,1},{1,0},{2,3},{3,2},{4,5},{5,4},{6,7},{7,6},{8,9},{9,8},{10,11... | collective-permute-start | bytes 2064392 | tf_op jit(solution)/shard_map/ppermute | solution.py:324
  135.0 1.7 %collective-permute-done.1.other_ref = bf16[16,168,128]{2,1,0:T(8,128)(2,1)S(1)} collective-permute-done((bf16[16,168,128]{2,1,0:T(8,128)(2,1)S(1)}, bf16[16,168,128]{2,1,0:T(8,128)(2,1)S(1)}, u32[]{:S(2)}, u32[]{:S(2)}) %collective-permute-start.1) | collective-permute-done | bytes 688160 | tf_op jit(solution)/shard_map/ppermute | solution.py:324
  136.7 2.8 %shard_map.81 = (bf16[9,36864]{1,0:T(8,128)(2,1)}, bf16[9,36864]{1,0:T(8,128)(2,1)}) custom-call(s32[1]{0:T(128)} %get-tuple-element.14.where_ref, bf16[16,168,128]{2,1,0:T(8,128)(2,1)S(1)} %all_to_all.28.own_ref, bf16[16,168,128]{2,1,0:T(8,128)(2,1)S(1)} %collective-permute-done.1.other_ref), custom_call_target="tpu_custom_call" | custom-call | tf_op jit(solution)/shard_map/pallas_call | solution.py:27
Async XLA Ops:
  2.4 25.3 %copy-start = (bf16[9,36864]{1,0:T(8,128)(2,1)S(1)}, bf16[9,36864]{1,0:T(8,128)(2,1)}, u32[]{:S(2)}) copy-start(bf16[9,36864]{1,0:T(8,128)(2,1)} %param.6) | copy-start | bytes 1990660
  2.4 42.8 %all-to-all-start = ((bf16[384,2,128]{2,1,0:T(2,128)(2,1)}), bf16[384,2,128]{2,1,0:T(2,128)(2,1)S(1)}, u32[]{:S(2)}, u32[]{:S(2)}) async-start(bf16[384,2,128]{2,1,0:T(2,128)(2,1)} %bitcast.8), calls=%async_computation | async-start | bytes 393216 | tf_op jit(solution)/shard_map/all_to_all | solution.py:264
  48.1 6.3 %collective-permute-start = (bf16[3,256,128]{2,1,0:T(8,128)(2,1)S(1)}, bf16[3,256,128]{2,1,0:T(8,128)(2,1)S(1)}, u32[]{:S(2)}, u32[]{:S(2)}) collective-permute-start(bf16[3,256,128]{2,1,0:T(8,128)(2,1)S(1)} %get-tuple-element.17), channel_id=1, source_target_pairs={{0,1},{1,0},{2,3},{3,2},{4,5},{5,4},{6,7},{7,6},{8,9},{9,8},{10,11... | collective-permute-start | bytes 589832 | tf_op jit(solution)/shard_map/ppermute | solution.py:300
  127.4 9.3 %collective-permute-start.1 = (bf16[16,168,128]{2,1,0:T(8,128)(2,1)S(1)}, bf16[16,168,128]{2,1,0:T(8,128)(2,1)S(1)}, u32[]{:S(2)}, u32[]{:S(2)}) collective-permute-start(bf16[16,168,128]{2,1,0:T(8,128)(2,1)S(1)} %all_to_all.28.own_ref), channel_id=1, source_target_pairs={{0,1},{1,0},{2,3},{3,2},{4,5},{5,4},{6,7},{7,6},{8,9},{9,8},{10,11... | collective-permute-start | bytes 2064392 | tf_op jit(solution)/shard_map/ppermute | solution.py:324

commit v6 on v5

--- a/solution.py
+++ b/solution.py
@@ -1,3 +1,5 @@
+import functools
+
 import jax
 import jax.numpy as jnp
 from jax import lax
@@ -8,18 +10,20 @@
 C = 192
 AXES = ("zl", "yh", "yl", "x", "zh", "core")
 SIZES = (4, 2, 2, 4, 4, 2)
-PEERS = ("x", "zh", "zl", "yh")
+PEERS = ("zh", "zl", "x", "yh")
 PLANE = ("yl", "x", "yh")
 BF16 = jnp.bfloat16
 F32 = jnp.float32
 ROWS = 168
+TERMS = 162
 PITCH = 169
-PAD = 32
+ZH = 64
+PAD = 2 * ZH
 CELLS = 256
 OFFSETS = [(a, b) for a in (-1, 0, 1) for b in (-1, 0, 1)]
 
 
-def call(kernel, out_shape, scratch=(), spaces={}, out_specs=None, limit=40 * 1024 * 1024):
+def call(kernel, out_shape, scratch=(), spaces={}, out_specs=None, limit=40 * 1024 * 1024, **extra):
     if out_specs is None:
         out_specs = jax.tree.map(lambda _: pl.BlockSpec(memory_space=pltpu.VMEM), out_shape)
 
@@ -33,6 +37,7 @@
             out_specs=out_specs,
             scratch_shapes=list(scratch),
             compiler_params=pltpu.CompilerParams(vmem_limit_bytes=limit),
+            **extra,
         )(*args)
 
     return run
@@ -62,21 +67,31 @@
 
 
 def put_taps(tap_ref, slot, field, step):
-    within = lax.broadcasted_iota(jnp.int32, (CELLS, C), 0) % 8
+    row = lax.broadcasted_iota(jnp.int32, (CELLS, C), 0)
+    zl_of, x_of, yh_of = (row // 16) % 4, (row % 8) // 2, row % 2
+
+    def ahead(value, rows):
+        return pltpu.roll(value, (-rows) % CELLS, 0)
+
+    more = step * ZH
     for a in (-1, 0, 1):
         moved = field
         if a != 0:
-            rolled = pltpu.roll(field, (-a * step) % CELLS, 0)
-            seen = (within + a * step >= 0) & (within + a * step < 8)
-            moved = jnp.where(seen, rolled, 0.0)
+            inside = (zl_of + a >= 0) & (zl_of + a < 4)
+            if step == 2:
+                moved = jnp.where(inside, ahead(field, 16 * a), 0.0)
+            else:
+                crossed = jnp.where(inside, ahead(field, 15 * a), 0.0)
+                moved = jnp.where(yh_of == (0 if a == 1 else 1), ahead(field, a), crossed)
+        before = jnp.where(x_of > 0, ahead(moved, -2), 0.0)[CELLS - more :]
+        after = jnp.where(x_of < 3, ahead(moved, 2), 0.0)[:more]
+        tap_ref[slot, a + 1, PAD - more : PAD, :] = before.astype(BF16)
         tap_ref[slot, a + 1, PAD : PAD + CELLS, :] = moved.astype(BF16)
-    for a in range(3):
-        tap_ref[slot, a, 0:PAD, :] = jnp.zeros((PAD, C), BF16)
-        tap_ref[slot, a, PAD + CELLS : 2 * PAD + CELLS, :] = jnp.zeros((PAD, C), BF16)
+        tap_ref[slot, a + 1, PAD + CELLS : PAD + CELLS + more, :] = after.astype(BF16)
 
 
 def get_tap(tap_ref, slot, a, b, step):
-    start = PAD + 16 * b * step
+    start = PAD + ZH * b * step
     return tap_ref[slot, a + 1, start : start + CELLS, :]
 
 
@@ -138,60 +153,54 @@
     send_ref[...] = pair_ref[1 - core]
 
 
-def weight_kernel(where_ref, own_ref, other_ref, o_ref, tap_ref, ft_ref, wg_ref):
-    turned = []
-    grads = []
-    for ref in (own_ref, other_ref):
-        first, mixed, last = [ref[n].astype(F32) for n in range(3)]
-        turned.append(jnp.concatenate([first, mixed[:, 0:64]], axis=1).T)
-        grads.append(jnp.concatenate([last, mixed[:, 64:128]], axis=1))
-    for n in range(4):
-        ft_ref[n] = turned[n // 2][:, (n % 2) * 128 : (n % 2) * 128 + 128]
-    left = [
-        jnp.concatenate(
-            [
-                jnp.concatenate(
-                    [ft_ref[n, pl.ds(odd, 96, stride=2), :] for n in (2 * half, 2 * half + 1)], axis=1
-                )
-                for odd in (0, 1)
-            ],
-            axis=0,
-        ).astype(BF16)
-        for half in (0, 1)
-    ]
-    for c in range(16):
-        wg_ref[c * ROWS + 162 : c * ROWS + 168, :] = jnp.zeros((6, 128), F32)
+def half_kernel(own, where_ref, pair_ref, *refs):
+    o_ref, tap_ref, ft_ref = refs[-4:-1] if not own else refs[-3:]
+    first, mixed, last = [pair_ref[n].astype(F32) for n in range(3)]
+    turned = jnp.concatenate([first, mixed[:, 0:64]], axis=1).T
+    grad = jnp.concatenate([last, mixed[:, 64:128]], axis=1)
+    for n in (0, 1):
+        ft_ref[n] = turned[:, n * 128 : n * 128 + 128]
+    left = jnp.concatenate(
+        [
+            jnp.concatenate([ft_ref[n, pl.ds(odd, 96, stride=2), :] for n in (0, 1)], axis=1)
+            for odd in (0, 1)
+        ],
+        axis=0,
+    ).astype(BF16)
 
     def weight_grad(step):
-        for half in (0, 1):
-            put_taps(tap_ref, half, grads[half], step)
+        put_taps(tap_ref, 0, grad, step)
         for t, (a, b) in enumerate(OFFSETS):
-            full = jnp.dot(left[0], get_tap(tap_ref, 0, -a, -b, step), preferred_element_type=F32)
-            full = full + jnp.dot(
-                left[1], get_tap(tap_ref, 1, -a, -b, step), preferred_element_type=F32
-            )
+            full = jnp.dot(left, get_tap(tap_ref, 0, -a, -b, step), preferred_element_type=F32)
+            if own:
+                o_ref[t] = full
+                continue
+            full = full + refs[0][t]
             even, odd = full[0:96], full[96:192]
             lanes = (
                 even[:, 0:128],
                 jnp.concatenate([even[:, 128:192], odd[:, 0:64]], axis=1),
                 odd[:, 64:192],
             )
+            wg_ref = refs[-1]
             for q in range(3):
                 for u in range(6):
-                    wg_ref[pl.ds(t * 18 + q * 6 + u, 16, stride=ROWS), :] = lanes[q][
+                    wg_ref[pl.ds(t * 18 + q * 6 + u, 16, stride=TERMS), :] = lanes[q][
                         u * 16 : u * 16 + 16
                     ]
 
     for core, step in ((0, 2), (1, 1)):
         pl.when(where_ref[0] == core)(lambda step=step: weight_grad(step))
-    for c in range(16):
-        o_ref[c] = wg_ref[c * ROWS : (c + 1) * ROWS, :].astype(BF16)
-
-
-def join_kernel(s_ref, f_ref, out_ref, sum_ref, row_ref):
-    total = s_ref[0].astype(F32)
+    if not own:
+        o_ref[...] = refs[-1][...].astype(BF16)
+
+
+def join_kernel(s_ref, f_ref, out_ref, sum_ref, row_ref, part_ref):
+    part_ref[0 : 16 * TERMS, :] = s_ref[...].astype(F32)
+    part_ref[16 * TERMS : 16 * TERMS + 8, :] = jnp.zeros((8, 128), F32)
+    total = part_ref[0:ROWS, :]
     for c in range(1, 16):
-        total = total + s_ref[c].astype(F32)
+        total = total + part_ref[c * TERMS : c * TERMS + ROWS, :]
     sum_ref[0:ROWS, :] = total
     sum_ref[ROWS : ROWS + 8, :] = jnp.zeros((8, 128), F32)
     value = f_ref[...].astype(F32)
@@ -204,36 +213,35 @@
                 first = t * 18 + zl * 6 if zl < 3 else 144 + t * 3
                 piece = sum_ref[first : first + 6, :]
                 for zh in range(4):
-                    start = (x * 32 + zh * 8 + zl * 2 + yh) * 12 + 6
+                    start = ((zh * 4 + zl) * 8 + t) * 12 + 6
                     row_ref[start : start + 6, :] = piece
     out_ref[...] = row_ref[...].astype(BF16)
 
 
-def split_kernel(r_ref, out_ref, ig_ref, z_ref, row_ref):
+def line_kernel(r_ref, z_ref, row_ref):
     row_ref[...] = r_ref[...].astype(F32)
-    tiles = [row_ref[pl.ds(t, 128, stride=12), :] for t in range(12)]
+    slots = []
+    for t in range(6, 12):
+        value = row_ref[pl.ds(t, 128, stride=12), :]
+        total = value[0:8]
+        for z in range(1, 16):
+            total = total + value[z * 8 : z * 8 + 8]
+        slots.append(total * (1.0 / 256.0))
+    mine = jnp.concatenate(slots, axis=0).astype(BF16)
+    for z in range(4):
+        z_ref[z] = mine
+
+
+def tile_kernel(r_ref, out_ref, ig_ref, row_ref):
+    row_ref[...] = r_ref[...].astype(F32)
     for f, ref in enumerate((out_ref, ig_ref)):
-        wide = jnp.concatenate(tiles[3 * f : 3 * f + 3], axis=1)
+        tiles = [row_ref[pl.ds(3 * f + t, 128, stride=12), :] for t in range(3)]
+        wide = jnp.concatenate(tiles, axis=1)
         halves = []
         for k in (0, 1):
             part = wide[:, k * C : (k + 1) * C]
             halves.append(jnp.concatenate([part[j * 8 : j * 8 + 8] for j in range(16)], axis=1))
         ref[...] = jnp.concatenate(halves, axis=0).astype(BF16)
-    row = lax.broadcasted_iota(jnp.int32, (8, 128), 0)
-    slots = []
-    for value in tiles[6:12]:
-        total = jnp.zeros((8, 128), F32)
-        for x in range(4):
-            part = value[x * 32 : x * 32 + 8]
-            for zh in range(1, 4):
-                part = part + value[x * 32 + zh * 8 : x * 32 + zh * 8 + 8]
-            part = part + pltpu.roll(part, 4, 0)
-            part = part + pltpu.roll(part, 2, 0)
-            total = jnp.where(row // 2 == x, part, total)
-        slots.append(total * (1.0 / 256.0))
-    mine = jnp.concatenate(slots, axis=0).astype(BF16)
-    for z in range(4):
-        z_ref[z] = mine
 
 
 def spread_kernel(z_ref, out_ref):
@@ -243,21 +251,36 @@
         out_ref[c, 160:168, :] = z_ref[3, 16:32, :][0:8]
 
 
-def final_kernel(where_ref, own_ref, other_ref, one_ref, two_ref, scr_ref):
-    core = where_ref[0]
+def final_kernel(own, where_ref, r_ref, *refs):
+    one_ref, two_ref, out_ref, scr_ref, sems = refs[-5:]
     for c in range(16):
-        scr_ref[core, c * PITCH : c * PITCH + ROWS, :] = own_ref[c].astype(F32)
-        scr_ref[1 - core, c * PITCH : c * PITCH + ROWS, :] = other_ref[c].astype(F32)
-    for index, ref in enumerate((two_ref, one_ref)):
-        for n in range(288):
-            m, q = n // 3, n % 3
-            u, c = m // 16, m % 16
-            v = q * 6 + u
-            first = (c // 8) * 8 * PITCH + c % 8
-            eight = scr_ref[index, pl.ds(first + v * 8, 8, stride=PITCH), :]
-            last = first + (v // 3) * PITCH + (18 + v % 3) * 8
-            nine = jnp.concatenate([eight, scr_ref[index, last : last + 1, :]], axis=0)
-            ref[:, n * 128 : (n + 1) * 128] = nine.astype(BF16)
+        scr_ref[c * PITCH : c * PITCH + ROWS, :] = r_ref[c].astype(F32)
+    def each_copy(part, act):
+        lanes = pl.ds(part * 9216, 9216)
+        for core in (0, 1):
+            target = two_ref if (core == 0) == own else one_ref
+
+            @pl.when(where_ref[0] == core)
+            def _(target=target):
+                act(
+                    pltpu.make_async_copy(
+                        out_ref.at[:, lanes], target.at[:, lanes], sems.at[part]
+                    )
+                )
+
+    for n in range(288):
+        m, q = n // 3, n % 3
+        u, c = m // 16, m % 16
+        v = q * 6 + u
+        first = (c // 8) * 8 * PITCH + c % 8
+        eight = scr_ref[pl.ds(first + v * 8, 8, stride=PITCH), :]
+        last = first + (v // 3) * PITCH + (18 + v % 3) * 8
+        nine = jnp.concatenate([eight, scr_ref[last : last + 1, :]], axis=0)
+        out_ref[:, n * 128 : (n + 1) * 128] = nine.astype(BF16)
+        if n % 72 == 71:
+            each_copy(n // 72, lambda copy: copy.start())
+    for part in range(4):
+        each_copy(part, lambda copy: copy.wait())
 
 
 def exchange(value, axes):
@@ -272,6 +295,7 @@
     smem, hbm, vmem = pltpu.SMEM, pltpu.HBM, pltpu.VMEM
     core = lax.axis_index("core").astype(jnp.int32).reshape(1)
     swap = [(0, 1), (1, 0)]
+    short = pl.CostEstimate(flops=10**9, bytes_accessed=3 * 10**6, transcendentals=0)
     kernel_one = first_weight.reshape(9 * C, C)
     kernel_two = second_weight.reshape(9 * C, C)
     packed, where = call(
@@ -298,36 +322,61 @@
         spaces={0: smem},
     )(where, received, kernel_one, kernel_two)
     other = lax.ppermute(send, "core", swap)
+    scratch = (vmem((1, 3, CELLS + 2 * PAD, C), BF16), vmem((2, C, 128), F32))
+    begun = call(
+        functools.partial(half_kernel, True),
+        shape(9, C, C, dtype=F32),
+        scratch=scratch,
+        spaces={0: smem},
+        cost_estimate=short,
+    )(where, keep)
     terms = call(
-        weight_kernel,
-        shape(16, ROWS, 128),
+        functools.partial(half_kernel, False),
+        shape(16 * TERMS, 128),
+        scratch=(*scratch, vmem((16 * TERMS, 128), F32)),
+        spaces={0: smem},
+    )(where, other, begun)
+    plane = exchange(terms.reshape(8 * TERMS, 2, 128), PLANE).reshape(16 * TERMS, 128)
+    joined = call(
+        join_kernel,
+        shape(1536, 128),
         scratch=(
-            vmem((2, 3, CELLS + 2 * PAD, C), BF16),
-            vmem((4, C, 128), F32),
-            vmem((16 * ROWS, 128), F32),
+            vmem((ROWS + 8, 128), F32),
+            vmem((1536, 128), F32),
+            vmem((16 * TERMS + 8, 128), F32),
         ),
-        spaces={0: smem},
-    )(where, keep, other)
-    plane = exchange(terms, PLANE)
-    joined = call(
-        join_kernel, shape(1536, 128), scratch=(vmem((ROWS + 8, 128), F32), vmem((1536, 128), F32))
     )(plane, fields)
     back = exchange(joined.reshape(384, 4, 128), PEERS).reshape(1536, 128)
-    output, input_grad, mine = call(
-        split_kernel,
-        (shape(16, 16 * C), shape(16, 16 * C), shape(4, 48, 128)),
-        scratch=(vmem((1536, 128), F32),),
-    )(back)
+    mine = call(line_kernel, shape(4, 48, 128), scratch=(vmem((1536, 128), F32),))(back)
     line = exchange(mine, "zl")
     spread = call(spread_kernel, shape(16, ROWS, 128))(line)
     gathered = exchange(spread, PLANE)
     partner = lax.ppermute(gathered, "core", swap)
+    output, input_grad = call(
+        tile_kernel,
+        (shape(16, 16 * C), shape(16, 16 * C)),
+        scratch=(vmem((1536, 128), F32),),
+        cost_estimate=short,
+    )(back)
+    weight = shape(9, C * C)
+    anywhere = pl.BlockSpec(memory_space=pl.ANY)
+    scratch = (vmem((9, C * C), BF16), vmem((16 * PITCH, 128), F32), pltpu.SemaphoreType.DMA((4,)))
     one, two = call(
-        final_kernel,
-        (shape(9, C * C), shape(9, C * C)),
-        scratch=(vmem((2, 16 * PITCH, 128), F32),),
+        functools.partial(final_kernel, True),
+        (weight, weight),
+        scratch=scratch,
         spaces={0: smem},
-    )(where, gathered, partner)
+        out_specs=(anywhere, anywhere),
+        cost_estimate=short,
+    )(where, gathered)
+    one, two = call(
+        functools.partial(final_kernel, False),
+        (weight, weight),
+        scratch=scratch,
+        spaces={0: smem, 2: pl.ANY, 3: pl.ANY},
+        out_specs=(anywhere, anywhere),
+        input_output_aliases={2: 0, 3: 1},
+    )(where, partner, one, two)
     return output, input_grad, one, two
 
 

time: 140 us -> 139 us (level)
  waiting for transfers between devices: 19.2 us -> 12.4 us
  blocking collectives: 70.1 us -> 72.8 us
  Pallas kernels: 10.3 us -> 12.5 us
    all_to_all x1, waiting for transfers between devices: 16.4 us -> 12.4 us  [exchange(): return lax.all_to_all(value, axes, split_axis=0, concat_axis=0, tiled=True)]
    all_to_all x4, blocking collectives: 70.1 us -> 72.8 us  [exchange(): return lax.all_to_all(value, axes, split_axis=0, concat_axis=0, tiled=True)]
    pallas_call x7 -> x10, Pallas kernels: 10.3 us -> 12.5 us  [run(): pl.pallas_call(kernel, out_shape=out_shape, in_specs=[pl.BlockSpec(memory...]
    ppermute x1, waiting for transfers between devices: 1.75 us -> 0.01 us  [per_device(): partner = lax.ppermute(gathered, 'core', swap)]
  transfers between devices with their start and end apart: 3 -> 3, of which waited for: 3 -> 1; matrix products, arithmetic and copies ran while one was open for 2% -> 2% of each run, Pallas kernels for 0% -> 3%
where the time goes in v6:
time: 139 us
  blocking collectives  72.8 us (52%)
  starting transfers between devices  37.2 us (27%)
  Pallas kernels  12.5 us (9%)
  waiting for transfers between devices  12.4 us (9%)
  local copies, waits for them, and re-layouts  3.28 us (2%)
    all_to_all x4, blocking collectives, exchange(): return lax.all_to_all(value, axes, split_axis=0, concat_axis=0, tiled=True)  72.8 us
    all_to_all x1, starting transfers between devices, exchange(): return lax.all_to_all(value, axes, split_axis=0, concat_axis=0, tiled=True)  23.1 us
    pallas_call x10, Pallas kernels, run(): pl.pallas_call(kernel, out_shape=out_shape, in_specs=[pl.BlockSpec(memory...  12.5 us
    all_to_all x1, waiting for transfers between devices, exchange(): return lax.all_to_all(value, axes, split_axis=0, concat_axis=0, tiled=True)  12.4 us
    ppermute x1, starting transfers between devices, per_device(): partner = lax.ppermute(gathered, 'core', swap)  8.13 us
    ppermute x1, starting transfers between devices, per_device(): other = lax.ppermute(send, 'core', swap)  6.02 us
  transfers between devices with their start and end apart: 3, of which 1 were waited for; matrix products, arithmetic and copies ran while one was open for 2% of the time, Pallas kernels for 3%

profile of v6, /device:TPU:1, one launch (start us, length us, event | category | flops | bytes accessed | tf_op | source)
XLA Modules:
  0.0 139.0 jit_solution(5601887905267432291)
XLA Ops:
  0.6 1.8 %shard_map.75 = (bf16[768,128]{1,0:T(8,128)(2,1)}, s32[1]{0:T(128)}) custom-call(s32[1]{0:T(128)} %bitcast.core_ref, bf16[16,3072]{1,0:T(8,128)(2,1)} %x_hbm.1, bf16[16,3072]{1,0:T(8,128)(2,1)} %g_hbm.1), custom_call_target="tpu_custom_call" | custom-call | tf_op jit(solution)/shard_map/pallas_call | solution.py:31
  2.4 0.0 copy-start
  2.4 23.1 %all-to-all-start = ((bf16[384,2,128]{2,1,0:T(2,128)(2,1)}), bf16[384,2,128]{2,1,0:T(2,128)(2,1)S(1)}, u32[]{:S(2)}, u32[]{:S(2)}) async-start(bf16[384,2,128]{2,1,0:T(2,128)(2,1)} %bitcast.13), calls=%async_computation | async-start | bytes 393216 | tf_op jit(solution)/shard_map/all_to_all | solution.py:287
  25.5 2.2 %reshape.38.w1_ref = bf16[1728,192]{1,0:T(8,128)(2,1)S(1)} reshape(bf16[9,36864]{1,0:T(8,128)(2,1)} %param.5) | data formatting | bytes 1327104 | tf_op jit(solution)/shard_map/reshape | solution.py:299
  27.7 0.0 copy-done
  27.7 1.1 reshape.39.w2_ref
  28.8 12.4 %all-to-all-done = bf16[384,2,128]{2,1,0:T(2,128)(2,1)S(1)} async-done(((bf16[384,2,128]{2,1,0:T(2,128)(2,1)}), bf16[384,2,128]{2,1,0:T(2,128)(2,1)S(1)}, u32[]{:S(2)}, u32[]{:S(2)}) %all-to-all-start) | async-done | bytes 196640 | tf_op jit(solution)/shard_map/all_to_all | solution.py:287
  41.3 3.2 %shard_map.76 = (bf16[128,768]{1,0:T(8,128)(2,1)S(1)}, bf16[3,256,128]{2,1,0:T(8,128)(2,1)S(1)}, bf16[3,256,128]{2,1,0:T(8,128)(2,1)S(1)}) custom-call(s32[1]{0:T(128)} %get-tuple-element.15.where_ref, bf16[768,128]{1,0:T(8,128)(2,1)S(1)} %bitcast.12, bf16[1728,192]{1,0:T(8,128)(2,1)S(1)} %reshape.38.w1_ref, bf16[1728,192]{1,0:T(8,128)(2,1)S(1)} %reshape.39.w2_ref), custom_call_target="tpu_custom_call" | custom-call | tf_op jit(solution)/shard_map/pallas_call | solution.py:31
  44.4 6.0 %collective-permute-start = (bf16[3,256,128]{2,1,0:T(8,128)(2,1)S(1)}, bf16[3,256,128]{2,1,0:T(8,128)(2,1)S(1)}, u32[]{:S(2)}, u32[]{:S(2)}) collective-permute-start(bf16[3,256,128]{2,1,0:T(8,128)(2,1)S(1)} %get-tuple-element.17), channel_id=1, source_target_pairs={{0,1},{1,0},{2,3},{3,2},{4,5},{5,4},{6,7},{7,6},{8,9},{9,8},{10,11... | collective-permute-start | bytes 589832 | tf_op jit(solution)/shard_map/ppermute | solution.py:324
  50.5 1.3 shard_map.77.refs_0_
  51.8 0.0 collective-permute-done.pair_ref
  51.8 1.5 %shard_map.78 = bf16[2592,128]{1,0:T(8,128)(2,1)S(1)} custom-call(s32[1]{0:T(128)} %get-tuple-element.15.where_ref, bf16[3,256,128]{2,1,0:T(8,128)(2,1)S(1)} %collective-permute-done.pair_ref, f32[9,192,192]{2,1,0:T(8,128)S(1)} %shard_map.77.refs_0_), custom_call_target="tpu_custom_call" | custom-call | tf_op jit(solution)/shard_map/pallas_call | solution.py:31
  53.2 18.7 %all_to_all.25 = bf16[1296,2,128]{2,1,0:T(2,128)(2,1)S(1)} all-to-all(bf16[1296,2,128]{2,1,0:T(2,128)(2,1)S(1)} %bitcast.8), channel_id=1, replica_groups=mesh['zl'=4,'yh'=2,'yl'=2,'x'=4,'zh'=4,'core'=2] {'yl','x','yh'}, dimensions={0} | all-to-all | bytes 1327104 | tf_op jit(solution)/shard_map/all_to_all | solution.py:287
  71.9 0.2 shard_map.79
  72.2 28.4 %all_to_all.26 = bf16[384,4,128]{2,1,0:T(4,128)(2,1)S(1)} all-to-all(bf16[384,4,128]{2,1,0:T(4,128)(2,1)S(1)} %bitcast.11), channel_id=1, replica_groups=mesh['zl'=4,'yh'=2,'yl'=2,'x'=4,'zh'=4,'core'=2] {'zh','zl','x','yh'}, dimensions={0} | all-to-all | bytes 786432 | tf_op jit(solution)/shard_map/all_to_all | solution.py:287
  100.6 0.1 shard_map.81
  100.7 13.0 %all_to_all.27.z_ref = bf16[4,48,128]{2,1,0:T(8,128)(2,1)S(1)} all-to-all(bf16[4,48,128]{2,1,0:T(8,128)(2,1)S(1)} %shard_map.81), channel_id=1, replica_groups=mesh['zl'=4,'yh'=2,'yl'=2,'x'=4,'zh'=4,'core'=2] {'zl'}, dimensions={0} | all-to-all | bytes 98304 | tf_op jit(solution)/shard_map/all_to_all | solution.py:287
  113.7 0.1 shard_map.82
  113.8 12.6 %all_to_all.28.r_ref = bf16[16,168,128]{2,1,0:T(8,128)(2,1)S(1)} all-to-all(bf16[16,168,128]{2,1,0:T(8,128)(2,1)S(1)} %shard_map.82), channel_id=1, replica_groups=mesh['zl'=4,'yh'=2,'yl'=2,'x'=4,'zh'=4,'core'=2] {'yl','x','yh'}, dimensions={0} | all-to-all | bytes 1376256 | tf_op jit(solution)/shard_map/all_to_all | solution.py:287
  126.4 8.1 %collective-permute-start.1 = (bf16[16,168,128]{2,1,0:T(8,128)(2,1)S(1)}, bf16[16,168,128]{2,1,0:T(8,128)(2,1)S(1)}, u32[]{:S(2)}, u32[]{:S(2)}) collective-permute-start(bf16[16,168,128]{2,1,0:T(8,128)(2,1)S(1)} %all_to_all.28.r_ref), channel_id=1, source_target_pairs={{0,1},{1,0},{2,3},{3,2},{4,5},{5,4},{6,7},{7,6},{8,9},{9,8},{10,11... | collective-permute-start | bytes 2064392 | tf_op jit(solution)/shard_map/ppermute | solution.py:354
  134.6 0.8 shard_map.80
  135.4 1.8 %shard_map.83 = (bf16[9,36864]{1,0:T(8,128)(2,1)}, bf16[9,36864]{1,0:T(8,128)(2,1)}) custom-call(s32[1]{0:T(128)} %get-tuple-element.15.where_ref, bf16[16,168,128]{2,1,0:T(8,128)(2,1)S(1)} %all_to_all.28.r_ref), custom_call_target="tpu_custom_call" | custom-call | flops 1000000000 | bytes 3000000 | tf_op jit(solution)/shard_map/pallas_call | solution.py:31
  137.2 0.0 collective-permute-done.1.r_ref
  137.2 1.8 %shard_map.84 = (bf16[9,36864]{1,0:T(8,128)(2,1)}, bf16[9,36864]{1,0:T(8,128)(2,1)}) custom-call(s32[1]{0:T(128)} %get-tuple-element.15.where_ref, bf16[16,168,128]{2,1,0:T(8,128)(2,1)S(1)} %collective-permute-done.1.r_ref, bf16[9,36864]{1,0:T(8,128)(2,1)} %get-tuple-element.22.refs_0_, ...), custom_call_target="tpu_custom_call", output_to_operand_aliasing={{0}: (2, {}), {1}: (3, {})} | custom-call | tf_op jit(solution)/shard_map/pallas_call | solution.py:31
Async XLA Ops:
  2.4 25.3 %copy-start = (bf16[9,36864]{1,0:T(8,128)(2,1)S(1)}, bf16[9,36864]{1,0:T(8,128)(2,1)}, u32[]{:S(2)}) copy-start(bf16[9,36864]{1,0:T(8,128)(2,1)} %param.6) | copy-start | bytes 1990660
  2.4 38.8 %all-to-all-start = ((bf16[384,2,128]{2,1,0:T(2,128)(2,1)}), bf16[384,2,128]{2,1,0:T(2,128)(2,1)S(1)}, u32[]{:S(2)}, u32[]{:S(2)}) async-start(bf16[384,2,128]{2,1,0:T(2,128)(2,1)} %bitcast.13), calls=%async_computation | async-start | bytes 393216 | tf_op jit(solution)/shard_map/all_to_all | solution.py:287
  44.4 7.3 %collective-permute-start = (bf16[3,256,128]{2,1,0:T(8,128)(2,1)S(1)}, bf16[3,256,128]{2,1,0:T(8,128)(2,1)S(1)}, u32[]{:S(2)}, u32[]{:S(2)}) collective-permute-start(bf16[3,256,128]{2,1,0:T(8,128)(2,1)S(1)} %get-tuple-element.17), channel_id=1, source_target_pairs={{0,1},{1,0},{2,3},{3,2},{4,5},{5,4},{6,7},{7,6},{8,9},{9,8},{10,11... | collective-permute-start | bytes 589832 | tf_op jit(solution)/shard_map/ppermute | solution.py:324
  126.4 10.8 %collective-permute-start.1 = (bf16[16,168,128]{2,1,0:T(8,128)(2,1)S(1)}, bf16[16,168,128]{2,1,0:T(8,128)(2,1)S(1)}, u32[]{:S(2)}, u32[]{:S(2)}) collective-permute-start(bf16[16,168,128]{2,1,0:T(8,128)(2,1)S(1)} %all_to_all.28.r_ref), channel_id=1, source_target_pairs={{0,1},{1,0},{2,3},{3,2},{4,5},{5,4},{6,7},{7,6},{8,9},{9,8},{10,11... | collective-permute-start | bytes 2064392 | tf_op jit(solution)/shard_map/ppermute | solution.py:354

commit v7 on v6

--- a/solution.py
+++ b/solution.py
@@ -12,11 +12,15 @@
 SIZES = (4, 2, 2, 4, 4, 2)
 PEERS = ("zh", "zl", "x", "yh")
 PLANE = ("yl", "x", "yh")
+LINE = ("zh", "zl")
 BF16 = jnp.bfloat16
 F32 = jnp.float32
 ROWS = 168
 TERMS = 162
-PITCH = 169
+FIELD = 96
+BOTH = TERMS + FIELD
+PIECE = 41
+LINE_ROWS = 48 + PIECE + 1
 ZH = 64
 PAD = 2 * ZH
 CELLS = 256
@@ -49,11 +53,12 @@
     return value * normal_cdf, normal_cdf + value * density
 
 
-def pack_kernel(core_ref, x_hbm, g_hbm, o_ref, where_ref, in_ref, row_ref, sems):
+def pack_kernel(core_ref, half_ref, x_hbm, g_hbm, o_ref, where_ref, in_ref, row_ref, sems):
     copies = [pltpu.make_async_copy(h, in_ref.at[n], sems.at[n]) for n, h in enumerate((x_hbm, g_hbm))]
     for copy in copies:
         copy.start()
     where_ref[0] = core_ref[0]
+    where_ref[1] = half_ref[0]
     for copy in copies:
         copy.wait()
     fields = [in_ref[n].astype(F32) for n in (0, 1)]
@@ -143,7 +148,12 @@
     put_taps(tap_ref, 3, hidden_grad, 1)
     output = hidden + forward(1, w2_ref, 2)
     input_grad = hidden_grad + backward(3, w1_ref, 1) * slope_one
-    o_ref[...] = jnp.concatenate([pack(output), pack(input_grad)], axis=1).astype(BF16)
+    wide = jnp.concatenate([pack(output), pack(input_grad)], axis=1)
+    for t in range(6):
+        row_ref[t * 128 : t * 128 + 128, :] = wide[:, t * 128 : t * 128 + 128]
+    for e in range(8):
+        tiles = [row_ref[pl.ds(t * 128 + e, 16, stride=8), :] for t in range(6)]
+        o_ref[e * FIELD : (e + 1) * FIELD, :] = jnp.concatenate(tiles, axis=0).astype(BF16)
     for index, (act, grad) in enumerate(((act_two, g), (act_one, hidden_grad))):
         pair_ref[index, 0] = act[:, 0:128].astype(BF16)
         pair_ref[index, 1] = jnp.concatenate([act[:, 128:C], grad[:, 128:C]], axis=1).astype(BF16)
@@ -155,6 +165,10 @@
 
 def half_kernel(own, where_ref, pair_ref, *refs):
     o_ref, tap_ref, ft_ref = refs[-4:-1] if not own else refs[-3:]
+    if not own:
+        for c in range(16):
+            piece = refs[1][(c % 8) * FIELD : (c % 8 + 1) * FIELD, :].astype(F32)
+            refs[-1][c * BOTH + TERMS : (c + 1) * BOTH, :] = piece
     first, mixed, last = [pair_ref[n].astype(F32) for n in range(3)]
     turned = jnp.concatenate([first, mixed[:, 0:64]], axis=1).T
     grad = jnp.concatenate([last, mixed[:, 64:128]], axis=1)
@@ -185,7 +199,7 @@
             wg_ref = refs[-1]
             for q in range(3):
                 for u in range(6):
-                    wg_ref[pl.ds(t * 18 + q * 6 + u, 16, stride=TERMS), :] = lanes[q][
+                    wg_ref[pl.ds(t * 18 + q * 6 + u, 16, stride=BOTH), :] = lanes[q][
                         u * 16 : u * 16 + 16
                     ]
 
@@ -195,39 +209,38 @@
         o_ref[...] = refs[-1][...].astype(BF16)
 
 
-def join_kernel(s_ref, f_ref, out_ref, sum_ref, row_ref, part_ref):
-    part_ref[0 : 16 * TERMS, :] = s_ref[...].astype(F32)
-    part_ref[16 * TERMS : 16 * TERMS + 8, :] = jnp.zeros((8, 128), F32)
+def line_kernel(where_ref, s_ref, out_ref, part_ref, sum_ref, row_ref):
+    part_ref[0 : 16 * BOTH, :] = s_ref[...].astype(F32)
     total = part_ref[0:ROWS, :]
     for c in range(1, 16):
-        total = total + part_ref[c * TERMS : c * TERMS + ROWS, :]
-    sum_ref[0:ROWS, :] = total
-    sum_ref[ROWS : ROWS + 8, :] = jnp.zeros((8, 128), F32)
-    value = f_ref[...].astype(F32)
-    for t in range(6):
-        row_ref[pl.ds(t, 128, stride=12), :] = value[:, t * 128 : t * 128 + 128]
-    for x in range(4):
-        for yh in range(2):
-            t = x * 2 + yh
-            for zl in range(4):
-                first = t * 18 + zl * 6 if zl < 3 else 144 + t * 3
-                piece = sum_ref[first : first + 6, :]
-                for zh in range(4):
-                    start = ((zh * 4 + zl) * 8 + t) * 12 + 6
-                    row_ref[start : start + 6, :] = piece
+        total = total + part_ref[c * BOTH : c * BOTH + ROWS, :]
+    sum_ref[...] = total
+    for zl in range(4):
+        piece = sum_ref[zl * PIECE : zl * PIECE + PIECE + 1, :]
+        for zh in range(4):
+            start = (zh * 4 + zl) * LINE_ROWS + 48
+            row_ref[start : start + PIECE + 1, :] = piece
+    for half in (0, 1):
+
+        @pl.when(where_ref[1] == half)
+        def _():
+            for z in range(16):
+                for t in range(6):
+                    first = half * 8 * BOTH + TERMS + t * 16 + z
+                    row_ref[z * LINE_ROWS + t * 8 : z * LINE_ROWS + t * 8 + 8, :] = part_ref[
+                        pl.ds(first, 8, stride=BOTH), :
+                    ]
+
     out_ref[...] = row_ref[...].astype(BF16)
 
 
-def line_kernel(r_ref, z_ref, row_ref):
-    row_ref[...] = r_ref[...].astype(F32)
-    slots = []
-    for t in range(6, 12):
-        value = row_ref[pl.ds(t, 128, stride=12), :]
-        total = value[0:8]
-        for z in range(1, 16):
-            total = total + value[z * 8 : z * 8 + 8]
-        slots.append(total * (1.0 / 256.0))
-    mine = jnp.concatenate(slots, axis=0).astype(BF16)
+def sum_kernel(r_ref, z_ref, row_ref):
+    row_ref[0 : 16 * LINE_ROWS, :] = r_ref[...].astype(F32)
+    row_ref[16 * LINE_ROWS :, :] = jnp.zeros((8, 128), F32)
+    total = row_ref[48:96, :]
+    for z in range(1, 16):
+        total = total + row_ref[z * LINE_ROWS + 48 : z * LINE_ROWS + 96, :]
+    mine = (total * (1.0 / 256.0)).astype(BF16)
     for z in range(4):
         z_ref[z] = mine
 
@@ -235,26 +248,32 @@
 def tile_kernel(r_ref, out_ref, ig_ref, row_ref):
     row_ref[...] = r_ref[...].astype(F32)
     for f, ref in enumerate((out_ref, ig_ref)):
-        tiles = [row_ref[pl.ds(3 * f + t, 128, stride=12), :] for t in range(3)]
-        wide = jnp.concatenate(tiles, axis=1)
         halves = []
         for k in (0, 1):
-            part = wide[:, k * C : (k + 1) * C]
-            halves.append(jnp.concatenate([part[j * 8 : j * 8 + 8] for j in range(16)], axis=1))
+            parts = []
+            for z in range(16):
+                tiles = [
+                    row_ref[z * LINE_ROWS + (3 * f + t) * 8 : z * LINE_ROWS + (3 * f + t) * 8 + 8, :]
+                    for t in (k, k + 1)
+                ]
+                both = jnp.concatenate(tiles, axis=1)
+                parts.append(both[:, k * 64 : k * 64 + C])
+            halves.append(jnp.concatenate(parts, axis=1))
         ref[...] = jnp.concatenate(halves, axis=0).astype(BF16)
 
 
-def spread_kernel(z_ref, out_ref):
-    mine = jnp.concatenate([z_ref[0], z_ref[1], z_ref[2], z_ref[3, 0:32, :]], axis=0)
+def spread_kernel(z_ref, out_ref, row_ref):
+    for z in range(4):
+        row_ref[z * PIECE : z * PIECE + 48, :] = z_ref[z].astype(F32)
+    mine = row_ref[0:ROWS, :].astype(BF16)
     for c in range(16):
-        out_ref[c, 0:160, :] = mine[0:160]
-        out_ref[c, 160:168, :] = z_ref[3, 16:32, :][0:8]
+        out_ref[c] = mine
 
 
 def final_kernel(own, where_ref, r_ref, *refs):
     one_ref, two_ref, out_ref, scr_ref, sems = refs[-5:]
     for c in range(16):
-        scr_ref[c * PITCH : c * PITCH + ROWS, :] = r_ref[c].astype(F32)
+        scr_ref[c * ROWS : (c + 1) * ROWS, :] = r_ref[c].astype(F32)
     def each_copy(part, act):
         lanes = pl.ds(part * 9216, 9216)
         for core in (0, 1):
@@ -270,11 +289,9 @@
 
     for n in range(288):
         m, q = n // 3, n % 3
-        u, c = m // 16, m % 16
-        v = q * 6 + u
-        first = (c // 8) * 8 * PITCH + c % 8
-        eight = scr_ref[pl.ds(first + v * 8, 8, stride=PITCH), :]
-        last = first + (v // 3) * PITCH + (18 + v % 3) * 8
+        first = (m % 16) * ROWS + q * 6 + m // 16
+        eight = scr_ref[pl.ds(first, 8, stride=18), :]
+        last = first + 144
         nine = jnp.concatenate([eight, scr_ref[last : last + 1, :]], axis=0)
         out_ref[:, n * 128 : (n + 1) * 128] = nine.astype(BF16)
         if n % 72 == 71:
@@ -294,26 +311,27 @@
 def per_device(inputs, first_weight, second_weight, cotangent):
     smem, hbm, vmem = pltpu.SMEM, pltpu.HBM, pltpu.VMEM
     core = lax.axis_index("core").astype(jnp.int32).reshape(1)
+    half = lax.axis_index("yl").astype(jnp.int32).reshape(1)
     swap = [(0, 1), (1, 0)]
     short = pl.CostEstimate(flops=10**9, bytes_accessed=3 * 10**6, transcendentals=0)
     kernel_one = first_weight.reshape(9 * C, C)
     kernel_two = second_weight.reshape(9 * C, C)
     packed, where = call(
         pack_kernel,
-        (shape(768, 128), shape(1, dtype=jnp.int32)),
+        (shape(768, 128), shape(2, dtype=jnp.int32)),
         scratch=(
             vmem((2, 16, 16 * C), BF16),
             vmem((768, 128), F32),
             pltpu.SemaphoreType.DMA((2,)),
         ),
-        spaces={0: smem, 1: hbm, 2: hbm},
+        spaces={0: smem, 1: smem, 2: hbm, 3: hbm},
         out_specs=(pl.BlockSpec(memory_space=vmem), pl.BlockSpec(memory_space=smem)),
         limit=63400000,
-    )(core, inputs, cotangent)
+    )(core, half, inputs, cotangent)
     received = exchange(packed.reshape(384, 2, 128), PEERS).reshape(768, 128)
     fields, keep, send = call(
         main_kernel,
-        (shape(128, 768), shape(3, CELLS, 128), shape(3, CELLS, 128)),
+        (shape(8 * FIELD, 128), shape(3, CELLS, 128), shape(3, CELLS, 128)),
         scratch=(
             vmem((768, 128), F32),
             vmem((4, 3, CELLS + 2 * PAD, C), BF16),
@@ -332,35 +350,38 @@
     )(where, keep)
     terms = call(
         functools.partial(half_kernel, False),
-        shape(16 * TERMS, 128),
-        scratch=(*scratch, vmem((16 * TERMS, 128), F32)),
+        shape(16 * BOTH, 128),
+        scratch=(*scratch, vmem((16 * BOTH, 128), F32)),
         spaces={0: smem},
-    )(where, other, begun)
-    plane = exchange(terms.reshape(8 * TERMS, 2, 128), PLANE).reshape(16 * TERMS, 128)
-    joined = call(
-        join_kernel,
-        shape(1536, 128),
+    )(where, other, begun, fields)
+    plane = exchange(terms.reshape(8 * BOTH, 2, 128), PLANE).reshape(16 * BOTH, 128)
+    lines = call(
+        line_kernel,
+        shape(16 * LINE_ROWS, 128),
         scratch=(
-            vmem((ROWS + 8, 128), F32),
-            vmem((1536, 128), F32),
-            vmem((16 * TERMS + 8, 128), F32),
+            vmem((16 * BOTH, 128), F32),
+            vmem((ROWS, 128), F32),
+            vmem((16 * LINE_ROWS, 128), F32),
         ),
-    )(plane, fields)
-    back = exchange(joined.reshape(384, 4, 128), PEERS).reshape(1536, 128)
-    mine = call(line_kernel, shape(4, 48, 128), scratch=(vmem((1536, 128), F32),))(back)
+        spaces={0: smem},
+    )(where, plane)
+    back = exchange(lines.reshape(8 * LINE_ROWS, 2, 128), LINE).reshape(16 * LINE_ROWS, 128)
+    mine = call(sum_kernel, shape(4, 48, 128), scratch=(vmem((16 * LINE_ROWS + 8, 128), F32),))(back)
     line = exchange(mine, "zl")
-    spread = call(spread_kernel, shape(16, ROWS, 128))(line)
+    spread = call(
+        spread_kernel, shape(16, ROWS, 128), scratch=(vmem((3 * PIECE + 53, 128), F32),)
+    )(line)
     gathered = exchange(spread, PLANE)
     partner = lax.ppermute(gathered, "core", swap)
     output, input_grad = call(
         tile_kernel,
         (shape(16, 16 * C), shape(16, 16 * C)),
-        scratch=(vmem((1536, 128), F32),),
+        scratch=(vmem((16 * LINE_ROWS, 128), F32),),
         cost_estimate=short,
     )(back)
     weight = shape(9, C * C)
     anywhere = pl.BlockSpec(memory_space=pl.ANY)
-    scratch = (vmem((9, C * C), BF16), vmem((16 * PITCH, 128), F32), pltpu.SemaphoreType.DMA((4,)))
+    scratch = (vmem((9, C * C), BF16), vmem((16 * ROWS, 128), F32), pltpu.SemaphoreType.DMA((4,)))
     one, two = call(
         functools.partial(final_kernel, True),
         (weight, weight),

time: 139 us -> 134 us (0.964)
  blocking collectives: 72.8 us -> 68.4 us
    all_to_all x4, blocking collectives: 72.8 us -> 68.4 us  [exchange(): return lax.all_to_all(value, axes, split_axis=0, concat_axis=0, tiled=True)]
where the time goes in v7:
time: 134 us
  blocking collectives  68.4 us (51%)
  starting transfers between devices  36.1 us (27%)
  Pallas kernels  12.7 us (9%)
  waiting for transfers between devices  12.4 us (9%)
  local copies, waits for them, and re-layouts  3.29 us (2%)
    all_to_all x4, blocking collectives, exchange(): return lax.all_to_all(value, axes, split_axis=0, concat_axis=0, tiled=True)  68.4 us
    all_to_all x1, starting transfers between devices, exchange(): return lax.all_to_all(value, axes, split_axis=0, concat_axis=0, tiled=True)  23.1 us
    pallas_call x10, Pallas kernels, run(): pl.pallas_call(kernel, out_shape=out_shape, in_specs=[pl.BlockSpec(memory...  12.7 us
    all_to_all x1, waiting for transfers between devices, exchange(): return lax.all_to_all(value, axes, split_axis=0, concat_axis=0, tiled=True)  12.4 us
    ppermute x1, starting transfers between devices, per_device(): partner = lax.ppermute(gathered, 'core', swap)  6.95 us
    ppermute x1, starting transfers between devices, per_device(): other = lax.ppermute(send, 'core', swap)  6.02 us
  transfers between devices with their start and end apart: 3, of which 1 were waited for; matrix products, arithmetic and copies ran while one was open for 2% of the time, Pallas kernels for 3%

profile of v7, /device:TPU:1, one launch (start us, length us, event | category | flops | bytes accessed | tf_op | source)
XLA Modules:
  0.0 133.6 jit_solution(13333217486604022639)
XLA Ops:
  0.6 1.8 %shard_map.75 = (bf16[768,128]{1,0:T(8,128)(2,1)}, s32[2]{0:T(128)}) custom-call(s32[1]{0:T(128)} %bitcast.core_ref, s32[1]{0:T(128)} %bitcast.1.half_ref, bf16[16,3072]{1,0:T(8,128)(2,1)} %x_hbm.1, bf16[16,3072]{1,0:T(8,128)(2,1)} %g_hbm.1), custom_call_target="tpu_custom_call" | custom-call | tf_op jit(solution)/shard_map/pallas_call | solution.py:35
  2.4 0.0 copy-start.1
  2.4 23.1 %all-to-all-start = ((bf16[384,2,128]{2,1,0:T(2,128)(2,1)}), bf16[384,2,128]{2,1,0:T(2,128)(2,1)S(1)}, u32[]{:S(2)}, u32[]{:S(2)}) async-start(bf16[384,2,128]{2,1,0:T(2,128)(2,1)} %bitcast.14), calls=%async_computation | async-start | bytes 393216 | tf_op jit(solution)/shard_map/all_to_all | solution.py:304
  25.5 2.2 %reshape.42.w1_ref = bf16[1728,192]{1,0:T(8,128)(2,1)S(1)} reshape(bf16[9,36864]{1,0:T(8,128)(2,1)} %param.5) | data formatting | bytes 1327104 | tf_op jit(solution)/shard_map/reshape | solution.py:317
  27.7 0.0 copy-done.1
  27.7 0.0 copy-start
  27.7 1.1 reshape.43.w2_ref
  28.9 12.4 %all-to-all-done = bf16[384,2,128]{2,1,0:T(2,128)(2,1)S(1)} async-done(((bf16[384,2,128]{2,1,0:T(2,128)(2,1)}), bf16[384,2,128]{2,1,0:T(2,128)(2,1)S(1)}, u32[]{:S(2)}, u32[]{:S(2)}) %all-to-all-start) | async-done | bytes 196640 | tf_op jit(solution)/shard_map/all_to_all | solution.py:304
  41.3 0.0 copy-done
  41.3 3.1 %shard_map.76 = (bf16[768,128]{1,0:T(8,128)(2,1)S(1)}, bf16[3,256,128]{2,1,0:T(8,128)(2,1)S(1)}, bf16[3,256,128]{2,1,0:T(8,128)(2,1)S(1)}) custom-call(s32[2]{0:T(128)S(1)} %copy-done, bf16[768,128]{1,0:T(8,128)(2,1)S(1)} %bitcast.13, bf16[1728,192]{1,0:T(8,128)(2,1)S(1)} %reshape.42.w1_ref, bf16[1728,192]{1,0:T(8,128)(2,1)S(1)} %reshape.43.w2_ref), custom_call_target="tpu_custom_call" | custom-call | tf_op jit(solution)/shard_map/pallas_call | solution.py:35
  44.4 6.0 %collective-permute-start = (bf16[3,256,128]{2,1,0:T(8,128)(2,1)S(1)}, bf16[3,256,128]{2,1,0:T(8,128)(2,1)S(1)}, u32[]{:S(2)}, u32[]{:S(2)}) collective-permute-start(bf16[3,256,128]{2,1,0:T(8,128)(2,1)S(1)} %get-tuple-element.17), channel_id=1, source_target_pairs={{0,1},{1,0},{2,3},{3,2},{4,5},{5,4},{6,7},{7,6},{8,9},{9,8},{10,11... | collective-permute-start | bytes 589832 | tf_op jit(solution)/shard_map/ppermute | solution.py:342
  50.4 1.2 shard_map.77.refs_0_
  51.6 0.0 collective-permute-done.pair_ref
  51.7 1.4 %shard_map.78 = bf16[4128,128]{1,0:T(8,128)(2,1)S(1)} custom-call(s32[2]{0:T(128)S(1)} %copy-done, bf16[3,256,128]{2,1,0:T(8,128)(2,1)S(1)} %collective-permute-done.pair_ref, f32[9,192,192]{2,1,0:T(8,128)S(1)} %shard_map.77.refs_0_, bf16[768,128]{1,0:T(8,128)(2,1)S(1)} %get-tuple-element.19.refs_1_), custom_call_target="tpu_custom_call" | custom-call | tf_op jit(solution)/shard_map/pallas_call | solution.py:35
  53.1 23.0 %all_to_all.25 = bf16[2064,2,128]{2,1,0:T(2,128)(2,1)S(1)} all-to-all(bf16[2064,2,128]{2,1,0:T(2,128)(2,1)S(1)} %bitcast.9), channel_id=1, replica_groups=mesh['zl'=4,'yh'=2,'yl'=2,'x'=4,'zh'=4,'core'=2] {'yl','x','yh'}, dimensions={0} | all-to-all | bytes 2113536 | tf_op jit(solution)/shard_map/all_to_all | solution.py:304
  76.1 0.8 shard_map.79
  76.9 19.2 %all_to_all.26 = bf16[720,2,128]{2,1,0:T(2,128)(2,1)S(1)} all-to-all(bf16[720,2,128]{2,1,0:T(2,128)(2,1)S(1)} %bitcast.12), channel_id=1, replica_groups=mesh['zl'=4,'yh'=2,'yl'=2,'x'=4,'zh'=4,'core'=2] {'zh','zl'}, dimensions={0} | all-to-all | bytes 737280 | tf_op jit(solution)/shard_map/all_to_all | solution.py:304
  96.1 12.9 %all_to_all.27.z_ref = bf16[4,48,128]{2,1,0:T(8,128)(2,1)S(1)} all-to-all(bf16[4,48,128]{2,1,0:T(8,128)(2,1)S(1)} %shard_map.81), channel_id=1, replica_groups=mesh['zl'=4,'yh'=2,'yl'=2,'x'=4,'zh'=4,'core'=2] {'zl'}, dimensions={0} | all-to-all | bytes 98304 | tf_op jit(solution)/shard_map/all_to_all | solution.py:304
  109.1 0.1 shard_map.82
  109.1 13.3 %all_to_all.28.r_ref = bf16[16,168,128]{2,1,0:T(8,128)(2,1)S(1)} all-to-all(bf16[16,168,128]{2,1,0:T(8,128)(2,1)S(1)} %shard_map.82), channel_id=1, replica_groups=mesh['zl'=4,'yh'=2,'yl'=2,'x'=4,'zh'=4,'core'=2] {'yl','x','yh'}, dimensions={0} | all-to-all | bytes 1376256 | tf_op jit(solution)/shard_map/all_to_all | solution.py:304
  122.4 6.9 %collective-permute-start.1 = (bf16[16,168,128]{2,1,0:T(8,128)(2,1)S(1)}, bf16[16,168,128]{2,1,0:T(8,128)(2,1)S(1)}, u32[]{:S(2)}, u32[]{:S(2)}) collective-permute-start(bf16[16,168,128]{2,1,0:T(8,128)(2,1)S(1)} %all_to_all.28.r_ref), channel_id=1, source_target_pairs={{0,1},{1,0},{2,3},{3,2},{4,5},{5,4},{6,7},{7,6},{8,9},{9,8},{10,11... | collective-permute-start | bytes 2064392 | tf_op jit(solution)/shard_map/ppermute | solution.py:375
  129.4 0.8 shard_map.80
  130.1 1.7 %shard_map.83 = (bf16[9,36864]{1,0:T(8,128)(2,1)}, bf16[9,36864]{1,0:T(8,128)(2,1)}) custom-call(s32[2]{0:T(128)S(1)} %copy-done, bf16[16,168,128]{2,1,0:T(8,128)(2,1)S(1)} %all_to_all.28.r_ref), custom_call_target="tpu_custom_call" | custom-call | flops 1000000000 | bytes 3000000 | tf_op jit(solution)/shard_map/pallas_call | solution.py:35
  131.9 0.0 collective-permute-done.1.r_ref
  131.9 1.7 %shard_map.84 = (bf16[9,36864]{1,0:T(8,128)(2,1)}, bf16[9,36864]{1,0:T(8,128)(2,1)}) custom-call(s32[2]{0:T(128)S(1)} %copy-done, bf16[16,168,128]{2,1,0:T(8,128)(2,1)S(1)} %collective-permute-done.1.r_ref, bf16[9,36864]{1,0:T(8,128)(2,1)} %get-tuple-element.22.refs_0_, ...), custom_call_target="tpu_custom_call", output_to_operand_aliasing={{0}: (2, {}), {1}: (3, {})} | custom-call | tf_op jit(solution)/shard_map/pallas_call | solution.py:35
  (1 shorter events, 0.0 us)
Async XLA Ops:
  2.4 25.3 %copy-start.1 = (bf16[9,36864]{1,0:T(8,128)(2,1)S(1)}, bf16[9,36864]{1,0:T(8,128)(2,1)}, u32[]{:S(2)}) copy-start(bf16[9,36864]{1,0:T(8,128)(2,1)} %param.6) | copy-start | bytes 1990660
  2.4 38.8 %all-to-all-start = ((bf16[384,2,128]{2,1,0:T(2,128)(2,1)}), bf16[384,2,128]{2,1,0:T(2,128)(2,1)S(1)}, u32[]{:S(2)}, u32[]{:S(2)}) async-start(bf16[384,2,128]{2,1,0:T(2,128)(2,1)} %bitcast.14), calls=%async_computation | async-start | bytes 393216 | tf_op jit(solution)/shard_map/all_to_all | solution.py:304
  27.7 13.6 %copy-start = (s32[2]{0:T(128)S(1)}, s32[2]{0:T(128)}, u32[]{:S(2)}) copy-start(s32[2]{0:T(128)} %get-tuple-element.15.where_ref) | copy-start | bytes 28
  44.4 7.2 %collective-permute-start = (bf16[3,256,128]{2,1,0:T(8,128)(2,1)S(1)}, bf16[3,256,128]{2,1,0:T(8,128)(2,1)S(1)}, u32[]{:S(2)}, u32[]{:S(2)}) collective-permute-start(bf16[3,256,128]{2,1,0:T(8,128)(2,1)S(1)} %get-tuple-element.17), channel_id=1, source_target_pairs={{0,1},{1,0},{2,3},{3,2},{4,5},{5,4},{6,7},{7,6},{8,9},{9,8},{10,11... | collective-permute-start | bytes 589832 | tf_op jit(solution)/shard_map/ppermute | solution.py:342
  122.4 9.5 %collective-permute-start.1 = (bf16[16,168,128]{2,1,0:T(8,128)(2,1)S(1)}, bf16[16,168,128]{2,1,0:T(8,128)(2,1)S(1)}, u32[]{:S(2)}, u32[]{:S(2)}) collective-permute-start(bf16[16,168,128]{2,1,0:T(8,128)(2,1)S(1)} %all_to_all.28.r_ref), channel_id=1, source_target_pairs={{0,1},{1,0},{2,3},{3,2},{4,5},{5,4},{6,7},{7,6},{8,9},{9,8},{10,11... | collective-permute-start | bytes 2064392 | tf_op jit(solution)/shard_map/ppermute | solution.py:375

commit v8 on v7

--- a/solution.py
+++ b/solution.py
@@ -20,6 +20,7 @@
 FIELD = 96
 BOTH = TERMS + FIELD
 PIECE = 41
+WIDE = 21 * 128
 LINE_ROWS = 48 + PIECE + 1
 ZH = 64
 PAD = 2 * ZH
@@ -176,8 +177,9 @@
         ft_ref[n] = turned[:, n * 128 : n * 128 + 128]
     left = jnp.concatenate(
         [
-            jnp.concatenate([ft_ref[n, pl.ds(odd, 96, stride=2), :] for n in (0, 1)], axis=1)
+            jnp.concatenate([ft_ref[n, pl.ds(2 * u + odd, 16, stride=12), :] for n in (0, 1)], axis=1)
             for odd in (0, 1)
+            for u in range(6)
         ],
         axis=0,
     ).astype(BF16)
@@ -199,7 +201,7 @@
             wg_ref = refs[-1]
             for q in range(3):
                 for u in range(6):
-                    wg_ref[pl.ds(t * 18 + q * 6 + u, 16, stride=BOTH), :] = lanes[q][
+                    wg_ref[pl.ds(t * 18 + u * 3 + q, 16, stride=BOTH), :] = lanes[q][
                         u * 16 : u * 16 + 16
                     ]
 
@@ -265,15 +267,16 @@
 def spread_kernel(z_ref, out_ref, row_ref):
     for z in range(4):
         row_ref[z * PIECE : z * PIECE + 48, :] = z_ref[z].astype(F32)
-    mine = row_ref[0:ROWS, :].astype(BF16)
+    tiles = [row_ref[pl.ds(v, 8, stride=18), :] for v in range(18)]
+    tiles += [row_ref[v : v + 8, :] for v in (144, 152, 160)]
+    mine = jnp.concatenate(tiles, axis=1).astype(BF16)
     for c in range(16):
         out_ref[c] = mine
 
 
 def final_kernel(own, where_ref, r_ref, *refs):
-    one_ref, two_ref, out_ref, scr_ref, sems = refs[-5:]
-    for c in range(16):
-        scr_ref[c * ROWS : (c + 1) * ROWS, :] = r_ref[c].astype(F32)
+    one_ref, two_ref, out_ref, sems = refs[-4:]
+
     def each_copy(part, act):
         lanes = pl.ds(part * 9216, 9216)
         for core in (0, 1):
@@ -287,15 +290,15 @@
                     )
                 )
 
-    for n in range(288):
-        m, q = n // 3, n % 3
-        first = (m % 16) * ROWS + q * 6 + m // 16
-        eight = scr_ref[pl.ds(first, 8, stride=18), :]
-        last = first + 144
-        nine = jnp.concatenate([eight, scr_ref[last : last + 1, :]], axis=0)
-        out_ref[:, n * 128 : (n + 1) * 128] = nine.astype(BF16)
-        if n % 72 == 71:
-            each_copy(n // 72, lambda copy: copy.start())
+    for c in range(16):
+        lanes = c * 2304
+        out_ref[0:8, lanes : lanes + 2304] = r_ref[c, :, 0:2304]
+        last = r_ref[c, :, 2304:WIDE].astype(F32)
+        for v in range(18):
+            row = last[v % 8 : v % 8 + 1, v // 8 * 128 : v // 8 * 128 + 128]
+            out_ref[8:9, lanes + v * 128 : lanes + v * 128 + 128] = row.astype(BF16)
+        if c % 4 == 3:
+            each_copy(c // 4, lambda copy: copy.start())
     for part in range(4):
         each_copy(part, lambda copy: copy.wait())
 
@@ -369,7 +372,7 @@
     mine = call(sum_kernel, shape(4, 48, 128), scratch=(vmem((16 * LINE_ROWS + 8, 128), F32),))(back)
     line = exchange(mine, "zl")
     spread = call(
-        spread_kernel, shape(16, ROWS, 128), scratch=(vmem((3 * PIECE + 53, 128), F32),)
+        spread_kernel, shape(16, 8, WIDE), scratch=(vmem((3 * PIECE + 53, 128), F32),)
     )(line)
     gathered = exchange(spread, PLANE)
     partner = lax.ppermute(gathered, "core", swap)
@@ -381,7 +384,7 @@
     )(back)
     weight = shape(9, C * C)
     anywhere = pl.BlockSpec(memory_space=pl.ANY)
-    scratch = (vmem((9, C * C), BF16), vmem((16 * ROWS, 128), F32), pltpu.SemaphoreType.DMA((4,)))
+    scratch = (vmem((9, C * C), BF16), pltpu.SemaphoreType.DMA((4,)))
     one, two = call(
         functools.partial(final_kernel, True),
         (weight, weight),

time: 134 us -> 134 us (level)
  no operation moved by 1% of the time
where the time goes in v8:
time: 134 us; the launch traced here: 133 us
  blocking collectives  68.3 us (51%)
  starting transfers between devices  35.9 us (27%)
  Pallas kernels  12.5 us (9%)
  waiting for transfers between devices  12.4 us (9%)
  local copies, waits for them, and re-layouts  3.29 us (2%)
    all_to_all x4, blocking collectives, exchange(): return lax.all_to_all(value, axes, split_axis=0, concat_axis=0, tiled=True)  68.3 us
    all_to_all x1, starting transfers between devices, exchange(): return lax.all_to_all(value, axes, split_axis=0, concat_axis=0, tiled=True)  23.1 us
    pallas_call x10, Pallas kernels, run(): pl.pallas_call(kernel, out_shape=out_shape, in_specs=[pl.BlockSpec(memory...  12.5 us
    all_to_all x1, waiting for transfers between devices, exchange(): return lax.all_to_all(value, axes, split_axis=0, concat_axis=0, tiled=True)  12.4 us
    ppermute x1, starting transfers between devices, per_device(): partner = lax.ppermute(gathered, 'core', swap)  6.8 us
    ppermute x1, starting transfers between devices, per_device(): other = lax.ppermute(send, 'core', swap)  6.02 us
  transfers between devices with their start and end apart: 3, of which 1 were waited for; matrix products, arithmetic and copies ran while one was open for 2% of the time, Pallas kernels for 3%

profile of v8, /device:TPU:1, one launch (start us, length us, event | category | flops | bytes accessed | tf_op | source)
XLA Modules:
  0.0 133.2 jit_solution(17558243280986843198)
XLA Ops:
  0.6 1.8 %shard_map.75 = (bf16[768,128]{1,0:T(8,128)(2,1)}, s32[2]{0:T(128)}) custom-call(s32[1]{0:T(128)} %bitcast.core_ref, s32[1]{0:T(128)} %bitcast.1.half_ref, bf16[16,3072]{1,0:T(8,128)(2,1)} %x_hbm.1, bf16[16,3072]{1,0:T(8,128)(2,1)} %g_hbm.1), custom_call_target="tpu_custom_call" | custom-call | tf_op jit(solution)/shard_map/pallas_call | solution.py:36
  2.4 0.0 copy-start.1
  2.4 23.1 %all-to-all-start = ((bf16[384,2,128]{2,1,0:T(2,128)(2,1)}), bf16[384,2,128]{2,1,0:T(2,128)(2,1)S(1)}, u32[]{:S(2)}, u32[]{:S(2)}) async-start(bf16[384,2,128]{2,1,0:T(2,128)(2,1)} %bitcast.14), calls=%async_computation | async-start | bytes 393216 | tf_op jit(solution)/shard_map/all_to_all | solution.py:307
  25.5 2.2 %reshape.42.w1_ref = bf16[1728,192]{1,0:T(8,128)(2,1)S(1)} reshape(bf16[9,36864]{1,0:T(8,128)(2,1)} %param.5) | data formatting | bytes 1327104 | tf_op jit(solution)/shard_map/reshape | solution.py:320
  27.7 0.0 copy-done.1
  27.7 0.0 copy-start
  27.7 1.1 reshape.43.w2_ref
  28.9 12.4 %all-to-all-done = bf16[384,2,128]{2,1,0:T(2,128)(2,1)S(1)} async-done(((bf16[384,2,128]{2,1,0:T(2,128)(2,1)}), bf16[384,2,128]{2,1,0:T(2,128)(2,1)S(1)}, u32[]{:S(2)}, u32[]{:S(2)}) %all-to-all-start) | async-done | bytes 196640 | tf_op jit(solution)/shard_map/all_to_all | solution.py:307
  41.3 0.0 copy-done
  41.3 3.1 %shard_map.76 = (bf16[768,128]{1,0:T(8,128)(2,1)S(1)}, bf16[3,256,128]{2,1,0:T(8,128)(2,1)S(1)}, bf16[3,256,128]{2,1,0:T(8,128)(2,1)S(1)}) custom-call(s32[2]{0:T(128)S(1)} %copy-done, bf16[768,128]{1,0:T(8,128)(2,1)S(1)} %bitcast.13, bf16[1728,192]{1,0:T(8,128)(2,1)S(1)} %reshape.42.w1_ref, bf16[1728,192]{1,0:T(8,128)(2,1)S(1)} %reshape.43.w2_ref), custom_call_target="tpu_custom_call" | custom-call | tf_op jit(solution)/shard_map/pallas_call | solution.py:36
  44.4 6.0 %collective-permute-start = (bf16[3,256,128]{2,1,0:T(8,128)(2,1)S(1)}, bf16[3,256,128]{2,1,0:T(8,128)(2,1)S(1)}, u32[]{:S(2)}, u32[]{:S(2)}) collective-permute-start(bf16[3,256,128]{2,1,0:T(8,128)(2,1)S(1)} %get-tuple-element.17), channel_id=1, source_target_pairs={{0,1},{1,0},{2,3},{3,2},{4,5},{5,4},{6,7},{7,6},{8,9},{9,8},{10,11... | collective-permute-start | bytes 589832 | tf_op jit(solution)/shard_map/ppermute | solution.py:345
  50.4 1.2 shard_map.77.refs_0_
  51.6 0.0 collective-permute-done.pair_ref
  51.6 1.4 %shard_map.78 = bf16[4128,128]{1,0:T(8,128)(2,1)S(1)} custom-call(s32[2]{0:T(128)S(1)} %copy-done, bf16[3,256,128]{2,1,0:T(8,128)(2,1)S(1)} %collective-permute-done.pair_ref, f32[9,192,192]{2,1,0:T(8,128)S(1)} %shard_map.77.refs_0_, bf16[768,128]{1,0:T(8,128)(2,1)S(1)} %get-tuple-element.19.refs_1_), custom_call_target="tpu_custom_call" | custom-call | tf_op jit(solution)/shard_map/pallas_call | solution.py:36
  53.1 23.0 %all_to_all.25 = bf16[2064,2,128]{2,1,0:T(2,128)(2,1)S(1)} all-to-all(bf16[2064,2,128]{2,1,0:T(2,128)(2,1)S(1)} %bitcast.9), channel_id=1, replica_groups=mesh['zl'=4,'yh'=2,'yl'=2,'x'=4,'zh'=4,'core'=2] {'yl','x','yh'}, dimensions={0} | all-to-all | bytes 2113536 | tf_op jit(solution)/shard_map/all_to_all | solution.py:307
  76.1 0.8 shard_map.79
  76.9 19.2 %all_to_all.26 = bf16[720,2,128]{2,1,0:T(2,128)(2,1)S(1)} all-to-all(bf16[720,2,128]{2,1,0:T(2,128)(2,1)S(1)} %bitcast.12), channel_id=1, replica_groups=mesh['zl'=4,'yh'=2,'yl'=2,'x'=4,'zh'=4,'core'=2] {'zh','zl'}, dimensions={0} | all-to-all | bytes 737280 | tf_op jit(solution)/shard_map/all_to_all | solution.py:307
  96.1 13.0 %all_to_all.27.z_ref = bf16[4,48,128]{2,1,0:T(8,128)(2,1)S(1)} all-to-all(bf16[4,48,128]{2,1,0:T(8,128)(2,1)S(1)} %shard_map.81), channel_id=1, replica_groups=mesh['zl'=4,'yh'=2,'yl'=2,'x'=4,'zh'=4,'core'=2] {'zl'}, dimensions={0} | all-to-all | bytes 98304 | tf_op jit(solution)/shard_map/all_to_all | solution.py:307
  109.0 0.1 shard_map.82
  109.1 13.2 %all_to_all.28.r_ref = bf16[16,8,2688]{2,1,0:T(8,128)(2,1)S(1)} all-to-all(bf16[16,8,2688]{2,1,0:T(8,128)(2,1)S(1)} %shard_map.82), channel_id=1, replica_groups=mesh['zl'=4,'yh'=2,'yl'=2,'x'=4,'zh'=4,'core'=2] {'yl','x','yh'}, dimensions={0} | all-to-all | bytes 1376256 | tf_op jit(solution)/shard_map/all_to_all | solution.py:307
  122.3 6.8 %collective-permute-start.1 = (bf16[16,8,2688]{2,1,0:T(8,128)(2,1)S(1)}, bf16[16,8,2688]{2,1,0:T(8,128)(2,1)S(1)}, u32[]{:S(2)}, u32[]{:S(2)}) collective-permute-start(bf16[16,8,2688]{2,1,0:T(8,128)(2,1)S(1)} %all_to_all.28.r_ref), channel_id=1, source_target_pairs={{0,1},{1,0},{2,3},{3,2},{4,5},{5,4},{6,7},{7,6},{8,9},{9,8},{10,11... | collective-permute-start | bytes 2064392 | tf_op jit(solution)/shard_map/ppermute | solution.py:378
  129.1 0.8 shard_map.80
  129.9 1.6 %shard_map.83 = (bf16[9,36864]{1,0:T(8,128)(2,1)}, bf16[9,36864]{1,0:T(8,128)(2,1)}) custom-call(s32[2]{0:T(128)S(1)} %copy-done, bf16[16,8,2688]{2,1,0:T(8,128)(2,1)S(1)} %all_to_all.28.r_ref), custom_call_target="tpu_custom_call" | custom-call | flops 1000000000 | bytes 3000000 | tf_op jit(solution)/shard_map/pallas_call | solution.py:36
  131.5 0.0 collective-permute-done.1.r_ref
  131.6 1.6 %shard_map.84 = (bf16[9,36864]{1,0:T(8,128)(2,1)}, bf16[9,36864]{1,0:T(8,128)(2,1)}) custom-call(s32[2]{0:T(128)S(1)} %copy-done, bf16[16,8,2688]{2,1,0:T(8,128)(2,1)S(1)} %collective-permute-done.1.r_ref, bf16[9,36864]{1,0:T(8,128)(2,1)} %get-tuple-element.22.refs_0_, ...), custom_call_target="tpu_custom_call", output_to_operand_aliasing={{0}: (2, {}), {1}: (3, {})} | custom-call | tf_op jit(solution)/shard_map/pallas_call | solution.py:36
  (1 shorter events, 0.0 us)
Async XLA Ops:
  2.4 25.3 %copy-start.1 = (bf16[9,36864]{1,0:T(8,128)(2,1)S(1)}, bf16[9,36864]{1,0:T(8,128)(2,1)}, u32[]{:S(2)}) copy-start(bf16[9,36864]{1,0:T(8,128)(2,1)} %param.6) | copy-start | bytes 1990660
  2.4 38.8 %all-to-all-start = ((bf16[384,2,128]{2,1,0:T(2,128)(2,1)}), bf16[384,2,128]{2,1,0:T(2,128)(2,1)S(1)}, u32[]{:S(2)}, u32[]{:S(2)}) async-start(bf16[384,2,128]{2,1,0:T(2,128)(2,1)} %bitcast.14), calls=%async_computation | async-start | bytes 393216 | tf_op jit(solution)/shard_map/all_to_all | solution.py:307
  27.7 13.6 %copy-start = (s32[2]{0:T(128)S(1)}, s32[2]{0:T(128)}, u32[]{:S(2)}) copy-start(s32[2]{0:T(128)} %get-tuple-element.15.where_ref) | copy-start | bytes 28
  44.4 7.2 %collective-permute-start = (bf16[3,256,128]{2,1,0:T(8,128)(2,1)S(1)}, bf16[3,256,128]{2,1,0:T(8,128)(2,1)S(1)}, u32[]{:S(2)}, u32[]{:S(2)}) collective-permute-start(bf16[3,256,128]{2,1,0:T(8,128)(2,1)S(1)} %get-tuple-element.17), channel_id=1, source_target_pairs={{0,1},{1,0},{2,3},{3,2},{4,5},{5,4},{6,7},{7,6},{8,9},{9,8},{10,11... | collective-permute-start | bytes 589832 | tf_op jit(solution)/shard_map/ppermute | solution.py:345
  122.3 9.2 %collective-permute-start.1 = (bf16[16,8,2688]{2,1,0:T(8,128)(2,1)S(1)}, bf16[16,8,2688]{2,1,0:T(8,128)(2,1)S(1)}, u32[]{:S(2)}, u32[]{:S(2)}) collective-permute-start(bf16[16,8,2688]{2,1,0:T(8,128)(2,1)S(1)} %all_to_all.28.r_ref), channel_id=1, source_target_pairs={{0,1},{1,0},{2,3},{3,2},{4,5},{5,4},{6,7},{7,6},{8,9},{9,8},{10,11... | collective-permute-start | bytes 2064392 | tf_op jit(solution)/shard_map/ppermute | solution.py:378

commit v9 on v8

--- a/solution.py
+++ b/solution.py
@@ -54,12 +54,10 @@
     return value * normal_cdf, normal_cdf + value * density
 
 
-def pack_kernel(core_ref, half_ref, x_hbm, g_hbm, o_ref, where_ref, in_ref, row_ref, sems):
+def pack_kernel(x_hbm, g_hbm, o_ref, in_ref, row_ref, sems):
     copies = [pltpu.make_async_copy(h, in_ref.at[n], sems.at[n]) for n, h in enumerate((x_hbm, g_hbm))]
     for copy in copies:
         copy.start()
-    where_ref[0] = core_ref[0]
-    where_ref[1] = half_ref[0]
     for copy in copies:
         copy.wait()
     fields = [in_ref[n].astype(F32) for n in (0, 1)]
@@ -101,7 +99,7 @@
     return tap_ref[slot, a + 1, start : start + CELLS, :]
 
 
-def main_kernel(where_ref, r_ref, w1_ref, w2_ref, o_ref, keep_ref, send_ref, row_ref, tap_ref, pair_ref):
+def main_kernel(r_ref, w1_ref, w2_ref, o_ref, keep_ref, send_ref, row_ref, tap_ref, pair_ref):
     row_ref[...] = r_ref[...].astype(F32)
 
     def unpack(f):
@@ -159,12 +157,12 @@
         pair_ref[index, 0] = act[:, 0:128].astype(BF16)
         pair_ref[index, 1] = jnp.concatenate([act[:, 128:C], grad[:, 128:C]], axis=1).astype(BF16)
         pair_ref[index, 2] = grad[:, 0:128].astype(BF16)
-    core = where_ref[0]
+    core = lax.axis_index("core")
     keep_ref[...] = pair_ref[core]
     send_ref[...] = pair_ref[1 - core]
 
 
-def half_kernel(own, where_ref, pair_ref, *refs):
+def half_kernel(own, pair_ref, *refs):
     o_ref, tap_ref, ft_ref = refs[-4:-1] if not own else refs[-3:]
     if not own:
         for c in range(16):
@@ -206,12 +204,12 @@
                     ]
 
     for core, step in ((0, 2), (1, 1)):
-        pl.when(where_ref[0] == core)(lambda step=step: weight_grad(step))
+        pl.when(lax.axis_index("core") == core)(lambda step=step: weight_grad(step))
     if not own:
         o_ref[...] = refs[-1][...].astype(BF16)
 
 
-def line_kernel(where_ref, s_ref, out_ref, part_ref, sum_ref, row_ref):
+def line_kernel(s_ref, out_ref, part_ref, sum_ref, row_ref):
     part_ref[0 : 16 * BOTH, :] = s_ref[...].astype(F32)
     total = part_ref[0:ROWS, :]
     for c in range(1, 16):
@@ -224,7 +222,7 @@
             row_ref[start : start + PIECE + 1, :] = piece
     for half in (0, 1):
 
-        @pl.when(where_ref[1] == half)
+        @pl.when(lax.axis_index("yl") == half)
         def _():
             for z in range(16):
                 for t in range(6):
@@ -274,7 +272,7 @@
         out_ref[c] = mine
 
 
-def final_kernel(own, where_ref, r_ref, *refs):
+def final_kernel(own, r_ref, *refs):
     one_ref, two_ref, out_ref, sems = refs[-4:]
 
     def each_copy(part, act):
@@ -282,7 +280,7 @@
         for core in (0, 1):
             target = two_ref if (core == 0) == own else one_ref
 
-            @pl.when(where_ref[0] == core)
+            @pl.when(lax.axis_index("core") == core)
             def _(target=target):
                 act(
                     pltpu.make_async_copy(
@@ -312,25 +310,22 @@
 
 
 def per_device(inputs, first_weight, second_weight, cotangent):
-    smem, hbm, vmem = pltpu.SMEM, pltpu.HBM, pltpu.VMEM
-    core = lax.axis_index("core").astype(jnp.int32).reshape(1)
-    half = lax.axis_index("yl").astype(jnp.int32).reshape(1)
+    hbm, vmem = pltpu.HBM, pltpu.VMEM
     swap = [(0, 1), (1, 0)]
     short = pl.CostEstimate(flops=10**9, bytes_accessed=3 * 10**6, transcendentals=0)
     kernel_one = first_weight.reshape(9 * C, C)
     kernel_two = second_weight.reshape(9 * C, C)
-    packed, where = call(
+    packed = call(
         pack_kernel,
-        (shape(768, 128), shape(2, dtype=jnp.int32)),
+        shape(768, 128),
         scratch=(
             vmem((2, 16, 16 * C), BF16),
             vmem((768, 128), F32),
             pltpu.SemaphoreType.DMA((2,)),
         ),
-        spaces={0: smem, 1: smem, 2: hbm, 3: hbm},
-        out_specs=(pl.BlockSpec(memory_space=vmem), pl.BlockSpec(memory_space=smem)),
+        spaces={0: hbm, 1: hbm},
         limit=63400000,
-    )(core, half, inputs, cotangent)
+    )(inputs, cotangent)
     received = exchange(packed.reshape(384, 2, 128), PEERS).reshape(768, 128)
     fields, keep, send = call(
         main_kernel,
@@ -340,23 +335,20 @@
             vmem((4, 3, CELLS + 2 * PAD, C), BF16),
             vmem((2, 3, CELLS, 128), BF16),
         ),
-        spaces={0: smem},
-    )(where, received, kernel_one, kernel_two)
+    )(received, kernel_one, kernel_two)
     other = lax.ppermute(send, "core", swap)
     scratch = (vmem((1, 3, CELLS + 2 * PAD, C), BF16), vmem((2, C, 128), F32))
     begun = call(
         functools.partial(half_kernel, True),
         shape(9, C, C, dtype=F32),
         scratch=scratch,
-        spaces={0: smem},
         cost_estimate=short,
-    )(where, keep)
+    )(keep)
     terms = call(
         functools.partial(half_kernel, False),
         shape(16 * BOTH, 128),
         scratch=(*scratch, vmem((16 * BOTH, 128), F32)),
-        spaces={0: smem},
-    )(where, other, begun, fields)
+    )(other, begun, fields)
     plane = exchange(terms.reshape(8 * BOTH, 2, 128), PLANE).reshape(16 * BOTH, 128)
     lines = call(
         line_kernel,
@@ -366,8 +358,7 @@
             vmem((ROWS, 128), F32),
             vmem((16 * LINE_ROWS, 128), F32),
         ),
-        spaces={0: smem},
-    )(where, plane)
+    )(plane)
     back = exchange(lines.reshape(8 * LINE_ROWS, 2, 128), LINE).reshape(16 * LINE_ROWS, 128)
     mine = call(sum_kernel, shape(4, 48, 128), scratch=(vmem((16 * LINE_ROWS + 8, 128), F32),))(back)
     line = exchange(mine, "zl")
@@ -389,18 +380,17 @@
         functools.partial(final_kernel, True),
         (weight, weight),
         scratch=scratch,
-        spaces={0: smem},
         out_specs=(anywhere, anywhere),
         cost_estimate=short,
-    )(where, gathered)
+    )(gathered)
     one, two = call(
         functools.partial(final_kernel, False),
         (weight, weight),
         scratch=scratch,
-        spaces={0: smem, 2: pl.ANY, 3: pl.ANY},
+        spaces={1: pl.ANY, 2: pl.ANY},
         out_specs=(anywhere, anywhere),
-        input_output_aliases={2: 0, 3: 1},
-    )(where, partner, one, two)
+        input_output_aliases={1: 0, 2: 1},
+    )(partner, one, two)
     return output, input_grad, one, two
 
 

time: 134 us -> 131 us (0.978)
  Pallas kernels: 12.5 us -> 9.2 us
    pallas_call x10, Pallas kernels: 12.5 us -> 9.2 us  [run(): pl.pallas_call(kernel, out_shape=out_shape, in_specs=[pl.BlockSpec(memory...]
  transfers between devices with their start and end apart: 3 -> 3, of which waited for: 1 -> 2; matrix products, arithmetic and copies ran while one was open for 2% -> 3% of each run, Pallas kernels for 3% -> 2%
where the time goes in v9:
time: 131 us; the launch traced here: 130 us
  blocking collectives  68.2 us (52%)
  starting transfers between devices  35.9 us (27%)
  waiting for transfers between devices  12.8 us (10%)
  Pallas kernels  9.2 us (7%)
  local copies, waits for them, and re-layouts  3.28 us (3%)
    all_to_all x4, blocking collectives, exchange(): return lax.all_to_all(value, axes, split_axis=0, concat_axis=0, tiled=True)  68.2 us
    all_to_all x1, starting transfers between devices, exchange(): return lax.all_to_all(value, axes, split_axis=0, concat_axis=0, tiled=True)  23.1 us
    all_to_all x1, waiting for transfers between devices, exchange(): return lax.all_to_all(value, axes, split_axis=0, concat_axis=0, tiled=True)  12.4 us
    pallas_call x10, Pallas kernels, run(): pl.pallas_call(kernel, out_shape=out_shape, in_specs=[pl.BlockSpec(memory...  9.2 us
    ppermute x1, starting transfers between devices, per_device(): partner = lax.ppermute(gathered, 'core', swap)  6.8 us
    ppermute x1, starting transfers between devices, per_device(): other = lax.ppermute(send, 'core', swap)  6.02 us
  transfers between devices with their start and end apart: 3, of which 2 were waited for; matrix products, arithmetic and copies ran while one was open for 3% of the time, Pallas kernels for 2%

profile of v9, /device:TPU:1, one launch (start us, length us, event | category | flops | bytes accessed | tf_op | source)
XLA Modules:
  0.0 130.2 jit_solution(16627266144503200726)
XLA Ops:
  0.6 1.8 %shard_map.75 = bf16[768,128]{1,0:T(8,128)(2,1)} custom-call(bf16[16,3072]{1,0:T(8,128)(2,1)} %x_hbm.1, bf16[16,3072]{1,0:T(8,128)(2,1)} %g_hbm.1), custom_call_target="tpu_custom_call" | custom-call | tf_op jit(solution)/shard_map/pallas_call | solution.py:36
  2.4 0.0 copy-start
  2.4 23.1 %all-to-all-start = ((bf16[384,2,128]{2,1,0:T(2,128)(2,1)}), bf16[384,2,128]{2,1,0:T(2,128)(2,1)S(1)}, u32[]{:S(2)}, u32[]{:S(2)}) async-start(bf16[384,2,128]{2,1,0:T(2,128)(2,1)} %bitcast.12), calls=%async_computation | async-start | bytes 393216 | tf_op jit(solution)/shard_map/all_to_all | solution.py:305
  25.5 2.2 %reshape.34.w1_ref = bf16[1728,192]{1,0:T(8,128)(2,1)S(1)} reshape(bf16[9,36864]{1,0:T(8,128)(2,1)} %param.5) | data formatting | bytes 1327104 | tf_op jit(solution)/shard_map/reshape | solution.py:316
  27.7 0.0 copy-done
  27.7 1.1 reshape.35.w2_ref
  28.8 12.4 %all-to-all-done = bf16[384,2,128]{2,1,0:T(2,128)(2,1)S(1)} async-done(((bf16[384,2,128]{2,1,0:T(2,128)(2,1)}), bf16[384,2,128]{2,1,0:T(2,128)(2,1)S(1)}, u32[]{:S(2)}, u32[]{:S(2)}) %all-to-all-start) | async-done | bytes 196640 | tf_op jit(solution)/shard_map/all_to_all | solution.py:305
  41.3 2.6 %shard_map.76 = (bf16[768,128]{1,0:T(8,128)(2,1)S(1)}, bf16[3,256,128]{2,1,0:T(8,128)(2,1)S(1)}, bf16[3,256,128]{2,1,0:T(8,128)(2,1)S(1)}) custom-call(bf16[768,128]{1,0:T(8,128)(2,1)S(1)} %bitcast.11, bf16[1728,192]{1,0:T(8,128)(2,1)S(1)} %reshape.34.w1_ref, bf16[1728,192]{1,0:T(8,128)(2,1)S(1)} %reshape.35.w2_ref), custom_call_target="tpu_custom_call" | custom-call | tf_op jit(solution)/shard_map/pallas_call | solution.py:36
  43.8 6.0 %collective-permute-start = (bf16[3,256,128]{2,1,0:T(8,128)(2,1)S(1)}, bf16[3,256,128]{2,1,0:T(8,128)(2,1)S(1)}, u32[]{:S(2)}, u32[]{:S(2)}) collective-permute-start(bf16[3,256,128]{2,1,0:T(8,128)(2,1)S(1)} %get-tuple-element.13), channel_id=1, source_target_pairs={{0,1},{1,0},{2,3},{3,2},{4,5},{5,4},{6,7},{7,6},{8,9},{9,8},{10,11... | collective-permute-start | bytes 589832 | tf_op jit(solution)/shard_map/ppermute | solution.py:339
  49.9 0.7 shard_map.77.refs_0_
  50.5 0.4 collective-permute-done.pair_ref
  50.9 0.9 shard_map.78
  51.8 22.8 %all_to_all.25 = bf16[2064,2,128]{2,1,0:T(2,128)(2,1)S(1)} all-to-all(bf16[2064,2,128]{2,1,0:T(2,128)(2,1)S(1)} %bitcast.6), channel_id=1, replica_groups=mesh['zl'=4,'yh'=2,'yl'=2,'x'=4,'zh'=4,'core'=2] {'yl','x','yh'}, dimensions={0} | all-to-all | bytes 2113536 | tf_op jit(solution)/shard_map/all_to_all | solution.py:305
  74.6 0.3 shard_map.79
  74.9 18.3 %all_to_all.26 = bf16[720,2,128]{2,1,0:T(2,128)(2,1)S(1)} all-to-all(bf16[720,2,128]{2,1,0:T(2,128)(2,1)S(1)} %bitcast.10), channel_id=1, replica_groups=mesh['zl'=4,'yh'=2,'yl'=2,'x'=4,'zh'=4,'core'=2] {'zh','zl'}, dimensions={0} | all-to-all | bytes 737280 | tf_op jit(solution)/shard_map/all_to_all | solution.py:305
  93.2 13.7 %all_to_all.27.z_ref = bf16[4,48,128]{2,1,0:T(8,128)(2,1)S(1)} all-to-all(bf16[4,48,128]{2,1,0:T(8,128)(2,1)S(1)} %shard_map.81), channel_id=1, replica_groups=mesh['zl'=4,'yh'=2,'yl'=2,'x'=4,'zh'=4,'core'=2] {'zl'}, dimensions={0} | all-to-all | bytes 98304 | tf_op jit(solution)/shard_map/all_to_all | solution.py:305
  106.9 0.1 shard_map.82
  107.0 13.4 %all_to_all.28.r_ref = bf16[16,8,2688]{2,1,0:T(8,128)(2,1)S(1)} all-to-all(bf16[16,8,2688]{2,1,0:T(8,128)(2,1)S(1)} %shard_map.82), channel_id=1, replica_groups=mesh['zl'=4,'yh'=2,'yl'=2,'x'=4,'zh'=4,'core'=2] {'yl','x','yh'}, dimensions={0} | all-to-all | bytes 1376256 | tf_op jit(solution)/shard_map/all_to_all | solution.py:305
  120.4 6.8 %collective-permute-start.1 = (bf16[16,8,2688]{2,1,0:T(8,128)(2,1)S(1)}, bf16[16,8,2688]{2,1,0:T(8,128)(2,1)S(1)}, u32[]{:S(2)}, u32[]{:S(2)}) collective-permute-start(bf16[16,8,2688]{2,1,0:T(8,128)(2,1)S(1)} %all_to_all.28.r_ref), channel_id=1, source_target_pairs={{0,1},{1,0},{2,3},{3,2},{4,5},{5,4},{6,7},{7,6},{8,9},{9,8},{10,11... | collective-permute-start | bytes 2064392 | tf_op jit(solution)/shard_map/ppermute | solution.py:369
  127.2 0.8 shard_map.80
  128.0 1.1 shard_map.83
  129.1 0.0 collective-permute-done.1.r_ref
  129.1 1.1 shard_map.84
  (1 shorter events, 0.0 us)
Async XLA Ops:
  2.4 25.3 %copy-start = (bf16[9,36864]{1,0:T(8,128)(2,1)S(1)}, bf16[9,36864]{1,0:T(8,128)(2,1)}, u32[]{:S(2)}) copy-start(bf16[9,36864]{1,0:T(8,128)(2,1)} %param.6) | copy-start | bytes 1990660
  2.4 38.8 %all-to-all-start = ((bf16[384,2,128]{2,1,0:T(2,128)(2,1)}), bf16[384,2,128]{2,1,0:T(2,128)(2,1)S(1)}, u32[]{:S(2)}, u32[]{:S(2)}) async-start(bf16[384,2,128]{2,1,0:T(2,128)(2,1)} %bitcast.12), calls=%async_computation | async-start | bytes 393216 | tf_op jit(solution)/shard_map/all_to_all | solution.py:305
  43.8 7.1 %collective-permute-start = (bf16[3,256,128]{2,1,0:T(8,128)(2,1)S(1)}, bf16[3,256,128]{2,1,0:T(8,128)(2,1)S(1)}, u32[]{:S(2)}, u32[]{:S(2)}) collective-permute-start(bf16[3,256,128]{2,1,0:T(8,128)(2,1)S(1)} %get-tuple-element.13), channel_id=1, source_target_pairs={{0,1},{1,0},{2,3},{3,2},{4,5},{5,4},{6,7},{7,6},{8,9},{9,8},{10,11... | collective-permute-start | bytes 589832 | tf_op jit(solution)/shard_map/ppermute | solution.py:339
  120.4 8.7 %collective-permute-start.1 = (bf16[16,8,2688]{2,1,0:T(8,128)(2,1)S(1)}, bf16[16,8,2688]{2,1,0:T(8,128)(2,1)S(1)}, u32[]{:S(2)}, u32[]{:S(2)}) collective-permute-start(bf16[16,8,2688]{2,1,0:T(8,128)(2,1)S(1)} %all_to_all.28.r_ref), channel_id=1, source_target_pairs={{0,1},{1,0},{2,3},{3,2},{4,5},{5,4},{6,7},{7,6},{8,9},{9,8},{10,11... | collective-permute-start | bytes 2064392 | tf_op jit(solution)/shard_map/ppermute | solution.py:369

commit v10 on v9

--- a/solution.py
+++ b/solution.py
@@ -206,7 +206,7 @@
     for core, step in ((0, 2), (1, 1)):
         pl.when(lax.axis_index("core") == core)(lambda step=step: weight_grad(step))
     if not own:
-        o_ref[...] = refs[-1][...].astype(BF16)
+        o_ref[...] = refs[-1][0 : 16 * BOTH, :].astype(BF16)
 
 
 def line_kernel(s_ref, out_ref, part_ref, sum_ref, row_ref):
@@ -214,7 +214,8 @@
     total = part_ref[0:ROWS, :]
     for c in range(1, 16):
         total = total + part_ref[c * BOTH : c * BOTH + ROWS, :]
-    sum_ref[...] = total
+    sum_ref[0:ROWS, :] = total
+    sum_ref[ROWS : ROWS + 16, :] = jnp.zeros((16, 128), F32)
     for zl in range(4):
         piece = sum_ref[zl * PIECE : zl * PIECE + PIECE + 1, :]
         for zh in range(4):
@@ -231,12 +232,12 @@
                         pl.ds(first, 8, stride=BOTH), :
                     ]
 
-    out_ref[...] = row_ref[...].astype(BF16)
+    out_ref[...] = row_ref[0 : 16 * LINE_ROWS, :].astype(BF16)
 
 
 def sum_kernel(r_ref, z_ref, row_ref):
     row_ref[0 : 16 * LINE_ROWS, :] = r_ref[...].astype(F32)
-    row_ref[16 * LINE_ROWS :, :] = jnp.zeros((8, 128), F32)
+    row_ref[16 * LINE_ROWS :, :] = jnp.zeros((16, 128), F32)
     total = row_ref[48:96, :]
     for z in range(1, 16):
         total = total + row_ref[z * LINE_ROWS + 48 : z * LINE_ROWS + 96, :]
@@ -347,23 +348,23 @@
     terms = call(
         functools.partial(half_kernel, False),
         shape(16 * BOTH, 128),
-        scratch=(*scratch, vmem((16 * BOTH, 128), F32)),
+        scratch=(*scratch, vmem((16 * BOTH + 8, 128), F32)),
     )(other, begun, fields)
     plane = exchange(terms.reshape(8 * BOTH, 2, 128), PLANE).reshape(16 * BOTH, 128)
     lines = call(
         line_kernel,
         shape(16 * LINE_ROWS, 128),
         scratch=(
-            vmem((16 * BOTH, 128), F32),
-            vmem((ROWS, 128), F32),
-            vmem((16 * LINE_ROWS, 128), F32),
+            vmem((16 * BOTH + 8, 128), F32),
+            vmem((ROWS + 16, 128), F32),
+            vmem((16 * LINE_ROWS + 8, 128), F32),
         ),
     )(plane)
     back = exchange(lines.reshape(8 * LINE_ROWS, 2, 128), LINE).reshape(16 * LINE_ROWS, 128)
-    mine = call(sum_kernel, shape(4, 48, 128), scratch=(vmem((16 * LINE_ROWS + 8, 128), F32),))(back)
+    mine = call(sum_kernel, shape(4, 48, 128), scratch=(vmem((16 * LINE_ROWS + 16, 128), F32),))(back)
     line = exchange(mine, "zl")
     spread = call(
-        spread_kernel, shape(16, 8, WIDE), scratch=(vmem((3 * PIECE + 53, 128), F32),)
+        spread_kernel, shape(16, 8, WIDE), scratch=(vmem((3 * PIECE + 61, 128), F32),)
     )(line)
     gathered = exchange(spread, PLANE)
     partner = lax.ppermute(gathered, "core", swap)

time: 131 us -> 131 us (level)
  no operation moved by 1% of the time
where the time goes in v10:
time: 131 us; the launch traced here: 130 us
  blocking collectives  68.2 us (52%)
  starting transfers between devices  35.9 us (27%)
  waiting for transfers between devices  12.8 us (10%)
  Pallas kernels  9.21 us (7%)
  local copies, waits for them, and re-layouts  3.28 us (3%)
    all_to_all x4, blocking collectives, exchange(): return lax.all_to_all(value, axes, split_axis=0, concat_axis=0, tiled=True)  68.2 us
    all_to_all x1, starting transfers between devices, exchange(): return lax.all_to_all(value, axes, split_axis=0, concat_axis=0, tiled=True)  23.1 us
    all_to_all x1, waiting for transfers between devices, exchange(): return lax.all_to_all(value, axes, split_axis=0, concat_axis=0, tiled=True)  12.4 us
    pallas_call x10, Pallas kernels, run(): pl.pallas_call(kernel, out_shape=out_shape, in_specs=[pl.BlockSpec(memory...  9.21 us
    ppermute x1, starting transfers between devices, per_device(): partner = lax.ppermute(gathered, 'core', swap)  6.8 us
    ppermute x1, starting transfers between devices, per_device(): other = lax.ppermute(send, 'core', swap)  6.02 us
  transfers between devices with their start and end apart: 3, of which 2 were waited for; matrix products, arithmetic and copies ran while one was open for 3% of the time, Pallas kernels for 2%

profile of v10, /device:TPU:1, one launch (start us, length us, event | category | flops | bytes accessed | tf_op | source)
XLA Modules:
  0.0 130.2 jit_solution(2522458436299122466)
XLA Ops:
  0.6 1.8 %shard_map.75 = bf16[768,128]{1,0:T(8,128)(2,1)} custom-call(bf16[16,3072]{1,0:T(8,128)(2,1)} %x_hbm.1, bf16[16,3072]{1,0:T(8,128)(2,1)} %g_hbm.1), custom_call_target="tpu_custom_call" | custom-call | tf_op jit(solution)/shard_map/pallas_call | solution.py:36
  2.4 0.0 copy-start
  2.4 23.1 %all-to-all-start = ((bf16[384,2,128]{2,1,0:T(2,128)(2,1)}), bf16[384,2,128]{2,1,0:T(2,128)(2,1)S(1)}, u32[]{:S(2)}, u32[]{:S(2)}) async-start(bf16[384,2,128]{2,1,0:T(2,128)(2,1)} %bitcast.12), calls=%async_computation | async-start | bytes 393216 | tf_op jit(solution)/shard_map/all_to_all | solution.py:306
  25.5 2.2 %reshape.34.w1_ref = bf16[1728,192]{1,0:T(8,128)(2,1)S(1)} reshape(bf16[9,36864]{1,0:T(8,128)(2,1)} %param.5) | data formatting | bytes 1327104 | tf_op jit(solution)/shard_map/reshape | solution.py:317
  27.7 0.0 copy-done
  27.7 1.1 reshape.35.w2_ref
  28.8 12.4 %all-to-all-done = bf16[384,2,128]{2,1,0:T(2,128)(2,1)S(1)} async-done(((bf16[384,2,128]{2,1,0:T(2,128)(2,1)}), bf16[384,2,128]{2,1,0:T(2,128)(2,1)S(1)}, u32[]{:S(2)}, u32[]{:S(2)}) %all-to-all-start) | async-done | bytes 196640 | tf_op jit(solution)/shard_map/all_to_all | solution.py:306
  41.3 2.6 %shard_map.76 = (bf16[768,128]{1,0:T(8,128)(2,1)S(1)}, bf16[3,256,128]{2,1,0:T(8,128)(2,1)S(1)}, bf16[3,256,128]{2,1,0:T(8,128)(2,1)S(1)}) custom-call(bf16[768,128]{1,0:T(8,128)(2,1)S(1)} %bitcast.11, bf16[1728,192]{1,0:T(8,128)(2,1)S(1)} %reshape.34.w1_ref, bf16[1728,192]{1,0:T(8,128)(2,1)S(1)} %reshape.35.w2_ref), custom_call_target="tpu_custom_call" | custom-call | tf_op jit(solution)/shard_map/pallas_call | solution.py:36
  43.8 6.0 %collective-permute-start = (bf16[3,256,128]{2,1,0:T(8,128)(2,1)S(1)}, bf16[3,256,128]{2,1,0:T(8,128)(2,1)S(1)}, u32[]{:S(2)}, u32[]{:S(2)}) collective-permute-start(bf16[3,256,128]{2,1,0:T(8,128)(2,1)S(1)} %get-tuple-element.13), channel_id=1, source_target_pairs={{0,1},{1,0},{2,3},{3,2},{4,5},{5,4},{6,7},{7,6},{8,9},{9,8},{10,11... | collective-permute-start | bytes 589832 | tf_op jit(solution)/shard_map/ppermute | solution.py:340
  49.9 0.7 shard_map.77.refs_0_
  50.5 0.4 collective-permute-done.pair_ref
  50.9 0.9 shard_map.78
  51.8 22.8 %all_to_all.25 = bf16[2064,2,128]{2,1,0:T(2,128)(2,1)S(1)} all-to-all(bf16[2064,2,128]{2,1,0:T(2,128)(2,1)S(1)} %bitcast.6), channel_id=1, replica_groups=mesh['zl'=4,'yh'=2,'yl'=2,'x'=4,'zh'=4,'core'=2] {'yl','x','yh'}, dimensions={0} | all-to-all | bytes 2113536 | tf_op jit(solution)/shard_map/all_to_all | solution.py:306
  74.6 0.3 shard_map.79
  74.9 18.3 %all_to_all.26 = bf16[720,2,128]{2,1,0:T(2,128)(2,1)S(1)} all-to-all(bf16[720,2,128]{2,1,0:T(2,128)(2,1)S(1)} %bitcast.10), channel_id=1, replica_groups=mesh['zl'=4,'yh'=2,'yl'=2,'x'=4,'zh'=4,'core'=2] {'zh','zl'}, dimensions={0} | all-to-all | bytes 737280 | tf_op jit(solution)/shard_map/all_to_all | solution.py:306
  93.2 13.7 %all_to_all.27.z_ref = bf16[4,48,128]{2,1,0:T(8,128)(2,1)S(1)} all-to-all(bf16[4,48,128]{2,1,0:T(8,128)(2,1)S(1)} %shard_map.81), channel_id=1, replica_groups=mesh['zl'=4,'yh'=2,'yl'=2,'x'=4,'zh'=4,'core'=2] {'zl'}, dimensions={0} | all-to-all | bytes 98304 | tf_op jit(solution)/shard_map/all_to_all | solution.py:306
  106.9 0.1 shard_map.82
  107.0 13.4 %all_to_all.28.r_ref = bf16[16,8,2688]{2,1,0:T(8,128)(2,1)S(1)} all-to-all(bf16[16,8,2688]{2,1,0:T(8,128)(2,1)S(1)} %shard_map.82), channel_id=1, replica_groups=mesh['zl'=4,'yh'=2,'yl'=2,'x'=4,'zh'=4,'core'=2] {'yl','x','yh'}, dimensions={0} | all-to-all | bytes 1376256 | tf_op jit(solution)/shard_map/all_to_all | solution.py:306
  120.4 6.8 %collective-permute-start.1 = (bf16[16,8,2688]{2,1,0:T(8,128)(2,1)S(1)}, bf16[16,8,2688]{2,1,0:T(8,128)(2,1)S(1)}, u32[]{:S(2)}, u32[]{:S(2)}) collective-permute-start(bf16[16,8,2688]{2,1,0:T(8,128)(2,1)S(1)} %all_to_all.28.r_ref), channel_id=1, source_target_pairs={{0,1},{1,0},{2,3},{3,2},{4,5},{5,4},{6,7},{7,6},{8,9},{9,8},{10,11... | collective-permute-start | bytes 2064392 | tf_op jit(solution)/shard_map/ppermute | solution.py:370
  127.2 0.8 shard_map.80
  128.0 1.1 shard_map.83
  129.1 0.0 collective-permute-done.1.r_ref
  129.1 1.1 shard_map.84
  (1 shorter events, 0.0 us)
Async XLA Ops:
  2.4 25.3 %copy-start = (bf16[9,36864]{1,0:T(8,128)(2,1)S(1)}, bf16[9,36864]{1,0:T(8,128)(2,1)}, u32[]{:S(2)}) copy-start(bf16[9,36864]{1,0:T(8,128)(2,1)} %param.6) | copy-start | bytes 1990660
  2.4 38.8 %all-to-all-start = ((bf16[384,2,128]{2,1,0:T(2,128)(2,1)}), bf16[384,2,128]{2,1,0:T(2,128)(2,1)S(1)}, u32[]{:S(2)}, u32[]{:S(2)}) async-start(bf16[384,2,128]{2,1,0:T(2,128)(2,1)} %bitcast.12), calls=%async_computation | async-start | bytes 393216 | tf_op jit(solution)/shard_map/all_to_all | solution.py:306
  43.8 7.1 %collective-permute-start = (bf16[3,256,128]{2,1,0:T(8,128)(2,1)S(1)}, bf16[3,256,128]{2,1,0:T(8,128)(2,1)S(1)}, u32[]{:S(2)}, u32[]{:S(2)}) collective-permute-start(bf16[3,256,128]{2,1,0:T(8,128)(2,1)S(1)} %get-tuple-element.13), channel_id=1, source_target_pairs={{0,1},{1,0},{2,3},{3,2},{4,5},{5,4},{6,7},{7,6},{8,9},{9,8},{10,11... | collective-permute-start | bytes 589832 | tf_op jit(solution)/shard_map/ppermute | solution.py:340
  120.4 8.7 %collective-permute-start.1 = (bf16[16,8,2688]{2,1,0:T(8,128)(2,1)S(1)}, bf16[16,8,2688]{2,1,0:T(8,128)(2,1)S(1)}, u32[]{:S(2)}, u32[]{:S(2)}) collective-permute-start(bf16[16,8,2688]{2,1,0:T(8,128)(2,1)S(1)} %all_to_all.28.r_ref), channel_id=1, source_target_pairs={{0,1},{1,0},{2,3},{3,2},{4,5},{5,4},{6,7},{7,6},{8,9},{9,8},{10,11... | collective-permute-start | bytes 2064392 | tf_op jit(solution)/shard_map/ppermute | solution.py:370

commit v11 on v10

--- a/solution.py
+++ b/solution.py
@@ -11,7 +11,7 @@
 AXES = ("zl", "yh", "yl", "x", "zh", "core")
 SIZES = (4, 2, 2, 4, 4, 2)
 PEERS = ("zh", "zl", "x", "yh")
-PLANE = ("yl", "x", "yh")
+PLANE = ("x", "yh", "yl")
 LINE = ("zh", "zl")
 BF16 = jnp.bfloat16
 F32 = jnp.float32
@@ -166,7 +166,7 @@
     o_ref, tap_ref, ft_ref = refs[-4:-1] if not own else refs[-3:]
     if not own:
         for c in range(16):
-            piece = refs[1][(c % 8) * FIELD : (c % 8 + 1) * FIELD, :].astype(F32)
+            piece = refs[1][(c // 2) * FIELD : (c // 2 + 1) * FIELD, :].astype(F32)
             refs[-1][c * BOTH + TERMS : (c + 1) * BOTH, :] = piece
     first, mixed, last = [pair_ref[n].astype(F32) for n in range(3)]
     turned = jnp.concatenate([first, mixed[:, 0:64]], axis=1).T
@@ -227,9 +227,9 @@
         def _():
             for z in range(16):
                 for t in range(6):
-                    first = half * 8 * BOTH + TERMS + t * 16 + z
+                    first = half * BOTH + TERMS + t * 16 + z
                     row_ref[z * LINE_ROWS + t * 8 : z * LINE_ROWS + t * 8 + 8, :] = part_ref[
-                        pl.ds(first, 8, stride=BOTH), :
+                        pl.ds(first, 8, stride=2 * BOTH), :
                     ]
 
     out_ref[...] = row_ref[0 : 16 * LINE_ROWS, :].astype(BF16)

time: 131 us -> 130 us (level)
  no operation moved by 1% of the time
where the time goes in v11:
time: 130 us
  blocking collectives  67.3 us (52%)
  starting transfers between devices  36.5 us (28%)
  waiting for transfers between devices  12.8 us (10%)
  Pallas kernels  9.21 us (7%)
  local copies, waits for them, and re-layouts  3.28 us (3%)
    all_to_all x4, blocking collectives, exchange(): return lax.all_to_all(value, axes, split_axis=0, concat_axis=0, tiled=True)  67.3 us
    all_to_all x1, starting transfers between devices, exchange(): return lax.all_to_all(value, axes, split_axis=0, concat_axis=0, tiled=True)  23.1 us
    all_to_all x1, waiting for transfers between devices, exchange(): return lax.all_to_all(value, axes, split_axis=0, concat_axis=0, tiled=True)  12.4 us
    pallas_call x10, Pallas kernels, run(): pl.pallas_call(kernel, out_shape=out_shape, in_specs=[pl.BlockSpec(memory...  9.21 us
    ppermute x1, starting transfers between devices, per_device(): partner = lax.ppermute(gathered, 'core', swap)  7.39 us
    ppermute x1, starting transfers between devices, per_device(): other = lax.ppermute(send, 'core', swap)  6.02 us
  transfers between devices with their start and end apart: 3, of which 2 were waited for; matrix products, arithmetic and copies ran while one was open for 3% of the time, Pallas kernels for 2%

profile of v11, /device:TPU:1, one launch (start us, length us, event | category | flops | bytes accessed | tf_op | source)
XLA Modules:
  0.0 129.9 jit_solution(14612083673750682959)
XLA Ops:
  0.6 1.8 %shard_map.75 = bf16[768,128]{1,0:T(8,128)(2,1)} custom-call(bf16[16,3072]{1,0:T(8,128)(2,1)} %x_hbm.1, bf16[16,3072]{1,0:T(8,128)(2,1)} %g_hbm.1), custom_call_target="tpu_custom_call" | custom-call | tf_op jit(solution)/shard_map/pallas_call | solution.py:36
  2.4 0.0 copy-start
  2.4 23.1 %all-to-all-start = ((bf16[384,2,128]{2,1,0:T(2,128)(2,1)}), bf16[384,2,128]{2,1,0:T(2,128)(2,1)S(1)}, u32[]{:S(2)}, u32[]{:S(2)}) async-start(bf16[384,2,128]{2,1,0:T(2,128)(2,1)} %bitcast.12), calls=%async_computation | async-start | bytes 393216 | tf_op jit(solution)/shard_map/all_to_all | solution.py:306
  25.5 2.2 %reshape.34.w1_ref = bf16[1728,192]{1,0:T(8,128)(2,1)S(1)} reshape(bf16[9,36864]{1,0:T(8,128)(2,1)} %param.5) | data formatting | bytes 1327104 | tf_op jit(solution)/shard_map/reshape | solution.py:317
  27.7 0.0 copy-done
  27.7 1.1 reshape.35.w2_ref
  28.8 12.4 %all-to-all-done = bf16[384,2,128]{2,1,0:T(2,128)(2,1)S(1)} async-done(((bf16[384,2,128]{2,1,0:T(2,128)(2,1)}), bf16[384,2,128]{2,1,0:T(2,128)(2,1)S(1)}, u32[]{:S(2)}, u32[]{:S(2)}) %all-to-all-start) | async-done | bytes 196640 | tf_op jit(solution)/shard_map/all_to_all | solution.py:306
  41.3 2.6 %shard_map.76 = (bf16[768,128]{1,0:T(8,128)(2,1)S(1)}, bf16[3,256,128]{2,1,0:T(8,128)(2,1)S(1)}, bf16[3,256,128]{2,1,0:T(8,128)(2,1)S(1)}) custom-call(bf16[768,128]{1,0:T(8,128)(2,1)S(1)} %bitcast.11, bf16[1728,192]{1,0:T(8,128)(2,1)S(1)} %reshape.34.w1_ref, bf16[1728,192]{1,0:T(8,128)(2,1)S(1)} %reshape.35.w2_ref), custom_call_target="tpu_custom_call" | custom-call | tf_op jit(solution)/shard_map/pallas_call | solution.py:36
  43.8 6.0 %collective-permute-start = (bf16[3,256,128]{2,1,0:T(8,128)(2,1)S(1)}, bf16[3,256,128]{2,1,0:T(8,128)(2,1)S(1)}, u32[]{:S(2)}, u32[]{:S(2)}) collective-permute-start(bf16[3,256,128]{2,1,0:T(8,128)(2,1)S(1)} %get-tuple-element.13), channel_id=1, source_target_pairs={{0,1},{1,0},{2,3},{3,2},{4,5},{5,4},{6,7},{7,6},{8,9},{9,8},{10,11... | collective-permute-start | bytes 589832 | tf_op jit(solution)/shard_map/ppermute | solution.py:340
  49.9 0.7 shard_map.77.refs_0_
  50.5 0.4 collective-permute-done.pair_ref
  50.9 0.9 shard_map.78
  51.8 22.8 %all_to_all.25 = bf16[2064,2,128]{2,1,0:T(2,128)(2,1)S(1)} all-to-all(bf16[2064,2,128]{2,1,0:T(2,128)(2,1)S(1)} %bitcast.6), channel_id=1, replica_groups=mesh['zl'=4,'yh'=2,'yl'=2,'x'=4,'zh'=4,'core'=2] {'x','yh','yl'}, dimensions={0} | all-to-all | bytes 2113536 | tf_op jit(solution)/shard_map/all_to_all | solution.py:306
  74.6 0.3 shard_map.79
  74.9 18.4 %all_to_all.26 = bf16[720,2,128]{2,1,0:T(2,128)(2,1)S(1)} all-to-all(bf16[720,2,128]{2,1,0:T(2,128)(2,1)S(1)} %bitcast.10), channel_id=1, replica_groups=mesh['zl'=4,'yh'=2,'yl'=2,'x'=4,'zh'=4,'core'=2] {'zh','zl'}, dimensions={0} | all-to-all | bytes 737280 | tf_op jit(solution)/shard_map/all_to_all | solution.py:306
  93.4 13.7 %all_to_all.27.z_ref = bf16[4,48,128]{2,1,0:T(8,128)(2,1)S(1)} all-to-all(bf16[4,48,128]{2,1,0:T(8,128)(2,1)S(1)} %shard_map.81), channel_id=1, replica_groups=mesh['zl'=4,'yh'=2,'yl'=2,'x'=4,'zh'=4,'core'=2] {'zl'}, dimensions={0} | all-to-all | bytes 98304 | tf_op jit(solution)/shard_map/all_to_all | solution.py:306
  107.0 0.1 shard_map.82
  107.1 12.5 %all_to_all.28.r_ref = bf16[16,8,2688]{2,1,0:T(8,128)(2,1)S(1)} all-to-all(bf16[16,8,2688]{2,1,0:T(8,128)(2,1)S(1)} %shard_map.82), channel_id=1, replica_groups=mesh['zl'=4,'yh'=2,'yl'=2,'x'=4,'zh'=4,'core'=2] {'x','yh','yl'}, dimensions={0} | all-to-all | bytes 1376256 | tf_op jit(solution)/shard_map/all_to_all | solution.py:306
  119.5 7.4 %collective-permute-start.1 = (bf16[16,8,2688]{2,1,0:T(8,128)(2,1)S(1)}, bf16[16,8,2688]{2,1,0:T(8,128)(2,1)S(1)}, u32[]{:S(2)}, u32[]{:S(2)}) collective-permute-start(bf16[16,8,2688]{2,1,0:T(8,128)(2,1)S(1)} %all_to_all.28.r_ref), channel_id=1, source_target_pairs={{0,1},{1,0},{2,3},{3,2},{4,5},{5,4},{6,7},{7,6},{8,9},{9,8},{10,11... | collective-permute-start | bytes 2064392 | tf_op jit(solution)/shard_map/ppermute | solution.py:370
  126.9 0.8 shard_map.80
  127.7 1.1 shard_map.83
  128.8 0.0 collective-permute-done.1.r_ref
  128.8 1.1 shard_map.84
  (1 shorter events, 0.0 us)
Async XLA Ops:
  2.4 25.3 %copy-start = (bf16[9,36864]{1,0:T(8,128)(2,1)S(1)}, bf16[9,36864]{1,0:T(8,128)(2,1)}, u32[]{:S(2)}) copy-start(bf16[9,36864]{1,0:T(8,128)(2,1)} %param.6) | copy-start | bytes 1990660
  2.4 38.8 %all-to-all-start = ((bf16[384,2,128]{2,1,0:T(2,128)(2,1)}), bf16[384,2,128]{2,1,0:T(2,128)(2,1)S(1)}, u32[]{:S(2)}, u32[]{:S(2)}) async-start(bf16[384,2,128]{2,1,0:T(2,128)(2,1)} %bitcast.12), calls=%async_computation | async-start | bytes 393216 | tf_op jit(solution)/shard_map/all_to_all | solution.py:306
  43.8 7.1 %collective-permute-start = (bf16[3,256,128]{2,1,0:T(8,128)(2,1)S(1)}, bf16[3,256,128]{2,1,0:T(8,128)(2,1)S(1)}, u32[]{:S(2)}, u32[]{:S(2)}) collective-permute-start(bf16[3,256,128]{2,1,0:T(8,128)(2,1)S(1)} %get-tuple-element.13), channel_id=1, source_target_pairs={{0,1},{1,0},{2,3},{3,2},{4,5},{5,4},{6,7},{7,6},{8,9},{9,8},{10,11... | collective-permute-start | bytes 589832 | tf_op jit(solution)/shard_map/ppermute | solution.py:340
  119.5 9.3 %collective-permute-start.1 = (bf16[16,8,2688]{2,1,0:T(8,128)(2,1)S(1)}, bf16[16,8,2688]{2,1,0:T(8,128)(2,1)S(1)}, u32[]{:S(2)}, u32[]{:S(2)}) collective-permute-start(bf16[16,8,2688]{2,1,0:T(8,128)(2,1)S(1)} %all_to_all.28.r_ref), channel_id=1, source_target_pairs={{0,1},{1,0},{2,3},{3,2},{4,5},{5,4},{6,7},{7,6},{8,9},{9,8},{10,11... | collective-permute-start | bytes 2064392 | tf_op jit(solution)/shard_map/ppermute | solution.py:370

commit v12 on v11

--- a/solution.py
+++ b/solution.py
@@ -99,60 +99,50 @@
     return tap_ref[slot, a + 1, start : start + CELLS, :]
 
 
-def main_kernel(r_ref, w1_ref, w2_ref, o_ref, keep_ref, send_ref, row_ref, tap_ref, pair_ref):
+def forward(tap_ref, slot, w_ref, step):
+    total = None
+    for t, (a, b) in enumerate(OFFSETS):
+        term = jnp.dot(
+            get_tap(tap_ref, slot, a, b, step), w_ref[t * C : (t + 1) * C, :], preferred_element_type=F32
+        )
+        total = term if total is None else total + term
+    return total
+
+
+def backward(tap_ref, slot, w_ref, step):
+    total = None
+    for t, (a, b) in enumerate(OFFSETS):
+        term = lax.dot_general(
+            get_tap(tap_ref, slot, -a, -b, step),
+            w_ref[t * C : (t + 1) * C, :],
+            (((1,), (1,)), ((), ())),
+            preferred_element_type=F32,
+        )
+        total = term if total is None else total + term
+    return total
+
+
+def unpack(row_ref, f):
+    tiles = [row_ref[pl.ds(3 * f + t, 128, stride=6), :] for t in range(3)]
+    part = jnp.concatenate(tiles, axis=1)
+    both = [part[:, k * C : (k + 1) * C].reshape(16, 1, 8, C) for k in (0, 1)]
+    return jnp.concatenate(both, axis=1).reshape(CELLS, C)
+
+
+def main_kernel(r_ref, w1_ref, w2_ref, keep_ref, send_ref, mid_ref, row_ref, tap_ref, pair_ref):
     row_ref[...] = r_ref[...].astype(F32)
-
-    def unpack(f):
-        tiles = [row_ref[pl.ds(3 * f + t, 128, stride=6), :] for t in range(3)]
-        part = jnp.concatenate(tiles, axis=1)
-        both = [part[:, k * C : (k + 1) * C].reshape(16, 1, 8, C) for k in (0, 1)]
-        return jnp.concatenate(both, axis=1).reshape(CELLS, C)
-
-    def pack(value):
-        split = value.reshape(16, 2, 8, C)
-        return jnp.concatenate([split[:, k].reshape(128, C) for k in (0, 1)], axis=1)
-
-    def forward(slot, w_ref, step):
-        total = None
-        for t, (a, b) in enumerate(OFFSETS):
-            term = jnp.dot(
-                get_tap(tap_ref, slot, a, b, step), w_ref[t * C : (t + 1) * C, :], preferred_element_type=F32
-            )
-            total = term if total is None else total + term
-        return total
-
-    def backward(slot, w_ref, step):
-        total = None
-        for t, (a, b) in enumerate(OFFSETS):
-            term = lax.dot_general(
-                get_tap(tap_ref, slot, -a, -b, step),
-                w_ref[t * C : (t + 1) * C, :],
-                (((1,), (1,)), ((), ())),
-                preferred_element_type=F32,
-            )
-            total = term if total is None else total + term
-        return total
-
-    x = unpack(0)
-    g = unpack(1)
-    gelu_one, slope_one = gelu_parts(x)
-    act_one = gelu_one.astype(BF16).astype(F32)
+    x = unpack(row_ref, 0)
+    g = unpack(row_ref, 1)
+    act_one = gelu_parts(x)[0].astype(BF16).astype(F32)
     put_taps(tap_ref, 0, act_one, 1)
-    put_taps(tap_ref, 2, g, 2)
-    hidden = (x + forward(0, w1_ref, 1)).astype(BF16).astype(F32)
-    gelu_two, slope_two = gelu_parts(hidden)
+    put_taps(tap_ref, 1, g, 2)
+    hidden = (x + forward(tap_ref, 0, w1_ref, 1)).astype(BF16)
+    gelu_two, slope_two = gelu_parts(hidden.astype(F32))
     act_two = gelu_two.astype(BF16).astype(F32)
-    put_taps(tap_ref, 1, act_two, 2)
-    hidden_grad = (g + backward(2, w2_ref, 2) * slope_two).astype(BF16).astype(F32)
-    put_taps(tap_ref, 3, hidden_grad, 1)
-    output = hidden + forward(1, w2_ref, 2)
-    input_grad = hidden_grad + backward(3, w1_ref, 1) * slope_one
-    wide = jnp.concatenate([pack(output), pack(input_grad)], axis=1)
-    for t in range(6):
-        row_ref[t * 128 : t * 128 + 128, :] = wide[:, t * 128 : t * 128 + 128]
-    for e in range(8):
-        tiles = [row_ref[pl.ds(t * 128 + e, 16, stride=8), :] for t in range(6)]
-        o_ref[e * FIELD : (e + 1) * FIELD, :] = jnp.concatenate(tiles, axis=0).astype(BF16)
+    hidden_grad = (g + backward(tap_ref, 1, w2_ref, 2) * slope_two).astype(BF16)
+    mid_ref[0] = hidden
+    mid_ref[1] = hidden_grad
+    hidden_grad = hidden_grad.astype(F32)
     for index, (act, grad) in enumerate(((act_two, g), (act_one, hidden_grad))):
         pair_ref[index, 0] = act[:, 0:128].astype(BF16)
         pair_ref[index, 1] = jnp.concatenate([act[:, 128:C], grad[:, 128:C]], axis=1).astype(BF16)
@@ -160,6 +150,27 @@
     core = lax.axis_index("core")
     keep_ref[...] = pair_ref[core]
     send_ref[...] = pair_ref[1 - core]
+
+
+def field_kernel(r_ref, w1_ref, w2_ref, mid_ref, o_ref, row_ref, tap_ref):
+    def pack(value):
+        split = value.reshape(16, 2, 8, C)
+        return jnp.concatenate([split[:, k].reshape(128, C) for k in (0, 1)], axis=1)
+
+    row_ref[...] = r_ref[...].astype(F32)
+    slope_one = gelu_parts(unpack(row_ref, 0))[1]
+    hidden, hidden_grad = mid_ref[0].astype(F32), mid_ref[1].astype(F32)
+    act_two = gelu_parts(hidden)[0].astype(BF16).astype(F32)
+    put_taps(tap_ref, 0, act_two, 2)
+    put_taps(tap_ref, 1, hidden_grad, 1)
+    output = hidden + forward(tap_ref, 0, w2_ref, 2)
+    input_grad = hidden_grad + backward(tap_ref, 1, w1_ref, 1) * slope_one
+    wide = jnp.concatenate([pack(output), pack(input_grad)], axis=1)
+    for t in range(6):
+        row_ref[t * 128 : t * 128 + 128, :] = wide[:, t * 128 : t * 128 + 128]
+    for e in range(8):
+        tiles = [row_ref[pl.ds(t * 128 + e, 16, stride=8), :] for t in range(6)]
+        o_ref[e * FIELD : (e + 1) * FIELD, :] = jnp.concatenate(tiles, axis=0).astype(BF16)
 
 
 def half_kernel(own, pair_ref, *refs):
@@ -328,14 +339,11 @@
         limit=63400000,
     )(inputs, cotangent)
     received = exchange(packed.reshape(384, 2, 128), PEERS).reshape(768, 128)
-    fields, keep, send = call(
+    taps = vmem((2, 3, CELLS + 2 * PAD, C), BF16)
+    keep, send, middle = call(
         main_kernel,
-        (shape(8 * FIELD, 128), shape(3, CELLS, 128), shape(3, CELLS, 128)),
-        scratch=(
-            vmem((768, 128), F32),
-            vmem((4, 3, CELLS + 2 * PAD, C), BF16),
-            vmem((2, 3, CELLS, 128), BF16),
-        ),
+        (shape(3, CELLS, 128), shape(3, CELLS, 128), shape(2, CELLS, C)),
+        scratch=(vmem((768, 128), F32), taps, vmem((2, 3, CELLS, 128), BF16)),
     )(received, kernel_one, kernel_two)
     other = lax.ppermute(send, "core", swap)
     scratch = (vmem((1, 3, CELLS + 2 * PAD, C), BF16), vmem((2, C, 128), F32))
@@ -345,6 +353,12 @@
         scratch=scratch,
         cost_estimate=short,
     )(keep)
+    fields = call(
+        field_kernel,
+        shape(8 * FIELD, 128),
+        scratch=(vmem((768, 128), F32), taps),
+        cost_estimate=short,
+    )(received, kernel_one, kernel_two, middle)
     terms = call(
         functools.partial(half_kernel, False),
         shape(16 * BOTH, 128),

time: 130 us -> 130 us (level)
    pallas_call x10 -> x11, Pallas kernels: 9.21 us -> 9.26 us  [run(): pl.pallas_call(kernel, out_shape=out_shape, in_specs=[pl.BlockSpec(memory...]
  transfers between devices with their start and end apart: 3 -> 3, of which waited for: 2 -> 1; matrix products, arithmetic and copies ran while one was open for 3% -> 3% of each run, Pallas kernels for 2% -> 3%
where the time goes in v12:
time: 130 us; the launch traced here: 129 us
  blocking collectives  67.9 us (52%)
  starting transfers between devices  35.8 us (28%)
  waiting for transfers between devices  12.4 us (10%)
  Pallas kernels  9.26 us (7%)
  local copies, waits for them, and re-layouts  3.28 us (3%)
    all_to_all x4, blocking collectives, exchange(): return lax.all_to_all(value, axes, split_axis=0, concat_axis=0, tiled=True)  67.9 us
    all_to_all x1, starting transfers between devices, exchange(): return lax.all_to_all(value, axes, split_axis=0, concat_axis=0, tiled=True)  23.1 us
    all_to_all x1, waiting for transfers between devices, exchange(): return lax.all_to_all(value, axes, split_axis=0, concat_axis=0, tiled=True)  12.4 us
    pallas_call x11, Pallas kernels, run(): pl.pallas_call(kernel, out_shape=out_shape, in_specs=[pl.BlockSpec(memory...  9.26 us
    ppermute x1, starting transfers between devices, per_device(): partner = lax.ppermute(gathered, 'core', swap)  6.71 us
    ppermute x1, starting transfers between devices, per_device(): other = lax.ppermute(send, 'core', swap)  6.01 us
  transfers between devices with their start and end apart: 3, of which 1 were waited for; matrix products, arithmetic and copies ran while one was open for 3% of the time, Pallas kernels for 3%

profile of v12, /device:TPU:1, one launch (start us, length us, event | category | flops | bytes accessed | tf_op | source)
XLA Modules:
  0.0 129.5 jit_solution(5025149516427405971)
XLA Ops:
  0.6 1.8 %shard_map.75 = bf16[768,128]{1,0:T(8,128)(2,1)} custom-call(bf16[16,3072]{1,0:T(8,128)(2,1)} %x_hbm.1, bf16[16,3072]{1,0:T(8,128)(2,1)} %g_hbm.1), custom_call_target="tpu_custom_call" | custom-call | tf_op jit(solution)/shard_map/pallas_call | solution.py:36
  2.4 0.0 copy-start
  2.4 23.1 %all-to-all-start = ((bf16[384,2,128]{2,1,0:T(2,128)(2,1)}), bf16[384,2,128]{2,1,0:T(2,128)(2,1)S(1)}, u32[]{:S(2)}, u32[]{:S(2)}) async-start(bf16[384,2,128]{2,1,0:T(2,128)(2,1)} %bitcast.13), calls=%async_computation | async-start | bytes 393216 | tf_op jit(solution)/shard_map/all_to_all | solution.py:317
  25.5 2.2 %reshape.34.w1_ref = bf16[1728,192]{1,0:T(8,128)(2,1)S(1)} reshape(bf16[9,36864]{1,0:T(8,128)(2,1)} %param.5) | data formatting | bytes 1327104 | tf_op jit(solution)/shard_map/reshape | solution.py:328
  27.7 0.0 copy-done
  27.7 1.1 reshape.35.w2_ref
  28.8 12.4 %all-to-all-done = bf16[384,2,128]{2,1,0:T(2,128)(2,1)S(1)} async-done(((bf16[384,2,128]{2,1,0:T(2,128)(2,1)}), bf16[384,2,128]{2,1,0:T(2,128)(2,1)S(1)}, u32[]{:S(2)}, u32[]{:S(2)}) %all-to-all-start) | async-done | bytes 196640 | tf_op jit(solution)/shard_map/all_to_all | solution.py:317
  41.3 1.5 %shard_map.76 = (bf16[3,256,128]{2,1,0:T(8,128)(2,1)S(1)}, bf16[3,256,128]{2,1,0:T(8,128)(2,1)S(1)}, bf16[2,256,192]{2,1,0:T(8,128)(2,1)S(1)}) custom-call(bf16[768,128]{1,0:T(8,128)(2,1)S(1)} %bitcast.11, bf16[1728,192]{1,0:T(8,128)(2,1)S(1)} %reshape.34.w1_ref, bf16[1728,192]{1,0:T(8,128)(2,1)S(1)} %reshape.35.w2_ref), custom_call_target="tpu_custom_call" | custom-call | tf_op jit(solution)/shard_map/pallas_call | solution.py:36
  42.7 6.0 %collective-permute-start = (bf16[3,256,128]{2,1,0:T(8,128)(2,1)S(1)}, bf16[3,256,128]{2,1,0:T(8,128)(2,1)S(1)}, u32[]{:S(2)}, u32[]{:S(2)}) collective-permute-start(bf16[3,256,128]{2,1,0:T(8,128)(2,1)S(1)} %get-tuple-element.13), channel_id=1, source_target_pairs={{0,1},{1,0},{2,3},{3,2},{4,5},{5,4},{6,7},{7,6},{8,9},{9,8},{10,11... | collective-permute-start | bytes 589832 | tf_op jit(solution)/shard_map/ppermute | solution.py:348
  48.8 1.2 shard_map.78.refs_1_
  49.9 0.7 shard_map.77.refs_0_
  50.6 0.0 collective-permute-done.pair_ref
  50.6 0.9 shard_map.79
  51.5 22.9 %all_to_all.25 = bf16[2064,2,128]{2,1,0:T(2,128)(2,1)S(1)} all-to-all(bf16[2064,2,128]{2,1,0:T(2,128)(2,1)S(1)} %bitcast.6), channel_id=1, replica_groups=mesh['zl'=4,'yh'=2,'yl'=2,'x'=4,'zh'=4,'core'=2] {'x','yh','yl'}, dimensions={0} | all-to-all | bytes 2113536 | tf_op jit(solution)/shard_map/all_to_all | solution.py:317
  74.4 0.3 shard_map.80
  74.7 18.6 %all_to_all.26 = bf16[720,2,128]{2,1,0:T(2,128)(2,1)S(1)} all-to-all(bf16[720,2,128]{2,1,0:T(2,128)(2,1)S(1)} %bitcast.10), channel_id=1, replica_groups=mesh['zl'=4,'yh'=2,'yl'=2,'x'=4,'zh'=4,'core'=2] {'zh','zl'}, dimensions={0} | all-to-all | bytes 737280 | tf_op jit(solution)/shard_map/all_to_all | solution.py:317
  93.4 13.4 %all_to_all.27.z_ref = bf16[4,48,128]{2,1,0:T(8,128)(2,1)S(1)} all-to-all(bf16[4,48,128]{2,1,0:T(8,128)(2,1)S(1)} %shard_map.82), channel_id=1, replica_groups=mesh['zl'=4,'yh'=2,'yl'=2,'x'=4,'zh'=4,'core'=2] {'zl'}, dimensions={0} | all-to-all | bytes 98304 | tf_op jit(solution)/shard_map/all_to_all | solution.py:317
  106.8 0.1 shard_map.83
  106.9 12.9 %all_to_all.28.r_ref = bf16[16,8,2688]{2,1,0:T(8,128)(2,1)S(1)} all-to-all(bf16[16,8,2688]{2,1,0:T(8,128)(2,1)S(1)} %shard_map.83), channel_id=1, replica_groups=mesh['zl'=4,'yh'=2,'yl'=2,'x'=4,'zh'=4,'core'=2] {'x','yh','yl'}, dimensions={0} | all-to-all | bytes 1376256 | tf_op jit(solution)/shard_map/all_to_all | solution.py:317
  119.8 6.7 %collective-permute-start.1 = (bf16[16,8,2688]{2,1,0:T(8,128)(2,1)S(1)}, bf16[16,8,2688]{2,1,0:T(8,128)(2,1)S(1)}, u32[]{:S(2)}, u32[]{:S(2)}) collective-permute-start(bf16[16,8,2688]{2,1,0:T(8,128)(2,1)S(1)} %all_to_all.28.r_ref), channel_id=1, source_target_pairs={{0,1},{1,0},{2,3},{3,2},{4,5},{5,4},{6,7},{7,6},{8,9},{9,8},{10,11... | collective-permute-start | bytes 2064392 | tf_op jit(solution)/shard_map/ppermute | solution.py:384
  126.5 0.8 shard_map.81
  127.3 1.1 shard_map.84
  128.4 0.0 collective-permute-done.1.r_ref
  128.4 1.1 shard_map.85
  (1 shorter events, 0.0 us)
Async XLA Ops:
  2.4 25.3 %copy-start = (bf16[9,36864]{1,0:T(8,128)(2,1)S(1)}, bf16[9,36864]{1,0:T(8,128)(2,1)}, u32[]{:S(2)}) copy-start(bf16[9,36864]{1,0:T(8,128)(2,1)} %param.6) | copy-start | bytes 1990660
  2.4 38.8 %all-to-all-start = ((bf16[384,2,128]{2,1,0:T(2,128)(2,1)}), bf16[384,2,128]{2,1,0:T(2,128)(2,1)S(1)}, u32[]{:S(2)}, u32[]{:S(2)}) async-start(bf16[384,2,128]{2,1,0:T(2,128)(2,1)} %bitcast.13), calls=%async_computation | async-start | bytes 393216 | tf_op jit(solution)/shard_map/all_to_all | solution.py:317
  42.7 7.9 %collective-permute-start = (bf16[3,256,128]{2,1,0:T(8,128)(2,1)S(1)}, bf16[3,256,128]{2,1,0:T(8,128)(2,1)S(1)}, u32[]{:S(2)}, u32[]{:S(2)}) collective-permute-start(bf16[3,256,128]{2,1,0:T(8,128)(2,1)S(1)} %get-tuple-element.13), channel_id=1, source_target_pairs={{0,1},{1,0},{2,3},{3,2},{4,5},{5,4},{6,7},{7,6},{8,9},{9,8},{10,11... | collective-permute-start | bytes 589832 | tf_op jit(solution)/shard_map/ppermute | solution.py:348
  119.8 8.6 %collective-permute-start.1 = (bf16[16,8,2688]{2,1,0:T(8,128)(2,1)S(1)}, bf16[16,8,2688]{2,1,0:T(8,128)(2,1)S(1)}, u32[]{:S(2)}, u32[]{:S(2)}) collective-permute-start(bf16[16,8,2688]{2,1,0:T(8,128)(2,1)S(1)} %all_to_all.28.r_ref), channel_id=1, source_target_pairs={{0,1},{1,0},{2,3},{3,2},{4,5},{5,4},{6,7},{7,6},{8,9},{9,8},{10,11... | collective-permute-start | bytes 2064392 | tf_op jit(solution)/shard_map/ppermute | solution.py:384

commit v13 on v12

--- a/solution.py
+++ b/solution.py
@@ -131,15 +131,16 @@
 
 def main_kernel(r_ref, w1_ref, w2_ref, keep_ref, send_ref, mid_ref, row_ref, tap_ref, pair_ref):
     row_ref[...] = r_ref[...].astype(F32)
+    g = unpack(row_ref, 1)
+    put_taps(tap_ref, 1, g, 2)
+    back_two = backward(tap_ref, 1, w2_ref, 2)
     x = unpack(row_ref, 0)
-    g = unpack(row_ref, 1)
     act_one = gelu_parts(x)[0].astype(BF16).astype(F32)
     put_taps(tap_ref, 0, act_one, 1)
-    put_taps(tap_ref, 1, g, 2)
     hidden = (x + forward(tap_ref, 0, w1_ref, 1)).astype(BF16)
     gelu_two, slope_two = gelu_parts(hidden.astype(F32))
     act_two = gelu_two.astype(BF16).astype(F32)
-    hidden_grad = (g + backward(tap_ref, 1, w2_ref, 2) * slope_two).astype(BF16)
+    hidden_grad = (g + back_two * slope_two).astype(BF16)
     mid_ref[0] = hidden
     mid_ref[1] = hidden_grad
     hidden_grad = hidden_grad.astype(F32)
@@ -158,13 +159,14 @@
         return jnp.concatenate([split[:, k].reshape(128, C) for k in (0, 1)], axis=1)
 
     row_ref[...] = r_ref[...].astype(F32)
+    hidden, hidden_grad = mid_ref[0].astype(F32), mid_ref[1].astype(F32)
+    put_taps(tap_ref, 1, hidden_grad, 1)
+    back_one = backward(tap_ref, 1, w1_ref, 1)
     slope_one = gelu_parts(unpack(row_ref, 0))[1]
-    hidden, hidden_grad = mid_ref[0].astype(F32), mid_ref[1].astype(F32)
     act_two = gelu_parts(hidden)[0].astype(BF16).astype(F32)
     put_taps(tap_ref, 0, act_two, 2)
-    put_taps(tap_ref, 1, hidden_grad, 1)
     output = hidden + forward(tap_ref, 0, w2_ref, 2)
-    input_grad = hidden_grad + backward(tap_ref, 1, w1_ref, 1) * slope_one
+    input_grad = hidden_grad + back_one * slope_one
     wide = jnp.concatenate([pack(output), pack(input_grad)], axis=1)
     for t in range(6):
         row_ref[t * 128 : t * 128 + 128, :] = wide[:, t * 128 : t * 128 + 128]

time: 130 us -> 130 us (level)
  no operation moved by 1% of the time
where the time goes in v13:
time: 130 us; the launch traced here: 129 us
  blocking collectives  67.9 us (52%)
  starting transfers between devices  35.8 us (28%)
  waiting for transfers between devices  12.4 us (10%)
  Pallas kernels  9.25 us (7%)
  local copies, waits for them, and re-layouts  3.28 us (3%)
    all_to_all x4, blocking collectives, exchange(): return lax.all_to_all(value, axes, split_axis=0, concat_axis=0, tiled=True)  67.9 us
    all_to_all x1, starting transfers between devices, exchange(): return lax.all_to_all(value, axes, split_axis=0, concat_axis=0, tiled=True)  23.1 us
    all_to_all x1, waiting for transfers between devices, exchange(): return lax.all_to_all(value, axes, split_axis=0, concat_axis=0, tiled=True)  12.4 us
    pallas_call x11, Pallas kernels, run(): pl.pallas_call(kernel, out_shape=out_shape, in_specs=[pl.BlockSpec(memory...  9.25 us
    ppermute x1, starting transfers between devices, per_device(): partner = lax.ppermute(gathered, 'core', swap)  6.71 us
    ppermute x1, starting transfers between devices, per_device(): other = lax.ppermute(send, 'core', swap)  6 us
  transfers between devices with their start and end apart: 3, of which 1 were waited for; matrix products, arithmetic and copies ran while one was open for 3% of the time, Pallas kernels for 3%

profile of v13, /device:TPU:1, one launch (start us, length us, event | category | flops | bytes accessed | tf_op | source)
XLA Modules:
  0.0 129.5 jit_solution(3638589474342649089)
XLA Ops:
  0.6 1.8 %shard_map.75 = bf16[768,128]{1,0:T(8,128)(2,1)} custom-call(bf16[16,3072]{1,0:T(8,128)(2,1)} %x_hbm.1, bf16[16,3072]{1,0:T(8,128)(2,1)} %g_hbm.1), custom_call_target="tpu_custom_call" | custom-call | tf_op jit(solution)/shard_map/pallas_call | solution.py:36
  2.4 0.0 copy-start
  2.4 23.1 %all-to-all-start = ((bf16[384,2,128]{2,1,0:T(2,128)(2,1)}), bf16[384,2,128]{2,1,0:T(2,128)(2,1)S(1)}, u32[]{:S(2)}, u32[]{:S(2)}) async-start(bf16[384,2,128]{2,1,0:T(2,128)(2,1)} %bitcast.13), calls=%async_computation | async-start | bytes 393216 | tf_op jit(solution)/shard_map/all_to_all | solution.py:319
  25.5 2.2 %reshape.34.w1_ref = bf16[1728,192]{1,0:T(8,128)(2,1)S(1)} reshape(bf16[9,36864]{1,0:T(8,128)(2,1)} %param.5) | data formatting | bytes 1327104 | tf_op jit(solution)/shard_map/reshape | solution.py:330
  27.7 0.0 copy-done
  27.7 1.1 reshape.35.w2_ref
  28.8 12.4 %all-to-all-done = bf16[384,2,128]{2,1,0:T(2,128)(2,1)S(1)} async-done(((bf16[384,2,128]{2,1,0:T(2,128)(2,1)}), bf16[384,2,128]{2,1,0:T(2,128)(2,1)S(1)}, u32[]{:S(2)}, u32[]{:S(2)}) %all-to-all-start) | async-done | bytes 196640 | tf_op jit(solution)/shard_map/all_to_all | solution.py:319
  41.3 1.5 %shard_map.76 = (bf16[3,256,128]{2,1,0:T(8,128)(2,1)S(1)}, bf16[3,256,128]{2,1,0:T(8,128)(2,1)S(1)}, bf16[2,256,192]{2,1,0:T(8,128)(2,1)S(1)}) custom-call(bf16[768,128]{1,0:T(8,128)(2,1)S(1)} %bitcast.11, bf16[1728,192]{1,0:T(8,128)(2,1)S(1)} %reshape.34.w1_ref, bf16[1728,192]{1,0:T(8,128)(2,1)S(1)} %reshape.35.w2_ref), custom_call_target="tpu_custom_call" | custom-call | tf_op jit(solution)/shard_map/pallas_call | solution.py:36
  42.7 6.0 %collective-permute-start = (bf16[3,256,128]{2,1,0:T(8,128)(2,1)S(1)}, bf16[3,256,128]{2,1,0:T(8,128)(2,1)S(1)}, u32[]{:S(2)}, u32[]{:S(2)}) collective-permute-start(bf16[3,256,128]{2,1,0:T(8,128)(2,1)S(1)} %get-tuple-element.13), channel_id=1, source_target_pairs={{0,1},{1,0},{2,3},{3,2},{4,5},{5,4},{6,7},{7,6},{8,9},{9,8},{10,11... | collective-permute-start | bytes 589832 | tf_op jit(solution)/shard_map/ppermute | solution.py:350
  48.7 1.1 shard_map.78.refs_1_
  49.9 0.7 shard_map.77.refs_0_
  50.6 0.0 collective-permute-done.pair_ref
  50.6 0.9 shard_map.79
  51.5 22.9 %all_to_all.25 = bf16[2064,2,128]{2,1,0:T(2,128)(2,1)S(1)} all-to-all(bf16[2064,2,128]{2,1,0:T(2,128)(2,1)S(1)} %bitcast.6), channel_id=1, replica_groups=mesh['zl'=4,'yh'=2,'yl'=2,'x'=4,'zh'=4,'core'=2] {'x','yh','yl'}, dimensions={0} | all-to-all | bytes 2113536 | tf_op jit(solution)/shard_map/all_to_all | solution.py:319
  74.4 0.3 shard_map.80
  74.7 18.6 %all_to_all.26 = bf16[720,2,128]{2,1,0:T(2,128)(2,1)S(1)} all-to-all(bf16[720,2,128]{2,1,0:T(2,128)(2,1)S(1)} %bitcast.10), channel_id=1, replica_groups=mesh['zl'=4,'yh'=2,'yl'=2,'x'=4,'zh'=4,'core'=2] {'zh','zl'}, dimensions={0} | all-to-all | bytes 737280 | tf_op jit(solution)/shard_map/all_to_all | solution.py:319
  93.4 13.4 %all_to_all.27.z_ref = bf16[4,48,128]{2,1,0:T(8,128)(2,1)S(1)} all-to-all(bf16[4,48,128]{2,1,0:T(8,128)(2,1)S(1)} %shard_map.82), channel_id=1, replica_groups=mesh['zl'=4,'yh'=2,'yl'=2,'x'=4,'zh'=4,'core'=2] {'zl'}, dimensions={0} | all-to-all | bytes 98304 | tf_op jit(solution)/shard_map/all_to_all | solution.py:319
  106.8 0.1 shard_map.83
  106.9 12.9 %all_to_all.28.r_ref = bf16[16,8,2688]{2,1,0:T(8,128)(2,1)S(1)} all-to-all(bf16[16,8,2688]{2,1,0:T(8,128)(2,1)S(1)} %shard_map.83), channel_id=1, replica_groups=mesh['zl'=4,'yh'=2,'yl'=2,'x'=4,'zh'=4,'core'=2] {'x','yh','yl'}, dimensions={0} | all-to-all | bytes 1376256 | tf_op jit(solution)/shard_map/all_to_all | solution.py:319
  119.8 6.7 %collective-permute-start.1 = (bf16[16,8,2688]{2,1,0:T(8,128)(2,1)S(1)}, bf16[16,8,2688]{2,1,0:T(8,128)(2,1)S(1)}, u32[]{:S(2)}, u32[]{:S(2)}) collective-permute-start(bf16[16,8,2688]{2,1,0:T(8,128)(2,1)S(1)} %all_to_all.28.r_ref), channel_id=1, source_target_pairs={{0,1},{1,0},{2,3},{3,2},{4,5},{5,4},{6,7},{7,6},{8,9},{9,8},{10,11... | collective-permute-start | bytes 2064392 | tf_op jit(solution)/shard_map/ppermute | solution.py:386
  126.5 0.8 shard_map.81
  127.3 1.1 shard_map.84
  128.4 0.0 collective-permute-done.1.r_ref
  128.4 1.1 shard_map.85
  (1 shorter events, 0.0 us)
Async XLA Ops:
  2.4 25.3 %copy-start = (bf16[9,36864]{1,0:T(8,128)(2,1)S(1)}, bf16[9,36864]{1,0:T(8,128)(2,1)}, u32[]{:S(2)}) copy-start(bf16[9,36864]{1,0:T(8,128)(2,1)} %param.6) | copy-start | bytes 1990660
  2.4 38.8 %all-to-all-start = ((bf16[384,2,128]{2,1,0:T(2,128)(2,1)}), bf16[384,2,128]{2,1,0:T(2,128)(2,1)S(1)}, u32[]{:S(2)}, u32[]{:S(2)}) async-start(bf16[384,2,128]{2,1,0:T(2,128)(2,1)} %bitcast.13), calls=%async_computation | async-start | bytes 393216 | tf_op jit(solution)/shard_map/all_to_all | solution.py:319
  42.7 7.8 %collective-permute-start = (bf16[3,256,128]{2,1,0:T(8,128)(2,1)S(1)}, bf16[3,256,128]{2,1,0:T(8,128)(2,1)S(1)}, u32[]{:S(2)}, u32[]{:S(2)}) collective-permute-start(bf16[3,256,128]{2,1,0:T(8,128)(2,1)S(1)} %get-tuple-element.13), channel_id=1, source_target_pairs={{0,1},{1,0},{2,3},{3,2},{4,5},{5,4},{6,7},{7,6},{8,9},{9,8},{10,11... | collective-permute-start | bytes 589832 | tf_op jit(solution)/shard_map/ppermute | solution.py:350
  119.8 8.6 %collective-permute-start.1 = (bf16[16,8,2688]{2,1,0:T(8,128)(2,1)S(1)}, bf16[16,8,2688]{2,1,0:T(8,128)(2,1)S(1)}, u32[]{:S(2)}, u32[]{:S(2)}) collective-permute-start(bf16[16,8,2688]{2,1,0:T(8,128)(2,1)S(1)} %all_to_all.28.r_ref), channel_id=1, source_target_pairs={{0,1},{1,0},{2,3},{3,2},{4,5},{5,4},{6,7},{7,6},{8,9},{9,8},{10,11... | collective-permute-start | bytes 2064392 | tf_op jit(solution)/shard_map/ppermute | solution.py:386

commit v14 on v13

--- a/solution.py
+++ b/solution.py
@@ -131,16 +131,15 @@
 
 def main_kernel(r_ref, w1_ref, w2_ref, keep_ref, send_ref, mid_ref, row_ref, tap_ref, pair_ref):
     row_ref[...] = r_ref[...].astype(F32)
+    x = unpack(row_ref, 0)
     g = unpack(row_ref, 1)
-    put_taps(tap_ref, 1, g, 2)
-    back_two = backward(tap_ref, 1, w2_ref, 2)
-    x = unpack(row_ref, 0)
     act_one = gelu_parts(x)[0].astype(BF16).astype(F32)
     put_taps(tap_ref, 0, act_one, 1)
+    put_taps(tap_ref, 1, g, 2)
     hidden = (x + forward(tap_ref, 0, w1_ref, 1)).astype(BF16)
     gelu_two, slope_two = gelu_parts(hidden.astype(F32))
     act_two = gelu_two.astype(BF16).astype(F32)
-    hidden_grad = (g + back_two * slope_two).astype(BF16)
+    hidden_grad = (g + backward(tap_ref, 1, w2_ref, 2) * slope_two).astype(BF16)
     mid_ref[0] = hidden
     mid_ref[1] = hidden_grad
     hidden_grad = hidden_grad.astype(F32)

time: 130 us -> 130 us (level)
  no operation moved by 1% of the time
where the time goes in v14:
time: 130 us; the launch traced here: 129 us
  blocking collectives  67.9 us (52%)
  starting transfers between devices  35.8 us (28%)
  waiting for transfers between devices  12.4 us (10%)
  Pallas kernels  9.25 us (7%)
  local copies, waits for them, and re-layouts  3.28 us (3%)
    all_to_all x4, blocking collectives, exchange(): return lax.all_to_all(value, axes, split_axis=0, concat_axis=0, tiled=True)  67.9 us
    all_to_all x1, starting transfers between devices, exchange(): return lax.all_to_all(value, axes, split_axis=0, concat_axis=0, tiled=True)  23.1 us
    all_to_all x1, waiting for transfers between devices, exchange(): return lax.all_to_all(value, axes, split_axis=0, concat_axis=0, tiled=True)  12.4 us
    pallas_call x11, Pallas kernels, run(): pl.pallas_call(kernel, out_shape=out_shape, in_specs=[pl.BlockSpec(memory...  9.25 us
    ppermute x1, starting transfers between devices, per_device(): partner = lax.ppermute(gathered, 'core', swap)  6.73 us
    ppermute x1, starting transfers between devices, per_device(): other = lax.ppermute(send, 'core', swap)  6.01 us
  transfers between devices with their start and end apart: 3, of which 1 were waited for; matrix products, arithmetic and copies ran while one was open for 3% of the time, Pallas kernels for 3%

profile of v14, /device:TPU:1, one launch (start us, length us, event | category | flops | bytes accessed | tf_op | source)
XLA Modules:
  0.0 129.5 jit_solution(3967225763791364694)
XLA Ops:
  0.6 1.8 %shard_map.75 = bf16[768,128]{1,0:T(8,128)(2,1)} custom-call(bf16[16,3072]{1,0:T(8,128)(2,1)} %x_hbm.1, bf16[16,3072]{1,0:T(8,128)(2,1)} %g_hbm.1), custom_call_target="tpu_custom_call" | custom-call | tf_op jit(solution)/shard_map/pallas_call | solution.py:36
  2.4 0.0 copy-start
  2.4 23.1 %all-to-all-start = ((bf16[384,2,128]{2,1,0:T(2,128)(2,1)}), bf16[384,2,128]{2,1,0:T(2,128)(2,1)S(1)}, u32[]{:S(2)}, u32[]{:S(2)}) async-start(bf16[384,2,128]{2,1,0:T(2,128)(2,1)} %bitcast.13), calls=%async_computation | async-start | bytes 393216 | tf_op jit(solution)/shard_map/all_to_all | solution.py:318
  25.5 2.2 %reshape.34.w1_ref = bf16[1728,192]{1,0:T(8,128)(2,1)S(1)} reshape(bf16[9,36864]{1,0:T(8,128)(2,1)} %param.5) | data formatting | bytes 1327104 | tf_op jit(solution)/shard_map/reshape | solution.py:329
  27.7 0.0 copy-done
  27.7 1.1 reshape.35.w2_ref
  28.8 12.4 %all-to-all-done = bf16[384,2,128]{2,1,0:T(2,128)(2,1)S(1)} async-done(((bf16[384,2,128]{2,1,0:T(2,128)(2,1)}), bf16[384,2,128]{2,1,0:T(2,128)(2,1)S(1)}, u32[]{:S(2)}, u32[]{:S(2)}) %all-to-all-start) | async-done | bytes 196640 | tf_op jit(solution)/shard_map/all_to_all | solution.py:318
  41.3 1.5 %shard_map.76 = (bf16[3,256,128]{2,1,0:T(8,128)(2,1)S(1)}, bf16[3,256,128]{2,1,0:T(8,128)(2,1)S(1)}, bf16[2,256,192]{2,1,0:T(8,128)(2,1)S(1)}) custom-call(bf16[768,128]{1,0:T(8,128)(2,1)S(1)} %bitcast.11, bf16[1728,192]{1,0:T(8,128)(2,1)S(1)} %reshape.34.w1_ref, bf16[1728,192]{1,0:T(8,128)(2,1)S(1)} %reshape.35.w2_ref), custom_call_target="tpu_custom_call" | custom-call | tf_op jit(solution)/shard_map/pallas_call | solution.py:36
  42.7 6.0 %collective-permute-start = (bf16[3,256,128]{2,1,0:T(8,128)(2,1)S(1)}, bf16[3,256,128]{2,1,0:T(8,128)(2,1)S(1)}, u32[]{:S(2)}, u32[]{:S(2)}) collective-permute-start(bf16[3,256,128]{2,1,0:T(8,128)(2,1)S(1)} %get-tuple-element.13), channel_id=1, source_target_pairs={{0,1},{1,0},{2,3},{3,2},{4,5},{5,4},{6,7},{7,6},{8,9},{9,8},{10,11... | collective-permute-start | bytes 589832 | tf_op jit(solution)/shard_map/ppermute | solution.py:349
  48.8 1.1 shard_map.78.refs_1_
  49.9 0.7 shard_map.77.refs_0_
  50.6 0.0 collective-permute-done.pair_ref
  50.6 0.9 shard_map.79
  51.5 22.9 %all_to_all.25 = bf16[2064,2,128]{2,1,0:T(2,128)(2,1)S(1)} all-to-all(bf16[2064,2,128]{2,1,0:T(2,128)(2,1)S(1)} %bitcast.6), channel_id=1, replica_groups=mesh['zl'=4,'yh'=2,'yl'=2,'x'=4,'zh'=4,'core'=2] {'x','yh','yl'}, dimensions={0} | all-to-all | bytes 2113536 | tf_op jit(solution)/shard_map/all_to_all | solution.py:318
  74.4 0.3 shard_map.80
  74.7 18.6 %all_to_all.26 = bf16[720,2,128]{2,1,0:T(2,128)(2,1)S(1)} all-to-all(bf16[720,2,128]{2,1,0:T(2,128)(2,1)S(1)} %bitcast.10), channel_id=1, replica_groups=mesh['zl'=4,'yh'=2,'yl'=2,'x'=4,'zh'=4,'core'=2] {'zh','zl'}, dimensions={0} | all-to-all | bytes 737280 | tf_op jit(solution)/shard_map/all_to_all | solution.py:318
  93.4 13.4 %all_to_all.27.z_ref = bf16[4,48,128]{2,1,0:T(8,128)(2,1)S(1)} all-to-all(bf16[4,48,128]{2,1,0:T(8,128)(2,1)S(1)} %shard_map.82), channel_id=1, replica_groups=mesh['zl'=4,'yh'=2,'yl'=2,'x'=4,'zh'=4,'core'=2] {'zl'}, dimensions={0} | all-to-all | bytes 98304 | tf_op jit(solution)/shard_map/all_to_all | solution.py:318
  106.8 0.1 shard_map.83
  106.9 12.9 %all_to_all.28.r_ref = bf16[16,8,2688]{2,1,0:T(8,128)(2,1)S(1)} all-to-all(bf16[16,8,2688]{2,1,0:T(8,128)(2,1)S(1)} %shard_map.83), channel_id=1, replica_groups=mesh['zl'=4,'yh'=2,'yl'=2,'x'=4,'zh'=4,'core'=2] {'x','yh','yl'}, dimensions={0} | all-to-all | bytes 1376256 | tf_op jit(solution)/shard_map/all_to_all | solution.py:318
  119.8 6.7 %collective-permute-start.1 = (bf16[16,8,2688]{2,1,0:T(8,128)(2,1)S(1)}, bf16[16,8,2688]{2,1,0:T(8,128)(2,1)S(1)}, u32[]{:S(2)}, u32[]{:S(2)}) collective-permute-start(bf16[16,8,2688]{2,1,0:T(8,128)(2,1)S(1)} %all_to_all.28.r_ref), channel_id=1, source_target_pairs={{0,1},{1,0},{2,3},{3,2},{4,5},{5,4},{6,7},{7,6},{8,9},{9,8},{10,11... | collective-permute-start | bytes 2064392 | tf_op jit(solution)/shard_map/ppermute | solution.py:385
  126.5 0.8 shard_map.81
  127.3 1.1 shard_map.84
  128.4 0.0 collective-permute-done.1.r_ref
  128.4 1.1 shard_map.85
  (1 shorter events, 0.0 us)
Async XLA Ops:
  2.4 25.3 %copy-start = (bf16[9,36864]{1,0:T(8,128)(2,1)S(1)}, bf16[9,36864]{1,0:T(8,128)(2,1)}, u32[]{:S(2)}) copy-start(bf16[9,36864]{1,0:T(8,128)(2,1)} %param.6) | copy-start | bytes 1990660
  2.4 38.8 %all-to-all-start = ((bf16[384,2,128]{2,1,0:T(2,128)(2,1)}), bf16[384,2,128]{2,1,0:T(2,128)(2,1)S(1)}, u32[]{:S(2)}, u32[]{:S(2)}) async-start(bf16[384,2,128]{2,1,0:T(2,128)(2,1)} %bitcast.13), calls=%async_computation | async-start | bytes 393216 | tf_op jit(solution)/shard_map/all_to_all | solution.py:318
  42.7 7.9 %collective-permute-start = (bf16[3,256,128]{2,1,0:T(8,128)(2,1)S(1)}, bf16[3,256,128]{2,1,0:T(8,128)(2,1)S(1)}, u32[]{:S(2)}, u32[]{:S(2)}) collective-permute-start(bf16[3,256,128]{2,1,0:T(8,128)(2,1)S(1)} %get-tuple-element.13), channel_id=1, source_target_pairs={{0,1},{1,0},{2,3},{3,2},{4,5},{5,4},{6,7},{7,6},{8,9},{9,8},{10,11... | collective-permute-start | bytes 589832 | tf_op jit(solution)/shard_map/ppermute | solution.py:349
  119.8 8.6 %collective-permute-start.1 = (bf16[16,8,2688]{2,1,0:T(8,128)(2,1)S(1)}, bf16[16,8,2688]{2,1,0:T(8,128)(2,1)S(1)}, u32[]{:S(2)}, u32[]{:S(2)}) collective-permute-start(bf16[16,8,2688]{2,1,0:T(8,128)(2,1)S(1)} %all_to_all.28.r_ref), channel_id=1, source_target_pairs={{0,1},{1,0},{2,3},{3,2},{4,5},{5,4},{6,7},{7,6},{8,9},{9,8},{10,11... | collective-permute-start | bytes 2064392 | tf_op jit(solution)/shard_map/ppermute | solution.py:385
